TPU v7x, 256 devices: a whole 4x4x8 slice. The times are simulated.
256 devices in a mesh: seq: 64 (over z, y_hi, x), chan: 4 (over y_lo, core).
Axes of the slice: x: 4, y: 4 (y_hi: 2, y_lo: 2; y = y_hi * 2 + y_lo), z: 8, core: 2. Of those that a mesh axis runs over, the one named last changes fastest.
Arguments:
- tokens: bfloat16 [256, 1048576], P('chan', 'seq'), may hold values from -6 to 6
- gate_in: bfloat16 [256, 1048576], P('chan', 'seq'), may hold values from -5 to 5
- gate_out: bfloat16 [256, 1048576], P('chan', 'seq'), may hold values from -5 to 5
- twiddle: float32 [1024, 1024], P('seq'), may hold values from -4 to 4
- first_factor: bfloat16 [1024, 1024], P(('seq', 'chan')), may hold values from -0.1875 to 0.1875
- second_factor: bfloat16 [1024, 1024], P(('seq', 'chan')), may hold values from -0.1875 to 0.1875
- w_up: bfloat16 [4, 64, 128], P('chan'), may hold values from -0.75 to 0.75
- w_down: bfloat16 [4, 128, 64], P('chan'), may hold values from -0.5 to 0.5
- cotangent: bfloat16 [256, 1048576], P('chan', 'seq'), may hold values from -6 to 6
Outputs:
- mixed_out: bfloat16 [256, 1048576], P('chan', 'seq')
- input_grad: bfloat16 [256, 1048576], P('chan', 'seq')
- first_grad: float32 [1024, 1024], P(('seq', 'chan'))
- second_grad: float32 [1024, 1024], P(('seq', 'chan'))
- up_grad: float32 [4, 64, 128], P('chan')
- down_grad: float32 [4, 128, 64], P('chan')
All inputs are finite; a program needn't handle non-finite values.
Results may differ from a plain program's by a relative error of at most 0.011.
Values may be sent and summed in bfloat16 or wider, within the bound.
No kernel may reach another device: no remote copies, remote signals or barrier semaphores. Data moves between devices by JAX's collectives and lax.ppermute only.
A program may use at most 128 MiB of HBM per device.

v0:
```python
import jax
import jax.numpy as jnp
from jax import lax
from jax.sharding import PartitionSpec as P


def gelu_value(values):
    return 0.5 * values * (1.0 + lax.erf(values * 0.7071067811865476))


def gelu_slope(values):
    cumulative = 0.5 * (1.0 + lax.erf(values * 0.7071067811865476))
    density = jnp.exp(-0.5 * values * values) * 0.3989422804014327
    return cumulative + values * density


def local(tokens, gate_in, gate_out, twiddle, first_factor, second_factor, w_up, w_down, cotangent):
    local_chan, local_rows = tokens.shape
    factor_size = twiddle.shape[1]
    block_rows = local_rows // factor_size
    groups = lax.axis_size("chan")
    hid_block = w_up.shape[2]
    sub_width = hid_block // groups
    first_full, second_full = (
        lax.all_gather(first_factor, ("seq", "chan"), axis=0, tiled=True),
        lax.all_gather(second_factor, ("seq", "chan"), axis=0, tiled=True),
    )
    gated = (tokens.astype(jnp.float32) * gate_in.astype(jnp.float32)).astype(jnp.bfloat16)
    gated_cube = gated.reshape(local_chan, block_rows, factor_size)
    segment_cube = (
        jnp.einsum("kb,cab->kac", first_full, gated_cube, preferred_element_type=jnp.float32)
        * twiddle.T[:, :, None]
    ).astype(jnp.bfloat16)
    segment_flat = segment_cube.reshape(factor_size, block_rows * local_chan)
    moved_flat = lax.all_to_all(segment_flat, "seq", split_axis=0, concat_axis=1, tiled=True)
    moved_in = moved_flat.reshape(block_rows, factor_size, local_chan)
    product_part = jnp.einsum(
        "ja,kac->ckj", second_full, moved_in, preferred_element_type=jnp.float32
    )
    arrived = jnp.transpose(moved_in, (2, 0, 1))
    mixer = (product_part.reshape(local_chan, local_rows) * gate_out.astype(jnp.float32)).astype(
        jnp.bfloat16
    )
    hidden = lax.dot_general(
        w_up[0], mixer, (((0,), (0,)), ((), ())), preferred_element_type=jnp.float32
    )
    spread_act = gelu_value(hidden).astype(jnp.bfloat16).reshape(groups, sub_width, local_rows)
    permuted = lax.all_to_all(spread_act, "chan", split_axis=0, concat_axis=0, tiled=True).reshape(
        hid_block, local_rows
    )
    down_part = lax.dot_general(
        w_down[0], permuted, (((0,), (0,)), ((), ())), preferred_element_type=jnp.float32
    )
    mixed_out = (mixer.astype(jnp.float32) + down_part).astype(jnp.bfloat16)
    down_local = lax.dot_general(
        permuted, cotangent, (((1,), (1,)), ((), ())), preferred_element_type=jnp.float32
    )
    permuted_grad = jnp.dot(w_down[0], cotangent, preferred_element_type=jnp.float32).astype(
        jnp.bfloat16
    )
    act_grad = lax.all_to_all(
        permuted_grad.reshape(groups, sub_width, local_rows),
        "chan",
        split_axis=0,
        concat_axis=0,
        tiled=True,
    ).reshape(hid_block, local_rows)
    hidden_grad = (act_grad.astype(jnp.float32) * gelu_slope(hidden)).astype(jnp.bfloat16)
    up_local = lax.dot_general(
        mixer, hidden_grad, (((1,), (1,)), ((), ())), preferred_element_type=jnp.float32
    )
    up_grad, down_grad = lax.psum((up_local, down_local), "seq")
    mixer_grad = cotangent.astype(jnp.float32) + jnp.dot(
        w_up[0], hidden_grad, preferred_element_type=jnp.float32
    )
    weighted = (
        (mixer_grad * gate_out.astype(jnp.float32))
        .astype(jnp.bfloat16)
        .reshape(local_chan, block_rows, factor_size)
    )
    back_one = jnp.einsum(
        "ja,ckj->akc", second_full, weighted, preferred_element_type=jnp.float32
    ).astype(jnp.bfloat16)
    returned = lax.all_to_all(
        back_one.reshape(factor_size, block_rows * local_chan),
        "seq",
        split_axis=0,
        concat_axis=1,
        tiled=True,
    )
    returned = returned.reshape(block_rows, factor_size, local_chan)
    shifted = (returned.astype(jnp.float32) * twiddle[:, :, None]).astype(jnp.bfloat16)
    spread = jnp.einsum(
        "kb,akc->cab", first_full, shifted, preferred_element_type=jnp.float32
    ).reshape(local_chan, local_rows)
    input_grad = (spread * gate_in.astype(jnp.float32)).astype(jnp.bfloat16)
    section = shifted
    first_grad = lax.psum_scatter(
        jnp.einsum("akc,cab->kb", section, gated_cube, preferred_element_type=jnp.float32),
        ("seq", "chan"),
        scatter_dimension=0,
        tiled=True,
    )
    section = weighted
    second_grad = lax.psum_scatter(
        jnp.einsum("ckj,cka->ja", section, arrived, preferred_element_type=jnp.float32),
        ("seq", "chan"),
        scatter_dimension=0,
        tiled=True,
    )
    return (mixed_out, input_grad, first_grad, second_grad, up_grad[None], down_grad[None])


def solution(mesh):
    placed = (
        P("chan", "seq"),
        P("chan", "seq"),
        P("chan", "seq"),
        P("seq", None),
        P(("seq", "chan"), None),
        P(("seq", "chan"), None),
        P("chan", None, None),
        P("chan", None, None),
        P("chan", "seq"),
    )
    return jax.shard_map(
        local,
        mesh=mesh,
        in_specs=placed,
        out_specs=(
            P("chan", "seq"),
            P("chan", "seq"),
            P(("seq", "chan"), None),
            P(("seq", "chan"), None),
            P("chan", None, None),
            P("chan", None, None),
        ),
        check_vma=False,
    )
```

profile of v0, /device:TPU:1, one launch (start us, length us, event | category | flops | bytes accessed | tf_op | source)
XLA Modules:
  0.0 1879.8 jit_solution(7303218868037803315)
XLA Ops:
  7.2 0.0 copy-start
  7.2 0.0 all-gather.5.cloned.1.call-start
  7.2 0.7 all-gather.5.cloned.1.call-update
  7.9 0.0 all-gather.7.cloned.1.call-start
  8.0 0.7 all-gather.7.cloned.1.call-update
  8.7 2.7 fusion.11
  11.4 0.0 copy-start.6
  11.4 1.4 copy-done.6
  12.7 2.5 copy.46
  15.3 405.2 %all-gather.5.cloned.1.call-done = bf16[256,4,1024]{2,1,0:T(4,128)(2,1)} async-done(((bf16[1,4,1024]{2,1,0:T(4,128)(2,1)}), bf16[256,4,1024]{2,1,0:T(4,128)(2,1)}) %all-gather.5.cloned.1.call-update) | async-done | bytes 2097168 | tf_op jit(solution)/shard_map/all_gather | solution.py:25
  420.4 2.5 reshape.70
  423.0 6.0 fusion.14
  429.1 8.2 copy.29
  437.2 6.6 all_to_all.28
  443.9 7.7 all-to-all-start
  451.6 3.3 convolution_convert_fusion
  454.9 377.0 %all-gather.7.cloned.1.call-done = bf16[256,4,1024]{2,1,0:T(4,128)(2,1)} async-done(((bf16[1,4,1024]{2,1,0:T(4,128)(2,1)}), bf16[256,4,1024]{2,1,0:T(4,128)(2,1)}) %all-gather.7.cloned.1.call-update) | async-done | bytes 2097168 | tf_op jit(solution)/shard_map/all_gather | solution.py:26
  831.9 3.9 reshape.71
  835.9 0.0 all-to-all-done
  835.9 8.4 all-to-all-start.2
  844.3 4.1 copy.30
  848.3 6.4 reshape.57
  854.7 7.4 convolution_bitcast_fusion.6
  862.1 0.0 copy-start.7
  862.1 0.3 copy.44
  862.4 1.3 copy-done.7
  863.7 1.7 fusion.13
  865.4 26.3 %all-to-all-done.2 = bf16[4,32,16384]{2,1,0:T(8,128)(2,1)} async-done(((bf16[4,32,16384]{2,1,0:T(8,128)(2,1)}), bf16[4,32,16384]{2,1,0:T(8,128)(2,1)}, u32[]{:S(2)}, u32[]{:S(2)}) %all-to-all-start.2) | async-done | bytes 4194336 | tf_op jit(solution)/shard_map/all_to_all | solution.py:61
  891.6 8.8 fusion.10
  900.4 1.3 fusion.4
  901.7 0.7 copy-done.3
  902.4 1.2 copy.47
  903.6 1.4 copy-done.11
  905.0 3.7 convert_bitcast_fusion.1
  908.6 8.2 copy.33
  916.8 6.5 all_to_all.33
  923.3 8.2 all-to-all-start.3
  931.6 0.0 all-reduce.7.cloned.1.call-start
  931.6 5.9 copy.39
  937.6 6.5 convolution_bitcast_fusion.3
  944.1 35.4 %all-to-all-done.3 = bf16[64,16,1024]{2,1,0:T(8,128)(2,1)} async-done(((bf16[64,16,1024]{2,1,0:T(8,128)(2,1)}), bf16[64,16,1024]{2,1,0:T(8,128)(2,1)}, u32[]{:S(2)}, u32[]{:S(2)}) %all-to-all-start.3) | async-done | bytes 2097184 | tf_op jit(solution)/shard_map/all_to_all | solution.py:84
  979.5 2.0 convert_bitcast_fusion
  981.5 4.5 copy.34
  986.0 7.3 reshape.65
  993.3 9.0 convolution_bitcast_fusion.4
  1002.4 0.0 all-reduce.7.cloned.1.call-update
  1002.4 8.8 all-to-all-start.1
  1011.2 5.6 convolution_bitcast_fusion.8
  1016.8 51.7 %all-to-all-done.1 = bf16[4,32,16384]{2,1,0:T(8,128)(2,1)} async-done(((bf16[4,32,16384]{2,1,0:T(8,128)(2,1)}), bf16[4,32,16384]{2,1,0:T(8,128)(2,1)}, u32[]{:S(2)}, u32[]{:S(2)}) %all-to-all-start.1) | async-done | bytes 4194336 | tf_op jit(solution)/shard_map/all_to_all | solution.py:48
  1068.5 4.4 convolution_bitcast_fusion.7
  1072.9 5.0 fusion.3
  1077.9 0.0 all-reduce.9.cloned.1.call-update
  1078.0 7.5 convolution_bitcast_fusion.5
  1085.5 0.0 copy-start.9
  1085.5 0.6 copy.45
  1086.1 0.0 copy-start.1
  1086.1 1.0 copy-done.9
  1087.1 1.7 fusion.12
  1088.8 191.8 %all-reduce.7.cloned.1.call-done = (f32[1024,1024]{1,0:T(8,128)}, f32[1024,1024]{1,0:T(8,128)}) async-done(((f32[1024,1024]{1,0:T(8,128)}, f32[1024,1024]{1,0:T(8,128)}), (f32[1024,1024]{1,0:T(8,128)}, f32[1024,1024]{1,0:T(8,128)})) %all-reduce.7.cloned.1.call-update) | async-done | bytes 8388624
  1280.6 1.4 constant_dynamic-slice_fusion
  1282.0 588.3 %all-reduce.9.cloned.1.call-done = (f32[1,64,128]{2,1,0:T(8,128)}, f32[1,128,64]{1,2,0:T(8,128)}) async-done(((f32[1,64,128]{2,1,0:T(8,128)}, f32[1,128,64]{1,2,0:T(8,128)}), (f32[1,64,128]{2,1,0:T(8,128)}, f32[1,128,64]{1,2,0:T(8,128)})) %all-reduce.9.cloned.1.call-update) | async-done | bytes 65552 | tf_op jit(solution)/shard_map/psum | solution.py:72
  1870.3 1.4 copy.56
  1871.7 1.4 copy.57
  1873.1 0.0 copy-done.1
  (18 shorter events, 0.0 us)
Async XLA Ops:
  7.2 884.5 %copy-start = (bf16[1,64,128]{2,1,0:T(8,128)(2,1)S(1)}, bf16[1,64,128]{2,1,0:T(8,128)(2,1)}, u32[]{:S(2)}) copy-start(bf16[1,64,128]{2,1,0:T(8,128)(2,1)} %param.15) | copy-start | bytes 49156
  7.2 413.3 %all-gather.5.cloned.1.call-start = ((), (), s32[]{:S(2)}) async-start(), calls=%async_computation.4 | async-start | bytes 2105344 | tf_op jit(solution)/shard_map/all_gather | solution.py:25
  7.9 824.0 %all-gather.7.cloned.1.call-start = ((), (), s32[]{:S(2)}) async-start(), calls=%async_computation.5 | async-start | bytes 2105344 | tf_op jit(solution)/shard_map/all_gather | solution.py:26
  11.4 1.4 copy-start.6
  12.7 410.3 %copy-start.12 = (f32[16,1024]{1,0:T(8,128)S(1)}, f32[16,1024]{1,0:T(8,128)}, u32[]{:S(2)}) copy-start(f32[16,1024]{1,0:T(8,128)} %param.12) | copy-start | bytes 196612
  423.0 6.1 copy-start.4
  437.2 14.3 copy-start.2
  437.2 14.4 copy-start.13
  443.9 392.0 %all-to-all-start = ((bf16[64,16,1024]{2,1,0:T(8,128)(2,1)}), bf16[64,16,1024]{2,1,0:T(8,128)(2,1)}, u32[]{:S(2)}, u32[]{:S(2)}) async-start(bf16[64,16,1024]{2,1,0:T(8,128)(2,1)} %all_to_all.28), calls=%async_computation | async-start | bytes 4194304 | tf_op jit(solution)/shard_map/all_to_all | solution.py:35
  835.9 55.8 %all-to-all-start.2 = ((bf16[4,32,16384]{2,1,0:T(8,128)(2,1)}), bf16[4,32,16384]{2,1,0:T(8,128)(2,1)}, u32[]{:S(2)}, u32[]{:S(2)}) async-start(bf16[4,32,16384]{2,1,0:T(8,128)(2,1)} %bitcast.89), calls=%async_computation.2 | async-start | bytes 8388608 | tf_op jit(solution)/shard_map/all_to_all | solution.py:61
  862.1 1.6 copy-start.7
  891.6 8.8 copy-start.8
  900.4 2.0 copy-start.3
  902.4 2.6 copy-start.10
  903.6 1.4 copy-start.11
  923.3 56.2 %all-to-all-start.3 = ((bf16[64,16,1024]{2,1,0:T(8,128)(2,1)}), bf16[64,16,1024]{2,1,0:T(8,128)(2,1)}, u32[]{:S(2)}, u32[]{:S(2)}) async-start(bf16[64,16,1024]{2,1,0:T(8,128)(2,1)} %all_to_all.33), calls=%async_computation.3 | async-start | bytes 4194304 | tf_op jit(solution)/shard_map/all_to_all | solution.py:84
  931.6 349.1 %all-reduce.7.cloned.1.call-start = ((), (), s32[]{:S(2)}) async-start(), calls=%async_computation.6 | async-start | bytes 16777216
  1002.4 66.1 %all-to-all-start.1 = ((bf16[4,32,16384]{2,1,0:T(8,128)(2,1)}), bf16[4,32,16384]{2,1,0:T(8,128)(2,1)}, u32[]{:S(2)}, u32[]{:S(2)}) async-start(bf16[4,32,16384]{2,1,0:T(8,128)(2,1)} %bitcast.95), calls=%async_computation.1 | async-start | bytes 8388608 | tf_op jit(solution)/shard_map/all_to_all | solution.py:48
  1011.2 859.1 %all-reduce.9.cloned.1.call-start = ((), (), s32[]{:S(2)}) async-start(), calls=%async_computation.7 | async-start | bytes 131072 | tf_op jit(solution)/shard_map/psum | solution.py:72
  1072.9 5.1 copy-start.5
  1085.5 1.6 copy-start.9
  1086.1 787.0 %copy-start.1 = (bf16[1,64,128]{2,1,0:T(8,128)(2,1)S(1)}, bf16[1,64,128]{2,1,0:T(8,128)(2,1)}, u32[]{:S(2)}) copy-start(bf16[1,64,128]{2,1,0:T(8,128)(2,1)} %param.15) | copy-start | bytes 49156
Sparse Core Ops, SparseCore 0:
  9.9 410.4 all-gather.4
  422.3 409.5 all-gather.6
  1002.5 278.0 all-reduce.6
  1284.0 586.3 all-reduce.8
where the time goes:
time: 1900 us; the launch traced here: 1880 us
  waiting for transfers between devices  1680 us (88%)
  local copies, waits for them, and re-layouts  78.7 us (4%)
  matrix products  68.5 us (4%)
  starting transfers between devices  33.3 us (2%)
    psum x1, waiting for transfers between devices, local(): up_grad, down_grad = lax.psum((up_local, down_local), 'seq')  588 us
    all_gather x1, waiting for transfers between devices, local(): lax.all_gather(first_factor, ('seq', 'chan'), axis=0, tiled=True)  405 us
    all_gather x1, waiting for transfers between devices, local(): lax.all_gather(second_factor, ('seq', 'chan'), axis=0, tiled=True)  377 us
    unnamed x5, waiting for transfers between devices  193 us
    all_to_all x1, waiting for transfers between devices, local(): lax.all_to_all(spread_act, 'chan', split_axis=0, concat_axis=0, tiled=True)  51.7 us
  transfers between devices with their start and end apart: 8, of which 7 were waited for; matrix products, arithmetic and copies ran while one was open for 5% of the time, Pallas kernels for 0%

commit v1 on v0

v1 whole, which is shorter than its diff:
```python
import functools

import jax
import jax.numpy as jnp
import numpy as np
from jax import lax
from jax.experimental import pallas as pl
from jax.experimental.pallas import tpu as pltpu
from jax.sharding import Mesh
from jax.sharding import PartitionSpec as P

AXES = ("z", "yh", "x", "yl", "core")
SIZES = (8, 2, 4, 2, 2)
SEQ = ("z", "yh", "x")
CHAN = ("yl", "core")
PLANE = ("yh", "x", "yl")
F32 = jnp.float32
BF16 = jnp.bfloat16
MIB = 1024 * 1024


def params(mib, **kw):
    return pltpu.CompilerParams(vmem_limit_bytes=mib * MIB, **kw)


def cost(us, flops=0):
    return pl.CostEstimate(flops=flops, bytes_accessed=int(us * 3.0e6), transcendentals=0)


def full(shape):
    return pl.BlockSpec(shape, lambda i: (0,) * len(shape))


def nt(a, b):
    return lax.dot_general(a, b, (((1,), (1,)), ((), ())), preferred_element_type=F32)


def nn(a, b):
    return lax.dot_general(a, b, (((1,), (0,)), ((), ())), preferred_element_type=F32)


def tn(a, b):
    return lax.dot_general(a, b, (((0,), (0,)), ((), ())), preferred_element_type=F32)


def prep_kernel(tok_ref, gate_ref, cot_ref, wd_ref, rows_ref, *grad_refs):
    rows_ref[...] = (tok_ref[...].astype(F32) * gate_ref[...].astype(F32)).astype(BF16)
    grad = nn(wd_ref[...], cot_ref[...]).astype(BF16)
    for i, ref in enumerate(grad_refs):
        ref[...] = grad[i * 32 : (i + 1) * 32]


def prep(tokens, gate_in, cotangent, wd):
    chan, positions = tokens.shape
    blocks = positions // 1024
    cols = pl.BlockSpec((chan, 1024), lambda i: (0, i))
    part = pl.BlockSpec((32, 1024), lambda i: (0, i))
    return pl.pallas_call(
        prep_kernel,
        grid=(blocks,),
        in_specs=[cols, cols, cols, full(wd.shape)],
        out_specs=[pl.BlockSpec((chan, 1024), lambda i: (i, 0))] + [part] * 4,
        out_shape=[jax.ShapeDtypeStruct((blocks * chan, 1024), BF16)]
        + [jax.ShapeDtypeStruct((32, positions), BF16)] * 4,
        compiler_params=params(32),
        cost_estimate=cost(5),
        name="prep",
    )(tokens, gate_in, cotangent, wd)


def assemble_kernel(table_ref, own_ref, other_ref, out_ref):
    first = table_ref[16] == 0
    for m in range(16):
        at = table_ref[m]
        own, other = own_ref[at], other_ref[at]
        out_ref[:, m, :, :512] = jnp.where(first, own, other)
        out_ref[:, m, :, 512:] = jnp.where(first, other, own)


def assemble(own, other, table):
    out = pl.pallas_call(
        assemble_kernel,
        in_specs=[pl.BlockSpec(memory_space=pltpu.SMEM)] + [pl.BlockSpec(memory_space=pltpu.VMEM)] * 2,
        out_specs=pl.BlockSpec(memory_space=pltpu.VMEM),
        out_shape=jax.ShapeDtypeStruct((8, 16, 8, 1024), BF16),
        compiler_params=params(32),
        cost_estimate=cost(3),
        name="assemble",
    )(table, own, other)
    return out.reshape(1024, 1024)


def spread_twiddle(tw):
    high = tw.astype(BF16)
    rest = tw - high.astype(F32)
    mid = rest.astype(BF16)
    low = (rest - mid.astype(F32)).astype(BF16)
    terms = jnp.concatenate([high, mid, low], axis=0)
    row = lax.broadcasted_iota(jnp.int32, (48, 1024), 0)
    lane = lax.broadcasted_iota(jnp.int32, (48, 1024), 1)
    pick = jnp.where(row % 16 == lane // 64, 1.0, 0.0).astype(BF16)
    return tn(terms, pick)


def segment_kernel(first_ref, rows_ref, tw_ref, out_ref):
    scale = spread_twiddle(tw_ref[...])
    out_ref[...] = (nt(first_ref[...], rows_ref[...]) * scale).astype(BF16)


def segment(first, rows, tw):
    return pl.pallas_call(
        segment_kernel,
        grid=(4,),
        in_specs=[
            pl.BlockSpec((256, 1024), lambda i: (i, 0)),
            full((1024, 1024)),
            pl.BlockSpec((16, 256), lambda i: (0, i)),
        ],
        out_specs=pl.BlockSpec((256, 1024), lambda i: (i, 0)),
        out_shape=jax.ShapeDtypeStruct((1024, 1024), BF16),
        compiler_params=params(32),
        cost_estimate=cost(6),
        name="segment",
    )(first, rows, tw)


def swap_lanes(values):
    return pltpu.roll(values, 64, 1)


def middle_kernel(
    moved_ref, second_ref, gate_ref, cot_ref, g0, g1, g2, g3, wu_ref,
    back_ref, left_ref, weighted_ref, mixer_ref, a0, a1, a2, a3, up_ref,
    wide_ref, prod_ref,
):
    step = pl.program_id(0)
    grads, acts = (g0, g1, g2, g3), (a0, a1, a2, a3)

    @pl.when(step == 0)
    def _():
        for p in range(8):
            wide_ref[p * 1024 : (p + 1) * 1024] = moved_ref[:, p * 128 : (p + 1) * 128].astype(F32)
        up_ref[...] = jnp.zeros_like(up_ref)

    low = lax.broadcasted_iota(jnp.int32, (64, 128), 1) < 64
    for pair in range(2):
        k = step * 4 + pair * 2
        for p in range(8):
            lanes = slice(p * 128, (p + 1) * 128)
            one = wide_ref[pl.ds(p * 1024 + k, 64, stride=16)]
            two = wide_ref[pl.ds(p * 1024 + k + 1, 64, stride=16)]
            both = jnp.concatenate(
                [jnp.where(low, one, swap_lanes(two)), jnp.where(low, swap_lanes(one), two)], axis=0
            )
            left_ref[pair * 128 : (pair + 1) * 128, lanes] = both.T.astype(BF16)
    prod_ref[...] = nt(left_ref[...], second_ref[...])
    wu = wu_ref[...]
    width = 256
    up = jnp.zeros((64, 128), F32)
    for kk in range(4):
        for t in range(0, 1024, width):
            at = slice(kk * 1024 + t, kk * 1024 + t + width)
            gate = gate_ref[:, at].astype(F32)
            mix = (prod_ref[kk * 64 : (kk + 1) * 64, t : t + width] * gate).astype(BF16)
            mixer_ref[:, at] = mix
            hidden = tn(wu, mix)
            cum = 0.5 * (1.0 + lax.erf(hidden * 0.7071067811865476))
            act = (hidden * cum).astype(BF16)
            slope = cum + hidden * (jnp.exp(-0.5 * hidden * hidden) * 0.3989422804014327)
            for i in range(4):
                acts[i][:, at] = act[i * 32 : (i + 1) * 32]
            grad = jnp.concatenate([g[:, at] for g in grads], axis=0)
            hgrad = (grad.astype(F32) * slope).astype(BF16)
            up += nt(mix, hgrad)
            mgrad = cot_ref[:, at].astype(F32) + nn(wu, hgrad)
            weighted_ref[kk * 64 : (kk + 1) * 64, t : t + width] = (mgrad * gate).astype(BF16)
    up_ref[...] += up
    prod_ref[...] = nn(weighted_ref[...], second_ref[...])
    for pair in range(2):
        k = step * 4 + pair * 2
        for p in range(8):
            lanes = slice(p * 128, (p + 1) * 128)
            both = prod_ref[pair * 128 : (pair + 1) * 128, lanes].T
            top, bottom = both[:64], both[64:]
            wide_ref[pl.ds(p * 1024 + k, 64, stride=16)] = jnp.where(low, top, swap_lanes(bottom))
            wide_ref[pl.ds(p * 1024 + k + 1, 64, stride=16)] = jnp.where(low, swap_lanes(top), bottom)

    @pl.when(step == 3)
    def _():
        for p in range(8):
            back_ref[:, p * 128 : (p + 1) * 128] = wide_ref[p * 1024 : (p + 1) * 1024].astype(BF16)


def middle(moved, second, gate_out, cotangent, grads, wu):
    chan, positions = gate_out.shape
    cols = pl.BlockSpec((chan, 4096), lambda i: (0, i))
    part = pl.BlockSpec((32, 4096), lambda i: (0, i))
    square = full((1024, 1024))
    rows = pl.BlockSpec((256, 1024), lambda i: (i, 0))
    big = jax.ShapeDtypeStruct((1024, 1024), BF16)
    small = jax.ShapeDtypeStruct((32, positions), BF16)
    return pl.pallas_call(
        middle_kernel,
        grid=(4,),
        in_specs=[square, square, cols, cols] + [part] * 4 + [full(wu.shape)],
        out_specs=[square, rows, rows, cols] + [part] * 4 + [full((64, 128))],
        out_shape=[big, big, big, jax.ShapeDtypeStruct((chan, positions), BF16)]
        + [small] * 4
        + [jax.ShapeDtypeStruct((64, 128), F32)],
        scratch_shapes=[pltpu.VMEM((8192, 128), F32), pltpu.VMEM((256, 1024), F32)],
        compiler_params=params(48),
        cost_estimate=cost(25),
        name="middle",
    )(moved, second, gate_out, cotangent, *grads, wu)


def split_columns(first, total, send_ref, keep_ref):
    for z in range(8):
        part = total[z * 128 : (z + 1) * 128].reshape(16, 8, 1024)
        lo, hi = part[:, :, :512], part[:, :, 512:]
        send_ref[:, z] = jnp.where(first, hi, lo).astype(BF16)
        keep_ref[:, z] = jnp.where(first, lo, hi)


def second_kernel(core_ref, weighted_ref, left_ref, send_ref, keep_ref):
    split_columns(core_ref[0] == 0, tn(weighted_ref[...], left_ref[...]), send_ref, keep_ref)


HALF = [
    jax.ShapeDtypeStruct((16, 8, 8, 512), BF16),
    jax.ShapeDtypeStruct((16, 8, 8, 512), F32),
]


def second_part(core, weighted, left):
    vmem = pl.BlockSpec(memory_space=pltpu.VMEM)
    return pl.pallas_call(
        second_kernel,
        in_specs=[pl.BlockSpec(memory_space=pltpu.SMEM), vmem, vmem],
        out_specs=[vmem, vmem],
        out_shape=HALF,
        compiler_params=params(40),
        cost_estimate=cost(7),
        name="second_part",
    )(core, weighted, left)


def first_kernel(core_ref, back_ref, rows_ref, tw_ref, send_ref, keep_ref, shifted_ref):
    for i in range(4):
        at = slice(i * 256, (i + 1) * 256)
        scale = spread_twiddle(tw_ref[:, at])
        shifted_ref[at] = (back_ref[at].astype(F32) * scale).astype(BF16)
    split_columns(core_ref[0] == 0, nn(shifted_ref[...], rows_ref[...]), send_ref, keep_ref)


def first_part(core, back, rows, tw):
    vmem = pl.BlockSpec(memory_space=pltpu.VMEM)
    return pl.pallas_call(
        first_kernel,
        in_specs=[pl.BlockSpec(memory_space=pltpu.SMEM), vmem, vmem, vmem],
        out_specs=[vmem, vmem, vmem],
        out_shape=HALF + [jax.ShapeDtypeStruct((1024, 1024), BF16)],
        compiler_params=params(40),
        cost_estimate=cost(7),
        name="first_part",
    )(core, back, rows, tw)


def input_kernel(shifted_ref, first_ref, gate_ref, out_ref):
    spread = tn(shifted_ref[...], first_ref[...])
    for q in range(4):
        at = slice(q * 1024, (q + 1) * 1024)
        out_ref[:, at] = (spread[q * 64 : (q + 1) * 64] * gate_ref[:, at].astype(F32)).astype(BF16)


def input_part(shifted, first, gate_in):
    cols = pl.BlockSpec((64, 4096), lambda i: (0, i))
    return pl.pallas_call(
        input_kernel,
        grid=(4,),
        in_specs=[pl.BlockSpec((1024, 256), lambda i: (0, i)), full((1024, 1024)), cols],
        out_specs=cols,
        out_shape=jax.ShapeDtypeStruct(gate_in.shape, BF16),
        compiler_params=params(32),
        cost_estimate=cost(7),
        name="input_part",
    )(shifted, first, gate_in)


def output_kernel(mixer_ref, p0, p1, p2, p3, cot_ref, wd_ref, out_ref, down_ref):
    @pl.when(pl.program_id(0) == 0)
    def _():
        down_ref[...] = jnp.zeros_like(down_ref)

    permuted = jnp.concatenate([p[...] for p in (p0, p1, p2, p3)], axis=0)
    out_ref[...] = (mixer_ref[...].astype(F32) + tn(wd_ref[...], permuted)).astype(BF16)
    down_ref[...] += nt(permuted, cot_ref[...])


def output_part(mixer, parts, cotangent, wd):
    cols = pl.BlockSpec((64, 4096), lambda i: (0, i))
    part = pl.BlockSpec((32, 4096), lambda i: (0, i))
    return pl.pallas_call(
        output_kernel,
        grid=(4,),
        in_specs=[cols] + [part] * 4 + [cols, full(wd.shape)],
        out_specs=[cols, full((128, 64))],
        out_shape=[jax.ShapeDtypeStruct(mixer.shape, BF16), jax.ShapeDtypeStruct((128, 64), F32)],
        compiler_params=params(32),
        cost_estimate=cost(8),
        name="output_part",
    )(mixer, *parts, cotangent, wd)


def swap(values, axis, bit):
    size = int(np.prod([SIZES[AXES.index(a)] for a in ((axis,) if isinstance(axis, str) else axis)]))
    return lax.ppermute(values, axis, [(i, i ^ bit) for i in range(size)])


def copies(values, count):
    return jnp.broadcast_to(values[None], (count,) + values.shape)


def chan_swap(parts):
    return [parts[0]] + [swap(parts[i], CHAN, i) for i in (1, 2, 3)]


def gather_factors(first, second, core):
    both = jnp.stack([first, second]).reshape(2, 4, 2, 512)
    mine = lax.dynamic_index_in_dim(both, core, 2, keepdims=False)
    theirs = lax.dynamic_index_in_dim(both, 1 - core, 2, keepdims=False)
    theirs = swap(theirs, "core", 1)
    rows = jnp.where(
        core == 0,
        jnp.concatenate([mine, theirs], axis=1),
        jnp.concatenate([theirs, mine], axis=1),
    )
    column = lax.all_to_all(copies(rows, 8), "z", 0, 0, tiled=True)
    plane = lax.all_to_all(copies(column, 16), PLANE, 0, 0, tiled=True)
    return plane[:, :, 0], plane[:, :, 1]


def scatter_sum(send, keep, core):
    total = (keep + swap(send, "core", 1).astype(F32)).astype(BF16)
    grads = total.shape[0]
    total = lax.all_to_all(jnp.swapaxes(total, 0, 1), PLANE, 0, 0, tiled=True)
    total = jnp.sum(total.astype(F32), axis=0)
    total = lax.all_to_all(jnp.swapaxes(total, 0, 1), "z", 0, 0, tiled=True)
    total = jnp.sum(total, axis=0).reshape(grads, 2, 4, 512)
    mine = lax.dynamic_index_in_dim(total, core, 1, keepdims=False)
    theirs = swap(lax.dynamic_index_in_dim(total, 1 - core, 1, keepdims=False), "core", 1)
    return jnp.where(
        core == 0,
        jnp.concatenate([mine, theirs], axis=2),
        jnp.concatenate([theirs, mine], axis=2),
    )


def local(tokens, gate_in, gate_out, twiddle, first_factor, second_factor, w_up, w_down, cotangent):
    core = lax.axis_index("core")
    chan = lax.axis_index(CHAN)
    order = chan ^ jnp.arange(4, dtype=jnp.int32)
    core_word = core.astype(jnp.int32).reshape(1)
    table = jnp.concatenate([jnp.arange(16, dtype=jnp.int32), core_word])
    wd = w_down[0].reshape(4, 32, 64)[order].reshape(128, 64)
    wu = w_up[0].reshape(64, 4, 32)[:, order].reshape(64, 128)

    second_turned = jnp.swapaxes(second_factor.reshape(4, 64, 16), 1, 2).reshape(4, 1024)
    first_half, second_half = gather_factors(first_factor, second_turned, core)
    rows, *grads = prep(tokens, gate_in, cotangent, wd)
    first = assemble(first_half, swap(first_half, "core", 1), table)
    seg = segment(first, rows, twiddle)
    moved = lax.all_to_all(seg.reshape(64, 16, 1024), SEQ, 0, 0, tiled=True).reshape(1024, 1024)
    grads = chan_swap(grads)
    second = assemble(second_half, swap(second_half, "core", 1), table)
    back, left, weighted, mixer, *rest = middle(moved, second, gate_out, cotangent, grads, wu)
    acts, up = rest[:4], rest[4]
    returned = lax.all_to_all(back.reshape(64, 16, 1024), SEQ, 0, 0, tiled=True).reshape(1024, 1024)
    acts = chan_swap(acts)
    second_send, second_keep = second_part(core_word, weighted, left)
    mixed_out, down = output_part(mixer, acts, cotangent, wd)
    first_send, first_keep, shifted = first_part(core_word, returned, rows, twiddle)
    both = scatter_sum(
        jnp.stack([first_send, second_send]), jnp.stack([first_keep, second_keep]), core
    )
    input_grad = input_part(shifted, first, gate_in)
    first_grad = both[0]
    second_grad = jnp.swapaxes(both[1].reshape(4, 16, 64), 1, 2).reshape(4, 1024)
    up = up.reshape(64, 4, 32)[:, order].reshape(64, 128)
    down = down.reshape(4, 32, 64)[order].reshape(128, 64)
    small = jnp.concatenate([up, down.reshape(64, 128)], axis=0)
    for axis, bit in (("x", 1), ("x", 2), ("yh", 1), ("z", 1), ("z", 2), ("z", 4)):
        small = small + swap(small, axis, bit)
    return (
        mixed_out,
        input_grad,
        first_grad,
        second_grad,
        small[:64][None],
        small[64:].reshape(1, 128, 64),
    )


def solution(mesh):
    fine = Mesh(mesh.devices.reshape(SIZES), AXES)
    wide = P(CHAN, SEQ)
    factor = P(AXES, None)
    weight = P(CHAN, None, None)
    return jax.shard_map(
        local,
        mesh=fine,
        in_specs=(wide, wide, wide, P(SEQ, None), factor, factor, weight, weight, wide),
        out_specs=(wide, wide, factor, factor, weight, weight),
        check_vma=False,
    )
```

time: 1900 us -> 400 us (0.21); the launches traced: 1880 us -> 399 us
  waiting for transfers between devices: 1680 us -> 188 us
  matrix products: 68.5 us -> 0 us
  Pallas kernels: 0 us -> 59 us
  blocking collectives: 0 us -> 47.4 us
  local copies, waits for them, and re-layouts: 78.7 us -> 37.9 us
  starting transfers between devices: 33.3 us -> 62.1 us
    all_gather x2 -> x0, waiting for transfers between devices: 782 us -> none  [the longest x1 405 us: local(): lax.all_gather(first_factor, ('seq', 'chan'), axis=0, tiled=True)]
    psum x1 -> x0, waiting for transfers between devices: 588 us -> none  [local(): up_grad, down_grad = lax.psum((up_local, down_local), 'seq')]
    unnamed x5 -> x0, waiting for transfers between devices: 193 us -> none
    ppermute x0 -> x17, waiting for transfers between devices: none -> 146 us  [swap(): return lax.ppermute(values, axis, [(i, i ^ bit) for i in range(size)])]
    all_to_all x4, waiting for transfers between devices: 113 us -> 41.7 us  [the longest x1 41.6 us: local(): lax.all_to_all(back.reshape(64, 16, 1024), SEQ, 0, 0, tiled=True)]
    dot_general x12 -> x0, matrix products: 68.5 us -> none  [the longest x1 9.04 us: local(): jnp.einsum('akc,cab->kb', section, gated_cube, preferred_element_type=jnp...]
    pallas_call x0 -> x9, Pallas kernels: none -> 59 us  [the longest x1 30 us: middle(): pl.pallas_call(middle_kernel, grid=(4,), in_specs=[square, square, cols,...]
    all_to_all x0 -> x2, blocking collectives: none -> 47.4 us  [the longest x1 33.2 us: gather_factors(): plane = lax.all_to_all(copies(column, 16), PLANE, 0, 0, tiled=True)]
  transfers between devices with their start and end apart: 8 -> 21, of which waited for: 7 -> 14; matrix products, arithmetic and copies ran while one was open for 5% -> 2% of each run, Pallas kernels for 0% -> 4%
where the time goes in v1:
time: 400 us; the launch traced here: 399 us
  waiting for transfers between devices  188 us (47%)
  starting transfers between devices  62.1 us (16%)
  Pallas kernels  59 us (15%)
  blocking collectives  47.4 us (12%)
  local copies, waits for them, and re-layouts  37.9 us (9%)
    ppermute x17, waiting for transfers between devices, swap(): return lax.ppermute(values, axis, [(i, i ^ bit) for i in range(size)])  146 us
    all_to_all x1, waiting for transfers between devices, local(): lax.all_to_all(back.reshape(64, 16, 1024), SEQ, 0, 0, tiled=True)  41.6 us
    ppermute x17, starting transfers between devices, swap(): return lax.ppermute(values, axis, [(i, i ^ bit) for i in range(size)])  34.8 us
    all_to_all x1, blocking collectives, gather_factors(): plane = lax.all_to_all(copies(column, 16), PLANE, 0, 0, tiled=True)  33.2 us
    pallas_call x1, Pallas kernels, middle(): pl.pallas_call(middle_kernel, grid=(4,), in_specs=[square, square, cols,...  30 us
    unnamed x65, local copies, waits for them, and re-layouts  28.1 us
    all_to_all x1, blocking collectives, gather_factors(): column = lax.all_to_all(copies(rows, 8), 'z', 0, 0, tiled=True)  14.2 us
    all_to_all x1, starting transfers between devices, local(): lax.all_to_all(back.reshape(64, 16, 1024), SEQ, 0, 0, tiled=True)  12 us
  transfers between devices with their start and end apart: 21, of which 14 were waited for; matrix products, arithmetic and copies ran while one was open for 2% of the time, Pallas kernels for 4%

profile of v1, /device:TPU:1, one launch (start us, length us, event | category | flops | bytes accessed | tf_op | source)
XLA Modules:
  0.0 398.9 jit_solution(15622366230644601300)
XLA Ops:
  2.4 3.3 collective-permute-start
  5.8 0.8 collective-permute-done
  6.6 14.2 %all_to_all.30 = bf16[8,2,8,512]{3,2,1,0:T(8,128)(2,1)S(1)} all-to-all(bf16[8,2,8,512]{3,2,1,0:T(8,128)(2,1)S(1)} %broadcast_in_dim.6), channel_id=1, replica_groups=mesh['z'=8,'yh'=2,'x'=4,'yl'=2,'core'=2] {'z'}, dimensions={0} | all-to-all | bytes 262144 | tf_op jit(solution)/shard_map/all_to_all | solution.py:338
  21.1 33.2 %all_to_all.31 = bf16[16,8,2,8,512]{4,3,1,2,0:T(8,128)(2,1)S(1)} all-to-all(bf16[16,8,2,8,512]{4,3,1,2,0:T(8,128)(2,1)S(1)} %broadcast_in_dim.7), channel_id=1, replica_groups=mesh['z'=8,'yh'=2,'x'=4,'yl'=2,'core'=2] {'yh','x','yl'}, dimensions={0} | all-to-all | bytes 4194304 | tf_op jit(solution)/shard_map/all_to_all | solution.py:339
  54.2 1.2 slice_bitcast_fusion
  55.4 2.7 collective-permute-start.1
  58.8 1.6 copy-done.5
  60.4 1.6 copy-done.8
  62.0 4.9 %prep.1 = (bf16[1024,1024]{1,0:T(8,128)(2,1)S(1)}, bf16[32,16384]{1,0:T(8,128)(2,1)S(1)}, bf16[32,16384]{1,0:T(8,128)(2,1)S(1)}, bf16[32,16384]{1,0:T(8,128)(2,1)S(1)}, bf16[32,16384]{1,0:T(8,128)(2,1)S(1)}) custom-call(bf16[64,16384]{1,0:T(8,128)(2,1)S(1)} %copy-done.8, bf16[64,16384]{1,0:T(8,128)(2,1)S(1)} %copy-done.5, bf16[64,16384]{1,0:T(8,128)(2,1)S(1)} %copy-done, ...), custom_call_target="tpu_custom_call" | custom-call | bytes 15000000 | tf_op jit(solution)/shard_map/prep/pallas_call | solution.py:58
  66.9 1.0 copy-done.25
  67.9 1.0 copy-done.26
  68.9 3.1 assemble.2
  72.1 3.5 segment.1
  75.7 1.3 copy-done.4
  77.0 5.7 %all-to-all-start.2 = ((bf16[64,16,1024]{2,1,0:T(8,128)(2,1)}), bf16[64,16,1024]{2,1,0:T(8,128)(2,1)}, u32[]{:S(2)}, u32[]{:S(2)}) async-start(bf16[64,16,1024]{2,1,0:T(8,128)(2,1)} %bitcast.56), calls=%async_computation.2 | async-start | bytes 4194304 | tf_op jit(solution)/shard_map/all_to_all | solution.py:373
  83.6 1.4 collective-permute-start.5
  85.8 1.3 collective-permute-done.2.other_ref
  87.1 1.4 assemble.3
  88.5 1.3 copy-done.7
  89.8 38.4 %collective-permute-done.4.g2 = bf16[32,16384]{1,0:T(8,128)(2,1)} collective-permute-done((bf16[32,16384]{1,0:T(8,128)(2,1)}, bf16[32,16384]{1,0:T(8,128)(2,1)}, u32[]{:S(2)}, u32[]{:S(2)}) %collective-permute-start.4) | collective-permute-done | bytes 1048608 | tf_op jit(solution)/shard_map/ppermute | solution.py:317
  128.2 24.2 %collective-permute-done.5.g3 = bf16[32,16384]{1,0:T(8,128)(2,1)} collective-permute-done((bf16[32,16384]{1,0:T(8,128)(2,1)}, bf16[32,16384]{1,0:T(8,128)(2,1)}, u32[]{:S(2)}, u32[]{:S(2)}) %collective-permute-start.5) | collective-permute-done | bytes 1048608 | tf_op jit(solution)/shard_map/ppermute | solution.py:317
  152.5 1.2 copy-done.17
  153.7 30.0 %middle.1 = (bf16[1024,1024]{1,0:T(8,128)(2,1)}, bf16[1024,1024]{1,0:T(8,128)(2,1)}, bf16[1024,1024]{1,0:T(8,128)(2,1)}, bf16[64,16384]{1,0:T(8,128)(2,1)}, bf16...) custom-call(bf16[1024,1024]{1,0:T(8,128)(2,1)} %bitcast.8.moved_ref,, ...), custom_call_target="tpu_custom_call" | custom-call | bytes 75000000 | tf_op jit(solution)/shard_map/middle/pallas_call | solution.py:202
  183.7 1.0 copy-done.18
  184.6 1.0 copy-done.21
  185.7 1.0 copy-done.22
  186.6 1.0 copy-done.23
  187.6 12.0 %all-to-all-start.3 = ((bf16[64,16,1024]{2,1,0:T(8,128)(2,1)}), bf16[64,16,1024]{2,1,0:T(8,128)(2,1)}, u32[]{:S(2)}, u32[]{:S(2)}) async-start(bf16[64,16,1024]{2,1,0:T(8,128)(2,1)} %bitcast.65), calls=%async_computation.3 | async-start | bytes 4194304 | tf_op jit(solution)/shard_map/all_to_all | solution.py:378
  199.6 1.6 copy-done.9
  201.2 1.6 copy-done.10
  202.8 2.4 second_part.1
  205.2 1.3 copy-done.14
  206.5 41.6 %all-to-all-done.3 = bf16[64,16,1024]{2,1,0:T(8,128)(2,1)} async-done(((bf16[64,16,1024]{2,1,0:T(8,128)(2,1)}), bf16[64,16,1024]{2,1,0:T(8,128)(2,1)}, u32[]{:S(2)}, u32[]{:S(2)}) %all-to-all-start.3) | async-done | bytes 2097184 | tf_op jit(solution)/shard_map/all_to_all | solution.py:378
  248.1 1.6 copy-done.3
  249.7 4.5 %first_part.1 = (bf16[16,8,8,512]{3,2,1,0:T(8,128)(2,1)S(1)}, f32[16,8,8,512]{3,2,1,0:T(8,128)S(1)}, bf16[1024,1024]{1,0:T(8,128)(2,1)S(1)}) custom-call(s32[1]{0:T(128)} %bitcast.core_ref, bf16[1024,1024]{1,0:T(8,128)(2,1)} %bitcast.15.back_ref, bf16[1024,1024]{1,0:T(8,128)(2,1)S(1)} %copy-done.3, f32[16,1024]{1,0:T(8,128)S(1)} %copy-done.20), custom_call_target="tpu_custom_call" | custom-call | bytes 21000000 | tf_op jit(solution)/shard_map/first_part/pallas_call | solution.py:258
  254.4 1.1 copy-done.11
  255.5 3.3 collective-permute-start.9
  258.9 3.8 collective-permute-done.9
  262.7 0.8 fusion.1
  263.5 1.5 copy.60
  265.0 6.1 %all-to-all-start.4 = ((bf16[16,2,8,8,512]{4,3,2,1,0:T(8,128)(2,1)}), bf16[16,2,8,8,512]{4,3,2,1,0:T(8,128)(2,1)}, u32[]{:S(2)}, u32[]{:S(2)}) async-start(bf16[16,2,8,8,512]{4,3,2,1,0:T(8,128)(2,1)} %copy.60), calls=%async_computation.4 | async-start | bytes 4194304 | tf_op jit(solution)/shard_map/all_to_all | solution.py:346
  271.9 1.5 collective-permute-start.7
  274.5 43.4 %collective-permute-done.7.p2 = bf16[32,16384]{1,0:T(8,128)(2,1)} collective-permute-done((bf16[32,16384]{1,0:T(8,128)(2,1)}, bf16[32,16384]{1,0:T(8,128)(2,1)}, u32[]{:S(2)}, u32[]{:S(2)}) %collective-permute-start.7) | collective-permute-done | bytes 1048608 | tf_op jit(solution)/shard_map/ppermute | solution.py:317
  317.9 23.3 %collective-permute-done.8.p3 = bf16[32,16384]{1,0:T(8,128)(2,1)} collective-permute-done((bf16[32,16384]{1,0:T(8,128)(2,1)}, bf16[32,16384]{1,0:T(8,128)(2,1)}, u32[]{:S(2)}, u32[]{:S(2)}) %collective-permute-start.8) | collective-permute-done | bytes 1048608 | tf_op jit(solution)/shard_map/ppermute | solution.py:317
  341.2 1.6 copy-done.1
  342.7 1.6 copy-done.13
  344.3 5.0 %output_part.1 = (bf16[64,16384]{1,0:T(8,128)(2,1)}, f32[128,64]{1,0:T(8,128)S(1)}) custom-call(bf16[64,16384]{1,0:T(8,128)(2,1)S(1)} %copy-done.13, bf16[32,16384]{1,0:T(8,128)(2,1)S(1)} %copy-done.19, bf16[32,16384]{1,0:T(8,128)(2,1)} %collective-permute-done.6.p1, bf16[32,16384]{1,0:T(8,128)(2,1)} %collective-permute-done.7.p2, ...), custom_call_target="tpu_custom_call" | custom-call | bytes 24000000 | tf_op jit(solution)/shard_map/output_part/pallas_call | solution.py:303
  350.2 1.3 collective-permute-start.11
  351.4 1.9 convert_reduce_fusion
  354.1 3.4 all-to-all-start.5
  357.6 2.5 collective-permute-start.12
  360.1 2.9 collective-permute-done.12
  363.0 2.5 collective-permute-start.13
  365.5 2.2 collective-permute-done.13
  367.7 1.1 collective-permute-start.14
  368.8 2.1 collective-permute-done.14
  370.9 2.2 collective-permute-start.15
  373.1 1.9 collective-permute-done.15
  375.0 5.5 %collective-permute-start.16 = (f32[128,128]{0,1:T(8,128)S(1)}, f32[128,128]{0,1:T(8,128)S(1)}, u32[]{:S(2)}, u32[]{:S(2)}) collective-permute-start(f32[128,128]{0,1:T(8,128)S(1)} %add.57), channel_id=1, source_target_pairs={{0,128},{32,160},{64,192},{96,224},{128,0},{160,32},{192,64},{224,... | collective-permute-start | bytes 196616 | tf_op jit(solution)/shard_map/ppermute | solution.py:317
  380.5 1.9 collective-permute-done.16
  382.5 5.7 %collective-permute-start.10 = (f32[2,4,512]{2,1,0:T(4,128)S(1)}, f32[2,4,512]{2,1,0:T(4,128)S(1)}, u32[]{:S(2)}, u32[]{:S(2)}) collective-permute-start(f32[2,4,512]{2,1,0:T(4,128)S(1)} %bitcast.78), channel_id=1, source_target_pairs={{0,1},{1,0},{2,3},{3,2},{4,5},{5,4},{6,7},{7,6},{8,9},{9,8},{10,11... | collective-permute-start | bytes 49160 | tf_op jit(solution)/shard_map/ppermute | solution.py:317
  389.9 1.6 copy-done.6
  391.5 1.6 copy-done.12
  393.1 4.2 %input_part.1 = bf16[64,16384]{1,0:T(8,128)(2,1)} custom-call(bf16[1024,1024]{1,0:T(8,128)(2,1)S(1)} %copy-done.12, bf16[1024,1024]{1,0:T(8,128)(2,1)S(1)} %bitcast.55, bf16[64,16384]{1,0:T(8,128)(2,1)S(1)} %copy-done.6), custom_call_target="tpu_custom_call" | custom-call | bytes 21000000 | tf_op jit(solution)/shard_map/input_part/pallas_call | solution.py:278
  (102 shorter events, 11.5 us)
Async XLA Ops:
  2.4 4.2 %collective-permute-start = (bf16[2,4,512]{2,1,0:T(4,128)(2,1)S(1)}, bf16[2,4,512]{2,1,0:T(4,128)(2,1)S(1)}, u32[]{:S(2)}, u32[]{:S(2)}) collective-permute-start(bf16[2,4,512]{2,1,0:T(4,128)(2,1)S(1)} %bitcast.79), channel_id=1, source_target_pairs={{0,1},{1,0},{2,3},{3,2},{4,5},{5,4},{6,7},{7,6},{8,9},{9,8},{10,11... | collective-permute-start | bytes 24584 | tf_op jit(solution)/shard_map/ppermute | solution.py:317
  54.2 3.9 copy-start.27
  54.2 4.6 %copy-start = (bf16[64,16384]{1,0:T(8,128)(2,1)S(1)}, bf16[64,16384]{1,0:T(8,128)(2,1)}, u32[]{:S(2)}) copy-start(bf16[64,16384]{1,0:T(8,128)(2,1)} %cot_ref.5) | copy-start | bytes 6291460
  55.4 13.5 %collective-permute-start.1 = (bf16[16,8,8,512]{3,2,1,0:T(8,128)(2,1)}, bf16[16,8,8,512]{3,2,1,0:T(8,128)(2,1)}, u32[]{:S(2)}, u32[]{:S(2)}) collective-permute-start(bf16[16,8,8,512]{3,2,1,0:T(8,128)(2,1)} %get-tuple-element.73.own_ref), channel_id=1, source_target_pairs={{0,1},{1,0},{2,3},{3,2},{4,5},{5,4},{6,7},{7,6},{8,9},{9,8},{10,11... | collective-permute-start | bytes 3145736 | tf_op jit(solution)/shard_map/ppermute | solution.py:317
  58.8 1.6 copy-start.5
  60.4 1.6 copy-start.8
  66.9 1.0 copy-start.25
  67.9 1.0 copy-start.26
  68.8 3.2 copy-start.16
  68.8 3.3 copy-start.24
  68.8 3.3 copy-start.2
  68.9 3.2 copy-start.20
  75.7 1.3 copy-start.4
  77.0 8.0 %copy-start.28 = (bf16[1,64,128]{2,1,0:T(8,128)(2,1)S(1)}, bf16[1,64,128]{2,1,0:T(8,128)(2,1)}, u32[]{:S(2)}) copy-start(bf16[1,64,128]{2,1,0:T(8,128)(2,1)} %param.15) | copy-start | bytes 49156
  77.0 75.5 %all-to-all-start.2 = ((bf16[64,16,1024]{2,1,0:T(8,128)(2,1)}), bf16[64,16,1024]{2,1,0:T(8,128)(2,1)}, u32[]{:S(2)}, u32[]{:S(2)}) async-start(bf16[64,16,1024]{2,1,0:T(8,128)(2,1)} %bitcast.56), calls=%async_computation.2 | async-start | bytes 4194304 | tf_op jit(solution)/shard_map/all_to_all | solution.py:373
  82.7 7.1 %collective-permute-start.3 = (bf16[32,16384]{1,0:T(8,128)(2,1)}, bf16[32,16384]{1,0:T(8,128)(2,1)}, u32[]{:S(2)}, u32[]{:S(2)}) collective-permute-start(bf16[32,16384]{1,0:T(8,128)(2,1)} %copy-done.26), channel_id=1, source_target_pairs={{0,1},{1,0},{2,3},{3,2},{4,5},{5,4},{6,7},{7,6},{8,9},{9,8},{10,11... | collective-permute-start | bytes 3145736 | tf_op jit(solution)/shard_map/ppermute | solution.py:317
  82.9 4.2 %collective-permute-start.2 = (bf16[16,8,8,512]{3,2,1,0:T(8,128)(2,1)S(1)}, bf16[16,8,8,512]{3,2,1,0:T(8,128)(2,1)}, u32[]{:S(2)}, u32[]{:S(2)}) collective-permute-start(bf16[16,8,8,512]{3,2,1,0:T(8,128)(2,1)S(1)} %get-tuple-element.72.own_ref), channel_id=1, source_target_pairs={{0,1},{1,0},{2,3},{3,2},{4,5},{5,4},{6,7},{7,6},{8,9},{9,8},{10,11... | collective-permute-start | bytes 3145736 | tf_op jit(solution)/shard_map/ppermute | solution.py:317
  83.3 44.9 %collective-permute-start.4 = (bf16[32,16384]{1,0:T(8,128)(2,1)}, bf16[32,16384]{1,0:T(8,128)(2,1)}, u32[]{:S(2)}, u32[]{:S(2)}) collective-permute-start(bf16[32,16384]{1,0:T(8,128)(2,1)} %copy-done.25), channel_id=1, source_target_pairs={{0,2},{1,3},{2,0},{3,1},{4,6},{5,7},{6,4},{7,5},{8,10},{9,11},{10,... | collective-permute-start | bytes 3145736 | tf_op jit(solution)/shard_map/ppermute | solution.py:317
  83.6 68.8 %collective-permute-start.5 = (bf16[32,16384]{1,0:T(8,128)(2,1)}, bf16[32,16384]{1,0:T(8,128)(2,1)}, u32[]{:S(2)}, u32[]{:S(2)}) collective-permute-start(bf16[32,16384]{1,0:T(8,128)(2,1)} %copy-done.24), channel_id=1, source_target_pairs={{0,3},{1,2},{2,1},{3,0},{4,7},{5,6},{6,5},{7,4},{8,11},{9,10},{10,... | collective-permute-start | bytes 3145736 | tf_op jit(solution)/shard_map/ppermute | solution.py:317
  88.5 1.3 copy-start.7
  152.5 1.2 copy-start.17
  183.7 1.0 copy-start.18
  184.6 1.0 copy-start.21
  185.7 1.0 copy-start.22
  186.6 1.0 copy-start.23
  187.6 60.5 %all-to-all-start.3 = ((bf16[64,16,1024]{2,1,0:T(8,128)(2,1)}), bf16[64,16,1024]{2,1,0:T(8,128)(2,1)}, u32[]{:S(2)}, u32[]{:S(2)}) async-start(bf16[64,16,1024]{2,1,0:T(8,128)(2,1)} %bitcast.65), calls=%async_computation.3 | async-start | bytes 4194304 | tf_op jit(solution)/shard_map/all_to_all | solution.py:378
  199.6 1.6 copy-start.9
  201.2 1.6 copy-start.10
  205.2 1.3 copy-start.14
  248.1 1.6 copy-start.3
  254.2 1.3 copy-start.11
  254.2 8.4 %copy-start.15 = (f32[16,8,8,512]{3,2,1,0:T(8,128)S(1)}, f32[16,8,8,512]{3,2,1,0:T(8,128)}, u32[]{:S(2)}) copy-start(f32[16,8,8,512]{3,2,1,0:T(8,128)} %copy-done.14) | copy-start | bytes 6291460
  255.5 7.1 %collective-permute-start.9 = (bf16[2,16,8,8,512]{4,3,2,1,0:T(8,128)(2,1)S(1)}, bf16[2,16,8,8,512]{4,3,2,1,0:T(8,128)(2,1)S(1)}, u32[]{:S(2)}, u32[]{:S(2)}) collective-permute-start(bf16[2,16,8,8,512]{4,3,2,1,0:T(8,128)(2,1)S(1)} %pad_maximum_fusion), channel_id=1, source_target_pairs={{0,1},{1,0},{2,3},{3,2},{4,5},{5,4},{6,7},{7,6},{8,9},{9,8},{10,11... | collective-permute-start | bytes 6291464 | tf_op jit(solution)/shard_map/ppermute | solution.py:317
  265.0 76.2 %copy-start.19 = (bf16[32,16384]{1,0:T(8,128)(2,1)S(1)}, bf16[32,16384]{1,0:T(8,128)(2,1)}, u32[]{:S(2)}) copy-start(bf16[32,16384]{1,0:T(8,128)(2,1)} %copy-done.18) | copy-start | bytes 3145732
  265.0 86.5 %all-to-all-start.4 = ((bf16[16,2,8,8,512]{4,3,2,1,0:T(8,128)(2,1)}), bf16[16,2,8,8,512]{4,3,2,1,0:T(8,128)(2,1)}, u32[]{:S(2)}, u32[]{:S(2)}) async-start(bf16[16,2,8,8,512]{4,3,2,1,0:T(8,128)(2,1)} %copy.60), calls=%async_computation.4 | async-start | bytes 4194304 | tf_op jit(solution)/shard_map/all_to_all | solution.py:346
  271.1 3.4 collective-permute-start.6
  271.9 46.0 %collective-permute-start.7 = (bf16[32,16384]{1,0:T(8,128)(2,1)}, bf16[32,16384]{1,0:T(8,128)(2,1)}, u32[]{:S(2)}, u32[]{:S(2)}) collective-permute-start(bf16[32,16384]{1,0:T(8,128)(2,1)} %copy-done.22), channel_id=1, source_target_pairs={{0,2},{1,3},{2,0},{3,1},{4,6},{5,7},{6,4},{7,5},{8,10},{9,11},{10,... | collective-permute-start | bytes 3145736 | tf_op jit(solution)/shard_map/ppermute | solution.py:317
  273.4 67.8 %collective-permute-start.8 = (bf16[32,16384]{1,0:T(8,128)(2,1)}, bf16[32,16384]{1,0:T(8,128)(2,1)}, u32[]{:S(2)}, u32[]{:S(2)}) collective-permute-start(bf16[32,16384]{1,0:T(8,128)(2,1)} %copy-done.21), channel_id=1, source_target_pairs={{0,3},{1,2},{2,1},{3,0},{4,7},{5,6},{6,5},{7,4},{8,11},{9,10},{10,... | collective-permute-start | bytes 3145736 | tf_op jit(solution)/shard_map/ppermute | solution.py:317
  341.2 1.6 copy-start.1
  342.7 1.6 copy-start.13
  350.2 7.3 %collective-permute-start.11 = (f32[128,128]{0,1:T(8,128)S(1)}, f32[128,128]{0,1:T(8,128)S(1)}, u32[]{:S(2)}, u32[]{:S(2)}) collective-permute-start(f32[128,128]{0,1:T(8,128)S(1)} %pad_maximum_fusion.1), channel_id=1, source_target_pairs={{0,4},{4,0},{8,12},{12,8},{1,5},{5,1},{9,13},{13,9},{2,6},{6,2},{1... | collective-permute-start | bytes 196616 | tf_op jit(solution)/shard_map/ppermute | solution.py:317
  354.1 28.4 %all-to-all-start.5 = ((f32[8,2,8,512]{3,2,1,0:T(8,128)}), f32[8,2,8,512]{3,2,1,0:T(8,128)S(1)}, u32[]{:S(2)}, u32[]{:S(2)}) async-start(f32[8,2,8,512]{3,2,1,0:T(8,128)} %copy.61), calls=%async_computation.5 | async-start | bytes 524288 | tf_op jit(solution)/shard_map/all_to_all | solution.py:348
  357.6 5.4 %collective-permute-start.12 = (f32[128,128]{0,1:T(8,128)S(1)}, f32[128,128]{0,1:T(8,128)S(1)}, u32[]{:S(2)}, u32[]{:S(2)}) collective-permute-start(f32[128,128]{0,1:T(8,128)S(1)} %fusion.5), channel_id=1, source_target_pairs={{0,8},{4,12},{8,0},{12,4},{1,9},{5,13},{9,1},{13,5},{2,10},{6,14},... | collective-permute-start | bytes 196616 | tf_op jit(solution)/shard_map/ppermute | solution.py:317
  363.0 4.7 %collective-permute-start.13 = (f32[128,128]{0,1:T(8,128)S(1)}, f32[128,128]{0,1:T(8,128)S(1)}, u32[]{:S(2)}, u32[]{:S(2)}) collective-permute-start(f32[128,128]{0,1:T(8,128)S(1)} %add.54), channel_id=1, source_target_pairs={{0,16},{16,0},{1,17},{17,1},{2,18},{18,2},{3,19},{19,3},{4,20},{20... | collective-permute-start | bytes 196616 | tf_op jit(solution)/shard_map/ppermute | solution.py:317
  367.7 3.2 collective-permute-start.14
  370.9 4.1 %collective-permute-start.15 = (f32[128,128]{0,1:T(8,128)S(1)}, f32[128,128]{0,1:T(8,128)S(1)}, u32[]{:S(2)}, u32[]{:S(2)}) collective-permute-start(f32[128,128]{0,1:T(8,128)S(1)} %add.56), channel_id=1, source_target_pairs={{0,64},{32,96},{64,0},{96,32},{128,192},{160,224},{192,128},{224,1... | collective-permute-start | bytes 196616 | tf_op jit(solution)/shard_map/ppermute | solution.py:317
  375.0 7.4 %collective-permute-start.16 = (f32[128,128]{0,1:T(8,128)S(1)}, f32[128,128]{0,1:T(8,128)S(1)}, u32[]{:S(2)}, u32[]{:S(2)}) collective-permute-start(f32[128,128]{0,1:T(8,128)S(1)} %add.57), channel_id=1, source_target_pairs={{0,128},{32,160},{64,192},{96,224},{128,0},{160,32},{192,64},{224,... | collective-permute-start | bytes 196616 | tf_op jit(solution)/shard_map/ppermute | solution.py:317
  382.5 14.8 %collective-permute-start.10 = (f32[2,4,512]{2,1,0:T(4,128)S(1)}, f32[2,4,512]{2,1,0:T(4,128)S(1)}, u32[]{:S(2)}, u32[]{:S(2)}) collective-permute-start(f32[2,4,512]{2,1,0:T(4,128)S(1)} %bitcast.78), channel_id=1, source_target_pairs={{0,1},{1,0},{2,3},{3,2},{4,5},{5,4},{6,7},{7,6},{8,9},{9,8},{10,11... | collective-permute-start | bytes 49160 | tf_op jit(solution)/shard_map/ppermute | solution.py:317
  389.9 1.6 copy-start.6
  391.5 1.6 copy-start.12

commit v2 on v1

--- a/solution.py
+++ b/solution.py
@@ -24,7 +24,7 @@
 
 
 def cost(us, flops=0):
-    return pl.CostEstimate(flops=flops, bytes_accessed=int(us * 3.0e6), transcendentals=0)
+    return pl.CostEstimate(flops=flops, bytes_accessed=int(us * 3.0e3), transcendentals=0)
 
 
 def full(shape):
@@ -43,29 +43,47 @@
     return lax.dot_general(a, b, (((0,), (0,)), ((), ())), preferred_element_type=F32)
 
 
-def prep_kernel(tok_ref, gate_ref, cot_ref, wd_ref, rows_ref, *grad_refs):
-    rows_ref[...] = (tok_ref[...].astype(F32) * gate_ref[...].astype(F32)).astype(BF16)
+def grads_kernel(cot_ref, wd_ref, *grad_refs):
     grad = nn(wd_ref[...], cot_ref[...]).astype(BF16)
     for i, ref in enumerate(grad_refs):
         ref[...] = grad[i * 32 : (i + 1) * 32]
 
 
-def prep(tokens, gate_in, cotangent, wd):
-    chan, positions = tokens.shape
-    blocks = positions // 1024
-    cols = pl.BlockSpec((chan, 1024), lambda i: (0, i))
-    part = pl.BlockSpec((32, 1024), lambda i: (0, i))
-    return pl.pallas_call(
-        prep_kernel,
-        grid=(blocks,),
-        in_specs=[cols, cols, cols, full(wd.shape)],
-        out_specs=[pl.BlockSpec((chan, 1024), lambda i: (i, 0))] + [part] * 4,
-        out_shape=[jax.ShapeDtypeStruct((blocks * chan, 1024), BF16)]
-        + [jax.ShapeDtypeStruct((32, positions), BF16)] * 4,
-        compiler_params=params(32),
-        cost_estimate=cost(5),
-        name="prep",
-    )(tokens, gate_in, cotangent, wd)
+def grads_part(cotangent, wd):
+    chan, positions = cotangent.shape
+    part = pl.BlockSpec((32, 4096), lambda i: (0, i))
+    return pl.pallas_call(
+        grads_kernel,
+        grid=(positions // 4096,),
+        in_specs=[pl.BlockSpec((chan, 4096), lambda i: (0, i)), full(wd.shape)],
+        out_specs=[part] * 4,
+        out_shape=[jax.ShapeDtypeStruct((32, positions), BF16)] * 4,
+        compiler_params=params(60),
+        cost_estimate=cost(4),
+        name="grads_part",
+    )(cotangent, wd)
+
+
+def gated_kernel(tok_ref, gate_ref, rows_ref):
+    for q in range(4):
+        at = slice(q * 1024, (q + 1) * 1024)
+        rows_ref[q * 64 : (q + 1) * 64] = (
+            tok_ref[:, at].astype(F32) * gate_ref[:, at].astype(F32)
+        ).astype(BF16)
+
+
+def gated_part(tokens, gate_in):
+    cols = pl.BlockSpec((64, 4096), lambda i: (0, i))
+    return pl.pallas_call(
+        gated_kernel,
+        grid=(4,),
+        in_specs=[cols, cols],
+        out_specs=pl.BlockSpec((256, 1024), lambda i: (i, 0)),
+        out_shape=jax.ShapeDtypeStruct((1024, 1024), BF16),
+        compiler_params=params(60),
+        cost_estimate=cost(4),
+        name="gated_part",
+    )(tokens, gate_in)
 
 
 def assemble_kernel(table_ref, own_ref, other_ref, out_ref):
@@ -83,11 +101,29 @@
         in_specs=[pl.BlockSpec(memory_space=pltpu.SMEM)] + [pl.BlockSpec(memory_space=pltpu.VMEM)] * 2,
         out_specs=pl.BlockSpec(memory_space=pltpu.VMEM),
         out_shape=jax.ShapeDtypeStruct((8, 16, 8, 1024), BF16),
-        compiler_params=params(32),
+        compiler_params=params(60),
         cost_estimate=cost(3),
         name="assemble",
     )(table, own, other)
     return out.reshape(1024, 1024)
+
+
+def fan_kernel(column_ref, *refs):
+    for m in range(refs[-1].shape[0]):
+        refs[-1][m] = column_ref[...]
+
+
+def fan(column, count, after):
+    vmem = pl.BlockSpec(memory_space=pltpu.VMEM)
+    return pl.pallas_call(
+        fan_kernel,
+        in_specs=[vmem] + [pl.BlockSpec(memory_space=pl.ANY)] * len(after),
+        out_specs=vmem,
+        out_shape=jax.ShapeDtypeStruct((count,) + column.shape, BF16),
+        compiler_params=params(60),
+        cost_estimate=cost(1),
+        name="fan",
+    )(column, *after)
 
 
 def spread_twiddle(tw):
@@ -118,7 +154,7 @@
         ],
         out_specs=pl.BlockSpec((256, 1024), lambda i: (i, 0)),
         out_shape=jax.ShapeDtypeStruct((1024, 1024), BF16),
-        compiler_params=params(32),
+        compiler_params=params(60),
         cost_estimate=cost(6),
         name="segment",
     )(first, rows, tw)
@@ -208,22 +244,26 @@
         + [small] * 4
         + [jax.ShapeDtypeStruct((64, 128), F32)],
         scratch_shapes=[pltpu.VMEM((8192, 128), F32), pltpu.VMEM((256, 1024), F32)],
-        compiler_params=params(48),
+        compiler_params=params(60),
         cost_estimate=cost(25),
         name="middle",
     )(moved, second, gate_out, cotangent, *grads, wu)
 
 
-def split_columns(first, total, send_ref, keep_ref):
-    for z in range(8):
-        part = total[z * 128 : (z + 1) * 128].reshape(16, 8, 1024)
-        lo, hi = part[:, :, :512], part[:, :, 512:]
-        send_ref[:, z] = jnp.where(first, hi, lo).astype(BF16)
-        keep_ref[:, z] = jnp.where(first, lo, hi)
-
-
-def second_kernel(core_ref, weighted_ref, left_ref, send_ref, keep_ref):
-    split_columns(core_ref[0] == 0, tn(weighted_ref[...], left_ref[...]), send_ref, keep_ref)
+def split_columns(table_ref, total, send_ref, keep_ref):
+    first = table_ref[16] == 0
+    for m in range(16):
+        at = table_ref[m]
+        for z in range(8):
+            row = z * 128 + m * 8
+            lo, hi = total[row : row + 8, :512], total[row : row + 8, 512:]
+            send_ref[at, z] = jnp.where(first, hi, lo).astype(BF16)
+            keep_ref[at, z] = jnp.where(first, lo, hi)
+
+
+def second_kernel(table_ref, weighted_ref, left_ref, send_ref, keep_ref, total_ref):
+    total_ref[...] = tn(weighted_ref[...], left_ref[...])
+    split_columns(table_ref, total_ref, send_ref, keep_ref)
 
 
 HALF = [
@@ -232,38 +272,87 @@
 ]
 
 
-def second_part(core, weighted, left):
+def second_part(table, weighted, left):
     vmem = pl.BlockSpec(memory_space=pltpu.VMEM)
     return pl.pallas_call(
         second_kernel,
         in_specs=[pl.BlockSpec(memory_space=pltpu.SMEM), vmem, vmem],
         out_specs=[vmem, vmem],
         out_shape=HALF,
-        compiler_params=params(40),
+        scratch_shapes=[pltpu.VMEM((1024, 1024), F32)],
+        compiler_params=params(60),
         cost_estimate=cost(7),
         name="second_part",
-    )(core, weighted, left)
-
-
-def first_kernel(core_ref, back_ref, rows_ref, tw_ref, send_ref, keep_ref, shifted_ref):
+    )(table, weighted, left)
+
+
+def first_kernel(table_ref, back_ref, rows_ref, tw_ref, *refs):
+    send_ref, keep_ref, shifted_ref, total_ref = refs[-4:]
     for i in range(4):
         at = slice(i * 256, (i + 1) * 256)
         scale = spread_twiddle(tw_ref[:, at])
         shifted_ref[at] = (back_ref[at].astype(F32) * scale).astype(BF16)
-    split_columns(core_ref[0] == 0, nn(shifted_ref[...], rows_ref[...]), send_ref, keep_ref)
-
-
-def first_part(core, back, rows, tw):
+    total_ref[...] = nn(shifted_ref[...], rows_ref[...])
+    split_columns(table_ref, total_ref, send_ref, keep_ref)
+
+
+def first_part(table, back, rows, tw, after):
     vmem = pl.BlockSpec(memory_space=pltpu.VMEM)
     return pl.pallas_call(
         first_kernel,
-        in_specs=[pl.BlockSpec(memory_space=pltpu.SMEM), vmem, vmem, vmem],
+        in_specs=[pl.BlockSpec(memory_space=pltpu.SMEM), vmem, vmem, vmem]
+        + [pl.BlockSpec(memory_space=pl.ANY)] * len(after),
         out_specs=[vmem, vmem, vmem],
         out_shape=HALF + [jax.ShapeDtypeStruct((1024, 1024), BF16)],
-        compiler_params=params(40),
+        scratch_shapes=[pltpu.VMEM((1024, 1024), F32)],
+        compiler_params=params(60),
         cost_estimate=cost(7),
         name="first_part",
-    )(core, back, rows, tw)
+    )(table, back, rows, tw, *after)
+
+
+def join_kernel(keep_ref, got_ref, second_ref, after_ref, out_ref):
+    for m in range(16):
+        out_ref[m, 0] = (keep_ref[m] + got_ref[m].astype(F32)).astype(BF16)
+        out_ref[m, 1] = second_ref[m]
+
+
+def join(keep, got, second, after):
+    vmem = pl.BlockSpec(memory_space=pltpu.VMEM)
+    return pl.pallas_call(
+        join_kernel,
+        in_specs=[vmem] * 3 + [pl.BlockSpec(memory_space=pl.ANY)],
+        out_specs=vmem,
+        out_shape=jax.ShapeDtypeStruct((16, 2, 8, 8, 512), BF16),
+        compiler_params=params(60),
+        cost_estimate=cost(3),
+        name="join",
+    )(keep, got, second, after)
+
+
+def plane_sum_kernel(parts_ref, small_ref, after_ref, out_ref):
+    small = small_ref[...].astype(BF16)
+    for z in range(8):
+        for grad in range(2):
+            total = parts_ref[0, grad, z].astype(F32)
+            for m in range(1, 16):
+                total += parts_ref[m, grad, z].astype(F32)
+            out_ref[z, grad] = total.astype(BF16)
+        for i in range(4):
+            out_ref[z, 2 + i] = small[i * 8 : (i + 1) * 8]
+
+
+def plane_sum(parts, small, after):
+    vmem = pl.BlockSpec(memory_space=pltpu.VMEM)
+    return pl.pallas_call(
+        plane_sum_kernel,
+        in_specs=[vmem, vmem, pl.BlockSpec(memory_space=pl.ANY)],
+        out_specs=vmem,
+        out_shape=jax.ShapeDtypeStruct((8, 6, 8, 512), BF16),
+        compiler_params=params(60),
+        cost_estimate=cost(2),
+        name="plane_sum",
+    )(parts, small, after)
 
 
 def input_kernel(shifted_ref, first_ref, gate_ref, out_ref):
@@ -281,7 +370,7 @@
         in_specs=[pl.BlockSpec((1024, 256), lambda i: (0, i)), full((1024, 1024)), cols],
         out_specs=cols,
         out_shape=jax.ShapeDtypeStruct(gate_in.shape, BF16),
-        compiler_params=params(32),
+        compiler_params=params(60),
         cost_estimate=cost(7),
         name="input_part",
     )(shifted, first, gate_in)
@@ -306,7 +395,7 @@
         in_specs=[cols] + [part] * 4 + [cols, full(wd.shape)],
         out_specs=[cols, full((128, 64))],
         out_shape=[jax.ShapeDtypeStruct(mixer.shape, BF16), jax.ShapeDtypeStruct((128, 64), F32)],
-        compiler_params=params(32),
+        compiler_params=params(60),
         cost_estimate=cost(8),
         name="output_part",
     )(mixer, *parts, cotangent, wd)
@@ -317,15 +406,11 @@
     return lax.ppermute(values, axis, [(i, i ^ bit) for i in range(size)])
 
 
-def copies(values, count):
-    return jnp.broadcast_to(values[None], (count,) + values.shape)
-
-
 def chan_swap(parts):
     return [parts[0]] + [swap(parts[i], CHAN, i) for i in (1, 2, 3)]
 
 
-def gather_factors(first, second, core):
+def start_gather(first, second, core, after):
     both = jnp.stack([first, second]).reshape(2, 4, 2, 512)
     mine = lax.dynamic_index_in_dim(both, core, 2, keepdims=False)
     theirs = lax.dynamic_index_in_dim(both, 1 - core, 2, keepdims=False)
@@ -335,69 +420,65 @@
         jnp.concatenate([mine, theirs], axis=1),
         jnp.concatenate([theirs, mine], axis=1),
     )
-    column = lax.all_to_all(copies(rows, 8), "z", 0, 0, tiled=True)
-    plane = lax.all_to_all(copies(column, 16), PLANE, 0, 0, tiled=True)
-    return plane[:, :, 0], plane[:, :, 1]
-
-
-def scatter_sum(send, keep, core):
-    total = (keep + swap(send, "core", 1).astype(F32)).astype(BF16)
-    grads = total.shape[0]
-    total = lax.all_to_all(jnp.swapaxes(total, 0, 1), PLANE, 0, 0, tiled=True)
-    total = jnp.sum(total.astype(F32), axis=0)
-    total = lax.all_to_all(jnp.swapaxes(total, 0, 1), "z", 0, 0, tiled=True)
-    total = jnp.sum(total, axis=0).reshape(grads, 2, 4, 512)
-    mine = lax.dynamic_index_in_dim(total, core, 1, keepdims=False)
-    theirs = swap(lax.dynamic_index_in_dim(total, 1 - core, 1, keepdims=False), "core", 1)
-    return jnp.where(
-        core == 0,
-        jnp.concatenate([mine, theirs], axis=2),
-        jnp.concatenate([theirs, mine], axis=2),
-    )
+    column = lax.all_to_all(fan(rows, 8, after), "z", 0, 0, tiled=True)
+    return column
 
 
 def local(tokens, gate_in, gate_out, twiddle, first_factor, second_factor, w_up, w_down, cotangent):
     core = lax.axis_index("core")
     chan = lax.axis_index(CHAN)
     order = chan ^ jnp.arange(4, dtype=jnp.int32)
-    core_word = core.astype(jnp.int32).reshape(1)
-    table = jnp.concatenate([jnp.arange(16, dtype=jnp.int32), core_word])
+    table = jnp.concatenate([jnp.arange(16, dtype=jnp.int32), core.astype(jnp.int32).reshape(1)])
     wd = w_down[0].reshape(4, 32, 64)[order].reshape(128, 64)
     wu = w_up[0].reshape(64, 4, 32)[:, order].reshape(64, 128)
 
     second_turned = jnp.swapaxes(second_factor.reshape(4, 64, 16), 1, 2).reshape(4, 1024)
-    first_half, second_half = gather_factors(first_factor, second_turned, core)
-    rows, *grads = prep(tokens, gate_in, cotangent, wd)
+    grads = grads_part(cotangent, wd)
+    column = start_gather(first_factor, second_turned, core, [grads[0]])
+    rows = gated_part(tokens, gate_in)
+    grads = chan_swap(grads)
+    plane = lax.all_to_all(fan(column, 16, [grads[1], grads[2], rows]), PLANE, 0, 0, tiled=True)
+    first_half, second_half = plane[:, :, 0], plane[:, :, 1]
     first = assemble(first_half, swap(first_half, "core", 1), table)
     seg = segment(first, rows, twiddle)
     moved = lax.all_to_all(seg.reshape(64, 16, 1024), SEQ, 0, 0, tiled=True).reshape(1024, 1024)
-    grads = chan_swap(grads)
     second = assemble(second_half, swap(second_half, "core", 1), table)
     back, left, weighted, mixer, *rest = middle(moved, second, gate_out, cotangent, grads, wu)
     acts, up = rest[:4], rest[4]
     returned = lax.all_to_all(back.reshape(64, 16, 1024), SEQ, 0, 0, tiled=True).reshape(1024, 1024)
     acts = chan_swap(acts)
-    second_send, second_keep = second_part(core_word, weighted, left)
+    second_send, second_keep = second_part(table, weighted, left)
+    second_total = (second_keep + swap(second_send, "core", 1).astype(F32)).astype(BF16)
     mixed_out, down = output_part(mixer, acts, cotangent, wd)
-    first_send, first_keep, shifted = first_part(core_word, returned, rows, twiddle)
-    both = scatter_sum(
-        jnp.stack([first_send, second_send]), jnp.stack([first_keep, second_keep]), core
-    )
-    input_grad = input_part(shifted, first, gate_in)
-    first_grad = both[0]
-    second_grad = jnp.swapaxes(both[1].reshape(4, 16, 64), 1, 2).reshape(4, 1024)
     up = up.reshape(64, 4, 32)[:, order].reshape(64, 128)
     down = down.reshape(4, 32, 64)[order].reshape(128, 64)
-    small = jnp.concatenate([up, down.reshape(64, 128)], axis=0)
-    for axis, bit in (("x", 1), ("x", 2), ("yh", 1), ("z", 1), ("z", 2), ("z", 4)):
-        small = small + swap(small, axis, bit)
+    small = jnp.concatenate([up.reshape(16, 512), down.reshape(16, 512)], axis=0)
+    first_send, first_keep, shifted = first_part(
+        table, returned, rows, twiddle, [mixed_out, second_total]
+    )
+    small = (small + swap(small, "x", 1)) + (swap(small, "x", 2) + swap(small, "x", 3))
+    joined = join(first_keep, swap(first_send, "core", 1), second_total, small)
+    parts = lax.all_to_all(joined, PLANE, 0, 0, tiled=True)
+    input_grad = input_part(shifted, first, gate_in)
+    small = small + swap(small, "yh", 1)
+    both = lax.all_to_all(plane_sum(parts, small, input_grad), "z", 0, 0, tiled=True)
+    both = jnp.sum(both.astype(F32), axis=0)
+    small = both[2:].reshape(32, 512)
+    both = both[:2].reshape(2, 2, 4, 512)
+    mine = lax.dynamic_index_in_dim(both, core, 1, keepdims=False)
+    theirs = swap(lax.dynamic_index_in_dim(both, 1 - core, 1, keepdims=False), "core", 1)
+    both = jnp.where(
+        core == 0,
+        jnp.concatenate([mine, theirs], axis=2),
+        jnp.concatenate([theirs, mine], axis=2),
+    )
     return (
         mixed_out,
         input_grad,
-        first_grad,
-        second_grad,
-        small[:64][None],
-        small[64:].reshape(1, 128, 64),
+        both[0],
+        jnp.swapaxes(both[1].reshape(4, 16, 64), 1, 2).reshape(4, 1024),
+        small[:16].reshape(1, 64, 128),
+        small[16:].reshape(1, 128, 64),
     )
 
 

time: 400 us -> 361 us (0.902)
  waiting for transfers between devices: 188 us -> 140 us
  Pallas kernels: 59 us -> 88.9 us
  local copies, waits for them, and re-layouts: 37.9 us -> 17.4 us
  starting transfers between devices: 62.1 us -> 52.9 us
  blocking collectives: 47.4 us -> 51.9 us
    all_to_all x1, waiting for transfers between devices: 41.6 us -> 0.01 us  [local(): lax.all_to_all(back.reshape(64, 16, 1024), SEQ, 0, 0, tiled=True)]
    ppermute x17 -> x16, waiting for transfers between devices: 146 us -> 127 us  [swap(): return lax.ppermute(values, axis, [(i, i ^ bit) for i in range(size)])]
    unnamed x65 -> x39, local copies, waits for them, and re-layouts: 28.1 us -> 8.73 us
    ppermute x17 -> x16, starting transfers between devices: 34.8 us -> 18.9 us  [swap(): return lax.ppermute(values, axis, [(i, i ^ bit) for i in range(size)])]
    pallas_call x1 -> x6, Pallas kernels: 4.88 us -> 19.3 us  [the longest x1 4.82 us: grads_part(): pl.pallas_call(grads_kernel, grid=(positions // 4096,), in_specs=[pl.Bloc...]
    all_to_all x2, waiting for transfers between devices: 0.01 us -> 11.2 us  [the longest x1 7.62 us: local(): parts = lax.all_to_all(joined, PLANE, 0, 0, tiled=True)]
    all_to_all x1, starting transfers between devices: 5.71 us -> 10.8 us  [local(): lax.all_to_all(seg.reshape(64, 16, 1024), SEQ, 0, 0, tiled=True)]
    all_to_all x2, blocking collectives: 47.4 us -> 51.9 us  [the longest x1 31.7 us: local(): lax.all_to_all(fan(column, 16, [grads[1], grads[2], rows]), PLANE, 0, 0,...]
  transfers between devices with their start and end apart: 21 -> 20, of which waited for: 14 -> 14; matrix products, arithmetic and copies ran while one was open for 2% -> 3% of each run, Pallas kernels for 4% -> 8%
where the time goes in v2:
time: 361 us; the launch traced here: 358 us
  waiting for transfers between devices  140 us (39%)
  Pallas kernels  88.9 us (25%)
  starting transfers between devices  52.9 us (15%)
  blocking collectives  51.9 us (14%)
  local copies, waits for them, and re-layouts  17.4 us (5%)
  other arithmetic  5.52 us (2%)
    ppermute x16, waiting for transfers between devices, swap(): return lax.ppermute(values, axis, [(i, i ^ bit) for i in range(size)])  127 us
    all_to_all x1, blocking collectives, local(): lax.all_to_all(fan(column, 16, [grads[1], grads[2], rows]), PLANE, 0, 0,...  31.7 us
    pallas_call x1, Pallas kernels, middle(): pl.pallas_call(middle_kernel, grid=(4,), in_specs=[square, square, cols,...  30.3 us
    all_to_all x1, blocking collectives, local(): lax.all_to_all(plane_sum(parts, small, input_grad), 'z', 0, 0, tiled=True)  20.2 us
    ppermute x16, starting transfers between devices, swap(): return lax.ppermute(values, axis, [(i, i ^ bit) for i in range(size)])  18.9 us
    all_to_all x1, starting transfers between devices, local(): lax.all_to_all(seg.reshape(64, 16, 1024), SEQ, 0, 0, tiled=True)  10.8 us
    all_to_all x1, starting transfers between devices, local(): lax.all_to_all(back.reshape(64, 16, 1024), SEQ, 0, 0, tiled=True)  10 us
    unnamed x39, local copies, waits for them, and re-layouts  8.73 us
  transfers between devices with their start and end apart: 20, of which 14 were waited for; matrix products, arithmetic and copies ran while one was open for 3% of the time, Pallas kernels for 8%

profile of v2, /device:TPU:1, one launch (start us, length us, event | category | flops | bytes accessed | tf_op | source)
XLA Modules:
  0.0 357.8 jit_solution(11870461478508326292)
XLA Ops:
  0.7 0.8 copy.43
  1.5 1.2 gather_fusion
  2.7 4.8 %grads_part.1 = (bf16[32,16384]{1,0:T(8,128)(2,1)}, bf16[32,16384]{1,0:T(8,128)(2,1)}, bf16[32,16384]{1,0:T(8,128)(2,1)}, bf16[32,16384]{1,0:T(8,128)(2,1)}) custom-call(bf16[64,16384]{1,0:T(8,128)(2,1)} %cot_ref.5, bf16[128,64]{1,0:T(8,128)(2,1)} %bitcast.54), custom_call_target="tpu_custom_call" | custom-call | bytes 12000 | tf_op jit(solution)/shard_map/grads_part/pallas_call | solution.py:55
  7.5 3.2 collective-permute-start.1
  11.4 1.7 collective-permute-done
  13.1 0.6 maximum_select_fusion.1.column_ref
  13.7 1.4 fan.2
  15.0 7.1 %all-to-all-start = ((bf16[8,2,8,512]{3,2,1,0:T(8,128)(2,1)}), bf16[8,2,8,512]{3,2,1,0:T(8,128)(2,1)S(1)}, u32[]{:S(2)}, u32[]{:S(2)}) async-start(bf16[8,2,8,512]{3,2,1,0:T(8,128)(2,1)} %fan.2), calls=%async_computation | async-start | bytes 262144 | tf_op jit(solution)/shard_map/all_to_all | solution.py:423
  22.2 4.3 %gated_part.1.refs_2_.rows_ref = bf16[1024,1024]{1,0:T(8,128)(2,1)} custom-call(bf16[64,16384]{1,0:T(8,128)(2,1)} %tok_ref.1, bf16[64,16384]{1,0:T(8,128)(2,1)} %gate_ref.5), custom_call_target="tpu_custom_call" | custom-call | bytes 12000 | tf_op jit(solution)/shard_map/gated_part/pallas_call | solution.py:77
  26.5 3.6 %all-to-all-done.column_ref = bf16[8,2,8,512]{3,2,1,0:T(8,128)(2,1)S(1)} async-done(((bf16[8,2,8,512]{3,2,1,0:T(8,128)(2,1)}), bf16[8,2,8,512]{3,2,1,0:T(8,128)(2,1)S(1)}, u32[]{:S(2)}, u32[]{:S(2)}) %all-to-all-start) | async-done | bytes 131104 | tf_op jit(solution)/shard_map/all_to_all | solution.py:423
  30.1 5.6 %collective-permute-done.2.refs_1_.g2 = bf16[32,16384]{1,0:T(8,128)(2,1)S(1)} collective-permute-done((bf16[32,16384]{1,0:T(8,128)(2,1)}, bf16[32,16384]{1,0:T(8,128)(2,1)S(1)}, u32[]{:S(2)}, u32[]{:S(2)}) %collective-permute-start.2) | collective-permute-done | bytes 1048608 | tf_op jit(solution)/shard_map/ppermute | solution.py:406
  35.7 1.0 copy-done.4
  36.7 2.4 fan.3
  39.1 1.9 copy.44
  40.9 31.7 %all_to_all.30 = bf16[16,8,2,8,512]{4,3,1,2,0:T(8,128)(2,1)S(1)} all-to-all(bf16[16,8,2,8,512]{4,3,1,2,0:T(8,128)(2,1)S(1)} %copy.44), channel_id=1, replica_groups=mesh['z'=8,'yh'=2,'x'=4,'yl'=2,'core'=2] {'yh','x','yl'}, dimensions={0} | all-to-all | bytes 4194304 | tf_op jit(solution)/shard_map/all_to_all | solution.py:440
  72.9 2.5 collective-permute-start.3
  75.4 0.6 pad_add_fusion.table_ref
  76.0 1.6 collective-permute-done.3.other_ref
  77.7 1.0 copy-done.8
  78.7 3.0 assemble.2
  81.7 6.7 %segment.1 = bf16[1024,1024]{1,0:T(8,128)(2,1)} custom-call(bf16[1024,1024]{1,0:T(8,128)(2,1)} %bitcast.44, bf16[1024,1024]{1,0:T(8,128)(2,1)} %gated_part.1.refs_2_.rows_ref, f32[16,1024]{1,0:T(8,128)} %tw_ref.3), custom_call_target="tpu_custom_call" | custom-call | bytes 18000 | tf_op jit(solution)/shard_map/segment/pallas_call | solution.py:147
  88.3 10.8 %all-to-all-start.2 = ((bf16[64,16,1024]{2,1,0:T(8,128)(2,1)}), bf16[64,16,1024]{2,1,0:T(8,128)(2,1)S(1)}, u32[]{:S(2)}, u32[]{:S(2)}) async-start(bf16[64,16,1024]{2,1,0:T(8,128)(2,1)} %bitcast.46), calls=%async_computation.2 | async-start | bytes 4194304 | tf_op jit(solution)/shard_map/all_to_all | solution.py:444
  99.2 0.7 collective-permute-start.4
  100.1 0.6 gather_fusion.1
  100.6 0.7 copy.48.wu_ref
  101.3 1.0 collective-permute-done.4.other_ref
  102.4 3.1 assemble.3
  105.5 40.1 %collective-permute-done.5.g3 = bf16[32,16384]{1,0:T(8,128)(2,1)} collective-permute-done((bf16[32,16384]{1,0:T(8,128)(2,1)}, bf16[32,16384]{1,0:T(8,128)(2,1)}, u32[]{:S(2)}, u32[]{:S(2)}) %collective-permute-start.5) | collective-permute-done | bytes 1048608 | tf_op jit(solution)/shard_map/ppermute | solution.py:406
  145.6 2.3 all-to-all-done.2
  147.9 1.3 copy-done.2
  149.3 30.3 %middle.1 = (bf16[1024,1024]{1,0:T(8,128)(2,1)}, bf16[1024,1024]{1,0:T(8,128)(2,1)}, bf16[1024,1024]{1,0:T(8,128)(2,1)}, bf16[64,16384]{1,0:T(8,128)(2,1)}, bf16...) custom-call(bf16[1024,1024]{1,0:T(8,128)(2,1)} %bitcast.48, ...), custom_call_target="tpu_custom_call" | custom-call | bytes 75000 | tf_op jit(solution)/shard_map/middle/pallas_call | solution.py:238
  179.6 10.0 %all-to-all-start.3 = ((bf16[64,16,1024]{2,1,0:T(8,128)(2,1)}), bf16[64,16,1024]{2,1,0:T(8,128)(2,1)S(1)}, u32[]{:S(2)}, u32[]{:S(2)}) async-start(bf16[64,16,1024]{2,1,0:T(8,128)(2,1)} %bitcast.50), calls=%async_computation.3 | async-start | bytes 4194304 | tf_op jit(solution)/shard_map/all_to_all | solution.py:448
  189.6 1.2 collective-permute-start.6
  190.8 1.7 collective-permute-start.8
  192.6 6.5 %second_part.1 = (bf16[16,8,8,512]{3,2,1,0:T(8,128)(2,1)}, f32[16,8,8,512]{3,2,1,0:T(8,128)}) custom-call(s32[17]{0:T(128)} %pad_add_fusion.table_ref, bf16[1024,1024]{1,0:T(8,128)(2,1)} %get-tuple-element.37.weighted_ref, bf16[1024,1024]{1,0:T(8,128)(2,1)} %get-tuple-element.38.left_ref), custom_call_target="tpu_custom_call" | custom-call | bytes 21000 | tf_op jit(solution)/shard_map/second_part/pallas_call | solution.py:277
  199.2 37.4 %collective-permute-done.7.p2 = bf16[32,16384]{1,0:T(8,128)(2,1)} collective-permute-done((bf16[32,16384]{1,0:T(8,128)(2,1)}, bf16[32,16384]{1,0:T(8,128)(2,1)}, u32[]{:S(2)}, u32[]{:S(2)}) %collective-permute-start.7) | collective-permute-done | bytes 1048608 | tf_op jit(solution)/shard_map/ppermute | solution.py:406
  236.6 23.5 %collective-permute-done.8.p3 = bf16[32,16384]{1,0:T(8,128)(2,1)} collective-permute-done((bf16[32,16384]{1,0:T(8,128)(2,1)}, bf16[32,16384]{1,0:T(8,128)(2,1)}, u32[]{:S(2)}, u32[]{:S(2)}) %collective-permute-start.8) | collective-permute-done | bytes 1048608 | tf_op jit(solution)/shard_map/ppermute | solution.py:406
  260.1 5.9 %output_part.1 = (bf16[64,16384]{1,0:T(8,128)(2,1)}, f32[128,64]{1,0:T(8,128)}) custom-call(bf16[64,16384]{1,0:T(8,128)(2,1)} %get-tuple-element.30.mixer_ref, bf16[32,16384]{1,0:T(8,128)(2,1)} %get-tuple-element.31.p0, bf16[32,16384]{1,0:T(8,128)(2,1)} %collective-permute-done.6.p1, bf16[32,16384]{1,0:T(8,128)(2,1)} %collective-permute-done.7.p2, ...), custom_call_target="tpu_custom_call" | custom-call | bytes 24000 | tf_op jit(solution)/shard_map/output_part/pallas_call | solution.py:392
  266.0 2.9 add_convert_fusion.refs_1_.second_ref
  268.9 1.4 copy-done.1
  270.3 7.7 %first_part.1 = (bf16[16,8,8,512]{3,2,1,0:T(8,128)(2,1)}, f32[16,8,8,512]{3,2,1,0:T(8,128)}, bf16[1024,1024]{1,0:T(8,128)(2,1)}) custom-call(s32[17]{0:T(128)} %pad_add_fusion.table_ref, bf16[1024,1024]{1,0:T(8,128)(2,1)} %bitcast.47, bf16[1024,1024]{1,0:T(8,128)(2,1)} %gated_part.1.refs_2_.rows_ref, f32[16,1024]{1,0:T(8,128)} %tw_ref.3, ...), custom_call_target="tpu_custom_call" | custom-call | bytes 21000 | tf_op jit(solution)/shard_map/first_part/pallas_call | solution.py:301
  278.5 0.6 gather_fusion.2
  280.0 1.4 collective-permute-start.13
  281.4 0.9 collective-permute-start.12
  282.3 1.0 collective-permute-start.11
  283.3 1.5 collective-permute-done.13
  284.8 1.2 collective-permute-done.12
  286.2 0.6 add_add_fusion.after_ref
  286.8 1.0 copy-done.7
  287.8 3.8 %join.1 = bf16[16,2,8,8,512]{4,3,2,1,0:T(8,128)(2,1)} custom-call(f32[16,8,8,512]{3,2,1,0:T(8,128)} %get-tuple-element.42.keep_ref, bf16[16,8,8,512]{3,2,1,0:T(8,128)(2,1)} %copy-done.7, bf16[16,8,8,512]{3,2,1,0:T(8,128)(2,1)} %add_convert_fusion.refs_1_.second_ref, f32[32,512]{1,0:T(8,128)} %add_add_fusion.after_ref), custom_call_target="tpu_custom_call" | custom-call | bytes 9000 | tf_op jit(solution)/shard_map/join/pallas_call | solution.py:322
  291.6 5.9 %all-to-all-start.4 = ((bf16[16,2,8,8,512]{4,3,2,1,0:T(8,128)(2,1)}), bf16[16,2,8,8,512]{4,3,2,1,0:T(8,128)(2,1)S(1)}, u32[]{:S(2)}, u32[]{:S(2)}) async-start(bf16[16,2,8,8,512]{4,3,2,1,0:T(8,128)(2,1)} %join.1), calls=%async_computation.4 | async-start | bytes 4194304 | tf_op jit(solution)/shard_map/all_to_all | solution.py:461
  297.6 3.0 collective-permute-start.14
  300.5 12.8 %collective-permute-done.14 = f32[32,512]{1,0:T(8,128)S(1)} collective-permute-done((f32[32,512]{1,0:T(8,128)S(1)}, f32[32,512]{1,0:T(8,128)S(1)}, u32[]{:S(2)}, u32[]{:S(2)}) %collective-permute-start.14) | collective-permute-done | bytes 65568 | tf_op jit(solution)/shard_map/ppermute | solution.py:406
  313.4 0.6 add.50.small_ref
  314.0 6.5 %input_part.1.after_ref = bf16[64,16384]{1,0:T(8,128)(2,1)} custom-call(bf16[1024,1024]{1,0:T(8,128)(2,1)} %get-tuple-element.41.shifted_ref, bf16[1024,1024]{1,0:T(8,128)(2,1)} %bitcast.45, bf16[64,16384]{1,0:T(8,128)(2,1)} %gate_ref.5), custom_call_target="tpu_custom_call" | custom-call | bytes 21000 | tf_op jit(solution)/shard_map/input_part/pallas_call | solution.py:367
  320.5 7.6 %all-to-all-done.4.parts_ref = bf16[16,2,8,8,512]{4,3,2,1,0:T(8,128)(2,1)S(1)} async-done(((bf16[16,2,8,8,512]{4,3,2,1,0:T(8,128)(2,1)}), bf16[16,2,8,8,512]{4,3,2,1,0:T(8,128)(2,1)S(1)}, u32[]{:S(2)}, u32[]{:S(2)}) %all-to-all-start.4) | async-done | bytes 2097184 | tf_op jit(solution)/shard_map/all_to_all | solution.py:461
  328.1 1.3 copy-done
  329.4 2.6 plane_sum.1
  332.1 20.2 %all_to_all.31 = bf16[8,6,8,512]{3,2,1,0:T(8,128)(2,1)S(1)} all-to-all(bf16[8,6,8,512]{3,2,1,0:T(8,128)(2,1)} %plane_sum.1), channel_id=1, replica_groups=mesh['z'=8,'yh'=2,'x'=4,'yl'=2,'core'=2] {'z'}, dimensions={0} | all-to-all | bytes 786432 | tf_op jit(solution)/shard_map/all_to_all | solution.py:464
  352.3 2.5 collective-permute-start.15
  355.0 0.7 copy.54
  355.6 0.6 reshape.100
  356.3 0.6 fusion.2
  357.1 0.7 reshape.99
  (68 shorter events, 3.0 us)
Async XLA Ops:
  0.6 10.1 %copy-start.15 = (bf16[4,1024]{1,0:T(4,128)(2,1)S(1)}, bf16[4,1024]{1,0:T(4,128)(2,1)}, u32[]{:S(2)}) copy-start(bf16[4,1024]{1,0:T(4,128)(2,1)} %param.13) | copy-start | bytes 24580
  0.6 10.1 %copy-start.14 = (bf16[4,1024]{1,0:T(4,128)(2,1)S(1)}, bf16[4,1024]{1,0:T(4,128)(2,1)}, u32[]{:S(2)}) copy-start(bf16[4,1024]{1,0:T(4,128)(2,1)} %param.14) | copy-start | bytes 24580
  7.5 22.6 %collective-permute-start.1 = (bf16[32,16384]{1,0:T(8,128)(2,1)}, bf16[32,16384]{1,0:T(8,128)(2,1)S(1)}, u32[]{:S(2)}, u32[]{:S(2)}) collective-permute-start(bf16[32,16384]{1,0:T(8,128)(2,1)} %get-tuple-element.27), channel_id=1, source_target_pairs={{0,1},{1,0},{2,3},{3,2},{4,5},{5,4},{6,7},{7,6},{8,9},{9,8},{10,11... | collective-permute-start | bytes 3145736 | tf_op jit(solution)/shard_map/ppermute | solution.py:406
  10.8 24.9 %collective-permute-start.2 = (bf16[32,16384]{1,0:T(8,128)(2,1)}, bf16[32,16384]{1,0:T(8,128)(2,1)S(1)}, u32[]{:S(2)}, u32[]{:S(2)}) collective-permute-start(bf16[32,16384]{1,0:T(8,128)(2,1)} %get-tuple-element.28), channel_id=1, source_target_pairs={{0,2},{1,3},{2,0},{3,1},{4,6},{5,7},{6,4},{7,5},{8,10},{9,11},{10,... | collective-permute-start | bytes 3145736 | tf_op jit(solution)/shard_map/ppermute | solution.py:406
  11.2 1.9 collective-permute-start
  15.0 15.0 %all-to-all-start = ((bf16[8,2,8,512]{3,2,1,0:T(8,128)(2,1)}), bf16[8,2,8,512]{3,2,1,0:T(8,128)(2,1)S(1)}, u32[]{:S(2)}, u32[]{:S(2)}) async-start(bf16[8,2,8,512]{3,2,1,0:T(8,128)(2,1)} %fan.2), calls=%async_computation | async-start | bytes 262144 | tf_op jit(solution)/shard_map/all_to_all | solution.py:423
  30.1 5.6 %copy-start.10 = (bf16[8,2,8,512]{3,2,1,0:T(8,128)(2,1)}, bf16[8,2,8,512]{3,2,1,0:T(8,128)(2,1)S(1)}, u32[]{:S(2)}) copy-start(bf16[8,2,8,512]{3,2,1,0:T(8,128)(2,1)S(1)} %all-to-all-done.column_ref) | copy-start | bytes 393220
  30.1 5.6 %copy-start.3 = (bf16[32,16384]{1,0:T(8,128)(2,1)}, bf16[32,16384]{1,0:T(8,128)(2,1)S(1)}, u32[]{:S(2)}) copy-start(bf16[32,16384]{1,0:T(8,128)(2,1)S(1)} %collective-permute-done.1.refs_0_.g1) | copy-start | bytes 3145732
  35.7 1.0 copy-start.4
  72.9 4.8 %copy-start.6 = (bf16[16,8,8,512]{3,2,1,0:T(8,128)(2,1)}, bf16[16,8,8,512]{3,2,1,0:T(8,128)(2,1)S(1)}, u32[]{:S(2)}) copy-start(bf16[16,8,8,512]{3,2,1,0:T(8,128)(2,1)S(1)} %get-tuple-element.65.own_ref) | copy-start | bytes 3145732
  72.9 26.3 %copy-start.5 = (bf16[16,8,8,512]{3,2,1,0:T(8,128)(2,1)}, bf16[16,8,8,512]{3,2,1,0:T(8,128)(2,1)S(1)}, u32[]{:S(2)}) copy-start(bf16[16,8,8,512]{3,2,1,0:T(8,128)(2,1)S(1)} %get-tuple-element.64.own_ref) | copy-start | bytes 3145732
  72.9 4.8 %collective-permute-start.3 = (bf16[16,8,8,512]{3,2,1,0:T(8,128)(2,1)S(1)}, bf16[16,8,8,512]{3,2,1,0:T(8,128)(2,1)S(1)}, u32[]{:S(2)}, u32[]{:S(2)}) collective-permute-start(bf16[16,8,8,512]{3,2,1,0:T(8,128)(2,1)S(1)} %get-tuple-element.65.own_ref), channel_id=1, source_target_pairs={{0,1},{1,0},{2,3},{3,2},{4,5},{5,4},{6,7},{7,6},{8,9},{9,8},{10,11... | collective-permute-start | bytes 3145736 | tf_op jit(solution)/shard_map/ppermute | solution.py:406
  77.7 1.0 copy-start.8
  88.3 11.6 %copy-start.13 = (bf16[1,64,128]{2,1,0:T(8,128)(2,1)S(1)}, bf16[1,64,128]{2,1,0:T(8,128)(2,1)}, u32[]{:S(2)}) copy-start(bf16[1,64,128]{2,1,0:T(8,128)(2,1)} %param.15) | copy-start | bytes 49156
  88.3 59.6 %all-to-all-start.2 = ((bf16[64,16,1024]{2,1,0:T(8,128)(2,1)}), bf16[64,16,1024]{2,1,0:T(8,128)(2,1)S(1)}, u32[]{:S(2)}, u32[]{:S(2)}) async-start(bf16[64,16,1024]{2,1,0:T(8,128)(2,1)} %bitcast.46), calls=%async_computation.2 | async-start | bytes 4194304 | tf_op jit(solution)/shard_map/all_to_all | solution.py:444
  99.2 3.2 collective-permute-start.4
  99.9 45.7 %collective-permute-start.5 = (bf16[32,16384]{1,0:T(8,128)(2,1)}, bf16[32,16384]{1,0:T(8,128)(2,1)}, u32[]{:S(2)}, u32[]{:S(2)}) collective-permute-start(bf16[32,16384]{1,0:T(8,128)(2,1)} %get-tuple-element.29), channel_id=1, source_target_pairs={{0,3},{1,2},{2,1},{3,0},{4,7},{5,6},{6,5},{7,4},{8,11},{9,10},{10,... | collective-permute-start | bytes 3145736 | tf_op jit(solution)/shard_map/ppermute | solution.py:406
  147.9 1.3 copy-start.2
  179.6 89.3 %all-to-all-start.3 = ((bf16[64,16,1024]{2,1,0:T(8,128)(2,1)}), bf16[64,16,1024]{2,1,0:T(8,128)(2,1)S(1)}, u32[]{:S(2)}, u32[]{:S(2)}) async-start(bf16[64,16,1024]{2,1,0:T(8,128)(2,1)} %bitcast.50), calls=%async_computation.3 | async-start | bytes 4194304 | tf_op jit(solution)/shard_map/all_to_all | solution.py:448
  189.6 9.5 %collective-permute-start.6 = (bf16[32,16384]{1,0:T(8,128)(2,1)}, bf16[32,16384]{1,0:T(8,128)(2,1)}, u32[]{:S(2)}, u32[]{:S(2)}) collective-permute-start(bf16[32,16384]{1,0:T(8,128)(2,1)} %get-tuple-element.32), channel_id=1, source_target_pairs={{0,1},{1,0},{2,3},{3,2},{4,5},{5,4},{6,7},{7,6},{8,9},{9,8},{10,11... | collective-permute-start | bytes 3145736 | tf_op jit(solution)/shard_map/ppermute | solution.py:406
  190.8 45.7 %collective-permute-start.7 = (bf16[32,16384]{1,0:T(8,128)(2,1)}, bf16[32,16384]{1,0:T(8,128)(2,1)}, u32[]{:S(2)}, u32[]{:S(2)}) collective-permute-start(bf16[32,16384]{1,0:T(8,128)(2,1)} %get-tuple-element.33), channel_id=1, source_target_pairs={{0,2},{1,3},{2,0},{3,1},{4,6},{5,7},{6,4},{7,5},{8,10},{9,11},{10,... | collective-permute-start | bytes 3145736 | tf_op jit(solution)/shard_map/ppermute | solution.py:406
  190.8 69.2 %collective-permute-start.8 = (bf16[32,16384]{1,0:T(8,128)(2,1)}, bf16[32,16384]{1,0:T(8,128)(2,1)}, u32[]{:S(2)}, u32[]{:S(2)}) collective-permute-start(bf16[32,16384]{1,0:T(8,128)(2,1)} %get-tuple-element.34), channel_id=1, source_target_pairs={{0,3},{1,2},{2,1},{3,0},{4,7},{5,6},{6,5},{7,4},{8,11},{9,10},{10,... | collective-permute-start | bytes 3145736 | tf_op jit(solution)/shard_map/ppermute | solution.py:406
  199.0 66.9 %collective-permute-start.9 = (bf16[16,8,8,512]{3,2,1,0:T(8,128)(2,1)}, bf16[16,8,8,512]{3,2,1,0:T(8,128)(2,1)S(1)}, u32[]{:S(2)}, u32[]{:S(2)}) collective-permute-start(bf16[16,8,8,512]{3,2,1,0:T(8,128)(2,1)} %get-tuple-element.40), channel_id=1, source_target_pairs={{0,1},{1,0},{2,3},{3,2},{4,5},{5,4},{6,7},{7,6},{8,9},{9,8},{10,11... | collective-permute-start | bytes 3145736 | tf_op jit(solution)/shard_map/ppermute | solution.py:406
  268.9 1.4 copy-start.1
  270.3 8.1 %copy-start.12 = (f32[64,128]{1,0:T(8,128)S(1)}, f32[64,128]{1,0:T(8,128)}, u32[]{:S(2)}) copy-start(f32[64,128]{1,0:T(8,128)} %get-tuple-element.44) | copy-start | bytes 98308
  270.3 9.0 %copy-start.11 = (f32[128,64]{1,0:T(8,128)S(1)}, f32[128,64]{1,0:T(8,128)}, u32[]{:S(2)}) copy-start(f32[128,64]{1,0:T(8,128)} %get-tuple-element.45) | copy-start | bytes 98308
  278.0 8.8 %collective-permute-start.10 = (bf16[16,8,8,512]{3,2,1,0:T(8,128)(2,1)}, bf16[16,8,8,512]{3,2,1,0:T(8,128)(2,1)S(1)}, u32[]{:S(2)}, u32[]{:S(2)}) collective-permute-start(bf16[16,8,8,512]{3,2,1,0:T(8,128)(2,1)} %get-tuple-element.43), channel_id=1, source_target_pairs={{0,1},{1,0},{2,3},{3,2},{4,5},{5,4},{6,7},{7,6},{8,9},{9,8},{10,11... | collective-permute-start | bytes 3145736 | tf_op jit(solution)/shard_map/ppermute | solution.py:406
  280.0 4.8 %collective-permute-start.13 = (f32[32,512]{1,0:T(8,128)S(1)}, f32[32,512]{1,0:T(8,128)S(1)}, u32[]{:S(2)}, u32[]{:S(2)}) collective-permute-start(f32[32,512]{1,0:T(8,128)S(1)} %constant_dynamic-update-slice_fusion.2), channel_id=1, source_target_pairs={{0,12},{4,8},{8,4},{12,0},{1,13},{5,9},{9,5},{13,1},{2,14},{6,10},... | collective-permute-start | bytes 196616 | tf_op jit(solution)/shard_map/ppermute | solution.py:406
  281.4 4.6 %collective-permute-start.12 = (f32[32,512]{1,0:T(8,128)S(1)}, f32[32,512]{1,0:T(8,128)S(1)}, u32[]{:S(2)}, u32[]{:S(2)}) collective-permute-start(f32[32,512]{1,0:T(8,128)S(1)} %constant_dynamic-update-slice_fusion.2), channel_id=1, source_target_pairs={{0,8},{4,12},{8,0},{12,4},{1,9},{5,13},{9,1},{13,5},{2,10},{6,14},... | collective-permute-start | bytes 196616 | tf_op jit(solution)/shard_map/ppermute | solution.py:406
  282.3 3.9 %collective-permute-start.11 = (f32[32,512]{1,0:T(8,128)S(1)}, f32[32,512]{1,0:T(8,128)S(1)}, u32[]{:S(2)}, u32[]{:S(2)}) collective-permute-start(f32[32,512]{1,0:T(8,128)S(1)} %constant_dynamic-update-slice_fusion.2), channel_id=1, source_target_pairs={{0,4},{4,0},{8,12},{12,8},{1,5},{5,1},{9,13},{13,9},{2,6},{6,2},{1... | collective-permute-start | bytes 196616 | tf_op jit(solution)/shard_map/ppermute | solution.py:406
  286.8 1.0 copy-start.7
  291.6 6.0 %copy-start.9 = (f32[32,512]{1,0:T(8,128)S(1)}, f32[32,512]{1,0:T(8,128)}, u32[]{:S(2)}) copy-start(f32[32,512]{1,0:T(8,128)} %add_add_fusion.after_ref) | copy-start | bytes 196612
  291.6 36.5 %all-to-all-start.4 = ((bf16[16,2,8,8,512]{4,3,2,1,0:T(8,128)(2,1)}), bf16[16,2,8,8,512]{4,3,2,1,0:T(8,128)(2,1)S(1)}, u32[]{:S(2)}, u32[]{:S(2)}) async-start(bf16[16,2,8,8,512]{4,3,2,1,0:T(8,128)(2,1)} %join.1), calls=%async_computation.4 | async-start | bytes 4194304 | tf_op jit(solution)/shard_map/all_to_all | solution.py:461
  297.6 15.8 %collective-permute-start.14 = (f32[32,512]{1,0:T(8,128)S(1)}, f32[32,512]{1,0:T(8,128)S(1)}, u32[]{:S(2)}, u32[]{:S(2)}) collective-permute-start(f32[32,512]{1,0:T(8,128)S(1)} %copy-done.9), channel_id=1, source_target_pairs={{0,16},{16,0},{1,17},{17,1},{2,18},{18,2},{3,19},{19,3},{4,20},{20... | collective-permute-start | bytes 196616 | tf_op jit(solution)/shard_map/ppermute | solution.py:406
  328.1 1.3 copy-start
  352.3 3.9 %collective-permute-start.15 = (f32[2,4,512]{2,1,0:T(4,128)S(1)}, f32[2,4,512]{2,1,0:T(4,128)S(1)}, u32[]{:S(2)}, u32[]{:S(2)}) collective-permute-start(f32[2,4,512]{2,1,0:T(4,128)S(1)} %get-tuple-element.72), channel_id=1, source_target_pairs={{0,1},{1,0},{2,3},{3,2},{4,5},{5,4},{6,7},{7,6},{8,9},{9,8},{10,11... | collective-permute-start | bytes 49160 | tf_op jit(solution)/shard_map/ppermute | solution.py:406

commit v3 on v2

--- a/solution.py
+++ b/solution.py
@@ -86,22 +86,22 @@
     )(tokens, gate_in)
 
 
-def assemble_kernel(table_ref, own_ref, other_ref, out_ref):
+def assemble_kernel(factor, table_ref, own_ref, other_ref, out_ref):
     first = table_ref[16] == 0
     for m in range(16):
         at = table_ref[m]
-        own, other = own_ref[at], other_ref[at]
+        own, other = own_ref[at, factor], other_ref[at]
         out_ref[:, m, :, :512] = jnp.where(first, own, other)
         out_ref[:, m, :, 512:] = jnp.where(first, other, own)
 
 
-def assemble(own, other, table):
+def assemble(own, other, table, factor):
     out = pl.pallas_call(
-        assemble_kernel,
+        functools.partial(assemble_kernel, factor),
         in_specs=[pl.BlockSpec(memory_space=pltpu.SMEM)] + [pl.BlockSpec(memory_space=pltpu.VMEM)] * 2,
         out_specs=pl.BlockSpec(memory_space=pltpu.VMEM),
         out_shape=jax.ShapeDtypeStruct((8, 16, 8, 1024), BF16),
-        compiler_params=params(60),
+        compiler_params=params(12),
         cost_estimate=cost(3),
         name="assemble",
     )(table, own, other)
@@ -113,14 +113,21 @@
         refs[-1][m] = column_ref[...]
 
 
-def fan(column, count, after):
+def fan_plane_kernel(column_ref, *refs):
+    for m in range(16):
+        for z in range(8):
+            for factor in range(2):
+                refs[-1][m, factor, z] = column_ref[z, factor]
+
+
+def fan(kernel, column, shape, after):
     vmem = pl.BlockSpec(memory_space=pltpu.VMEM)
     return pl.pallas_call(
-        fan_kernel,
+        kernel,
         in_specs=[vmem] + [pl.BlockSpec(memory_space=pl.ANY)] * len(after),
         out_specs=vmem,
-        out_shape=jax.ShapeDtypeStruct((count,) + column.shape, BF16),
-        compiler_params=params(60),
+        out_shape=jax.ShapeDtypeStruct(shape, BF16),
+        compiler_params=params(10),
         cost_estimate=cost(1),
         name="fan",
     )(column, *after)
@@ -154,7 +161,7 @@
         ],
         out_specs=pl.BlockSpec((256, 1024), lambda i: (i, 0)),
         out_shape=jax.ShapeDtypeStruct((1024, 1024), BF16),
-        compiler_params=params(60),
+        compiler_params=params(24),
         cost_estimate=cost(6),
         name="segment",
     )(first, rows, tw)
@@ -191,25 +198,28 @@
             left_ref[pair * 128 : (pair + 1) * 128, lanes] = both.T.astype(BF16)
     prod_ref[...] = nt(left_ref[...], second_ref[...])
     wu = wu_ref[...]
-    width = 256
     up = jnp.zeros((64, 128), F32)
-    for kk in range(4):
-        for t in range(0, 1024, width):
-            at = slice(kk * 1024 + t, kk * 1024 + t + width)
-            gate = gate_ref[:, at].astype(F32)
-            mix = (prod_ref[kk * 64 : (kk + 1) * 64, t : t + width] * gate).astype(BF16)
-            mixer_ref[:, at] = mix
-            hidden = tn(wu, mix)
-            cum = 0.5 * (1.0 + lax.erf(hidden * 0.7071067811865476))
-            act = (hidden * cum).astype(BF16)
-            slope = cum + hidden * (jnp.exp(-0.5 * hidden * hidden) * 0.3989422804014327)
-            for i in range(4):
-                acts[i][:, at] = act[i * 32 : (i + 1) * 32]
-            grad = jnp.concatenate([g[:, at] for g in grads], axis=0)
-            hgrad = (grad.astype(F32) * slope).astype(BF16)
-            up += nt(mix, hgrad)
-            mgrad = cot_ref[:, at].astype(F32) + nn(wu, hgrad)
-            weighted_ref[kk * 64 : (kk + 1) * 64, t : t + width] = (mgrad * gate).astype(BF16)
+    for unit in range(0, 4, 4):
+        at = slice(unit * 1024, (unit + 4) * 1024)
+        for kk in range(unit, unit + 4):
+            cols = slice(kk * 1024, (kk + 1) * 1024)
+            gate = gate_ref[:, cols].astype(F32)
+            mixer_ref[:, cols] = (prod_ref[kk * 64 : (kk + 1) * 64] * gate).astype(BF16)
+        mix = mixer_ref[:, at]
+        hidden = tn(wu, mix)
+        cum = 0.5 * (1.0 + lax.erf(hidden * 0.7071067811865476))
+        act = (hidden * cum).astype(BF16)
+        slope = cum + hidden * (jnp.exp(-0.5 * hidden * hidden) * 0.3989422804014327)
+        for i in range(4):
+            acts[i][:, at] = act[i * 32 : (i + 1) * 32]
+        grad = jnp.concatenate([g[:, at] for g in grads], axis=0)
+        hgrad = (grad.astype(F32) * slope).astype(BF16)
+        up += nt(mix, hgrad)
+        mgrad = nn(wu, hgrad)
+        for kk in range(unit, unit + 4):
+            cols = slice(kk * 1024, (kk + 1) * 1024)
+            total = cot_ref[:, cols].astype(F32) + mgrad[:, (kk - unit) * 1024 : (kk - unit + 1) * 1024]
+            weighted_ref[kk * 64 : (kk + 1) * 64] = (total * gate_ref[:, cols].astype(F32)).astype(BF16)
     up_ref[...] += up
     prod_ref[...] = nn(weighted_ref[...], second_ref[...])
     for pair in range(2):
@@ -244,7 +254,7 @@
         + [small] * 4
         + [jax.ShapeDtypeStruct((64, 128), F32)],
         scratch_shapes=[pltpu.VMEM((8192, 128), F32), pltpu.VMEM((256, 1024), F32)],
-        compiler_params=params(60),
+        compiler_params=params(44),
         cost_estimate=cost(25),
         name="middle",
     )(moved, second, gate_out, cotangent, *grads, wu)
@@ -280,7 +290,7 @@
         out_specs=[vmem, vmem],
         out_shape=HALF,
         scratch_shapes=[pltpu.VMEM((1024, 1024), F32)],
-        compiler_params=params(60),
+        compiler_params=params(28),
         cost_estimate=cost(7),
         name="second_part",
     )(table, weighted, left)
@@ -305,32 +315,32 @@
         out_specs=[vmem, vmem, vmem],
         out_shape=HALF + [jax.ShapeDtypeStruct((1024, 1024), BF16)],
         scratch_shapes=[pltpu.VMEM((1024, 1024), F32)],
-        compiler_params=params(60),
+        compiler_params=params(28),
         cost_estimate=cost(7),
         name="first_part",
     )(table, back, rows, tw, *after)
 
 
-def join_kernel(keep_ref, got_ref, second_ref, after_ref, out_ref):
+def join_kernel(keep_ref, got_ref, second_keep_ref, second_got_ref, out_ref):
     for m in range(16):
         out_ref[m, 0] = (keep_ref[m] + got_ref[m].astype(F32)).astype(BF16)
-        out_ref[m, 1] = second_ref[m]
-
-
-def join(keep, got, second, after):
+        out_ref[m, 1] = (second_keep_ref[m] + second_got_ref[m].astype(F32)).astype(BF16)
+
+
+def join(keep, got, second_keep, second_got):
     vmem = pl.BlockSpec(memory_space=pltpu.VMEM)
     return pl.pallas_call(
         join_kernel,
-        in_specs=[vmem] * 3 + [pl.BlockSpec(memory_space=pl.ANY)],
+        in_specs=[vmem] * 4,
         out_specs=vmem,
         out_shape=jax.ShapeDtypeStruct((16, 2, 8, 8, 512), BF16),
-        compiler_params=params(60),
+        compiler_params=params(20),
         cost_estimate=cost(3),
         name="join",
-    )(keep, got, second, after)
-
-
-def plane_sum_kernel(parts_ref, small_ref, after_ref, out_ref):
+    )(keep, got, second_keep, second_got)
+
+
+def plane_sum_kernel(parts_ref, small_ref, out_ref):
     small = small_ref[...].astype(BF16)
     for z in range(8):
         for grad in range(2):
@@ -342,38 +352,63 @@
             out_ref[z, 2 + i] = small[i * 8 : (i + 1) * 8]
 
 
-def plane_sum(parts, small, after):
+def plane_sum(parts, small):
     vmem = pl.BlockSpec(memory_space=pltpu.VMEM)
     return pl.pallas_call(
         plane_sum_kernel,
-        in_specs=[vmem, vmem, pl.BlockSpec(memory_space=pl.ANY)],
+        in_specs=[vmem, vmem],
         out_specs=vmem,
         out_shape=jax.ShapeDtypeStruct((8, 6, 8, 512), BF16),
-        compiler_params=params(60),
+        compiler_params=params(12),
         cost_estimate=cost(2),
         name="plane_sum",
-    )(parts, small, after)
-
-
-def input_kernel(shifted_ref, first_ref, gate_ref, out_ref):
+    )(parts, small)
+
+
+def z_sum_kernel(parts_ref, after_ref, out_ref):
+    total = parts_ref[0].astype(F32)
+    for z in range(1, 8):
+        total += parts_ref[z].astype(F32)
+    out_ref[...] = total
+
+
+def z_sum(parts, after):
+    vmem = pl.BlockSpec(memory_space=pltpu.VMEM)
+    return pl.pallas_call(
+        z_sum_kernel,
+        in_specs=[vmem, pl.BlockSpec(memory_space=pl.ANY)],
+        out_specs=vmem,
+        out_shape=jax.ShapeDtypeStruct(parts.shape[1:], F32),
+        compiler_params=params(10),
+        cost_estimate=cost(1),
+        name="z_sum",
+    )(parts, after)
+
+
+def input_kernel(shifted_ref, first_ref, gate_ref, after_ref, out_ref):
     spread = tn(shifted_ref[...], first_ref[...])
     for q in range(4):
         at = slice(q * 1024, (q + 1) * 1024)
         out_ref[:, at] = (spread[q * 64 : (q + 1) * 64] * gate_ref[:, at].astype(F32)).astype(BF16)
 
 
-def input_part(shifted, first, gate_in):
+def input_part(shifted, first, gate_in, after):
     cols = pl.BlockSpec((64, 4096), lambda i: (0, i))
     return pl.pallas_call(
         input_kernel,
         grid=(4,),
-        in_specs=[pl.BlockSpec((1024, 256), lambda i: (0, i)), full((1024, 1024)), cols],
+        in_specs=[
+            pl.BlockSpec((1024, 256), lambda i: (0, i)),
+            full((1024, 1024)),
+            cols,
+            pl.BlockSpec(memory_space=pl.ANY),
+        ],
         out_specs=cols,
         out_shape=jax.ShapeDtypeStruct(gate_in.shape, BF16),
         compiler_params=params(60),
         cost_estimate=cost(7),
         name="input_part",
-    )(shifted, first, gate_in)
+    )(shifted, first, gate_in, after)
 
 
 def output_kernel(mixer_ref, p0, p1, p2, p3, cot_ref, wd_ref, out_ref, down_ref):
@@ -420,7 +455,7 @@
         jnp.concatenate([mine, theirs], axis=1),
         jnp.concatenate([theirs, mine], axis=1),
     )
-    column = lax.all_to_all(fan(rows, 8, after), "z", 0, 0, tiled=True)
+    column = lax.all_to_all(fan(fan_kernel, rows, (8,) + rows.shape, after), "z", 0, 0, tiled=True)
     return column
 
 
@@ -437,32 +472,34 @@
     column = start_gather(first_factor, second_turned, core, [grads[0]])
     rows = gated_part(tokens, gate_in)
     grads = chan_swap(grads)
-    plane = lax.all_to_all(fan(column, 16, [grads[1], grads[2], rows]), PLANE, 0, 0, tiled=True)
-    first_half, second_half = plane[:, :, 0], plane[:, :, 1]
-    first = assemble(first_half, swap(first_half, "core", 1), table)
+    plane = lax.all_to_all(
+        fan(fan_plane_kernel, column, (16, 2, 8, 8, 512), [grads[1], grads[2], rows]), PLANE, 0, 0, tiled=True
+    )
+    first = assemble(plane, swap(plane[:, 0], "core", 1), table, 0)
     seg = segment(first, rows, twiddle)
     moved = lax.all_to_all(seg.reshape(64, 16, 1024), SEQ, 0, 0, tiled=True).reshape(1024, 1024)
-    second = assemble(second_half, swap(second_half, "core", 1), table)
+    second = assemble(plane, swap(plane[:, 1], "core", 1), table, 1)
     back, left, weighted, mixer, *rest = middle(moved, second, gate_out, cotangent, grads, wu)
     acts, up = rest[:4], rest[4]
     returned = lax.all_to_all(back.reshape(64, 16, 1024), SEQ, 0, 0, tiled=True).reshape(1024, 1024)
     acts = chan_swap(acts)
     second_send, second_keep = second_part(table, weighted, left)
-    second_total = (second_keep + swap(second_send, "core", 1).astype(F32)).astype(BF16)
+    second_got = swap(second_send, "core", 1)
     mixed_out, down = output_part(mixer, acts, cotangent, wd)
     up = up.reshape(64, 4, 32)[:, order].reshape(64, 128)
     down = down.reshape(4, 32, 64)[order].reshape(128, 64)
     small = jnp.concatenate([up.reshape(16, 512), down.reshape(16, 512)], axis=0)
     first_send, first_keep, shifted = first_part(
-        table, returned, rows, twiddle, [mixed_out, second_total]
+        table, returned, rows, twiddle, [mixed_out, second_got]
     )
     small = (small + swap(small, "x", 1)) + (swap(small, "x", 2) + swap(small, "x", 3))
-    joined = join(first_keep, swap(first_send, "core", 1), second_total, small)
+    joined = join(first_keep, swap(first_send, "core", 1), second_keep, second_got)
     parts = lax.all_to_all(joined, PLANE, 0, 0, tiled=True)
-    input_grad = input_part(shifted, first, gate_in)
     small = small + swap(small, "yh", 1)
-    both = lax.all_to_all(plane_sum(parts, small, input_grad), "z", 0, 0, tiled=True)
-    both = jnp.sum(both.astype(F32), axis=0)
+    both = plane_sum(parts, small)
+    input_grad = input_part(shifted, first, gate_in, both)
+    both = lax.all_to_all(both, "z", 0, 0, tiled=True)
+    both = z_sum(both, input_grad)
     small = both[2:].reshape(32, 512)
     both = both[:2].reshape(2, 2, 4, 512)
     mine = lax.dynamic_index_in_dim(both, core, 1, keepdims=False)

time: 361 us -> 334 us (0.925)
  Pallas kernels: 88.9 us -> 60.7 us
  blocking collectives: 51.9 us -> 31.7 us
  local copies, waits for them, and re-layouts: 17.4 us -> 30.8 us
  waiting for transfers between devices: 140 us -> 148 us
  starting transfers between devices: 52.9 us -> 60.3 us
  other arithmetic: 5.52 us -> 0.15 us
    all_to_all x2 -> x1, blocking collectives: 51.9 us -> 31.7 us  [local(): lax.all_to_all(fan(fan_plane_kernel, column, (16, 2, 8, 8, 512), [grads[1...]
    unnamed x39 -> x57, local copies, waits for them, and re-layouts: 8.73 us -> 23.4 us
    pallas_call x6 -> x7, Pallas kernels: 16.3 us -> 4.32 us  [the longest x2 2.06 us: assemble(): pl.pallas_call(functools.partial(assemble_kernel, factor), in_specs=[pl.B...]
    ppermute x16, waiting for transfers between devices: 127 us -> 137 us  [swap(): return lax.ppermute(values, axis, [(i, i ^ bit) for i in range(size)])]
    pallas_call x1, Pallas kernels: 30.3 us -> 22.4 us  [middle(): pl.pallas_call(middle_kernel, grid=(4,), in_specs=[square, square, cols,...]
    all_to_all x1, waiting for transfers between devices: 7.62 us -> 0.01 us  [local(): parts = lax.all_to_all(joined, PLANE, 0, 0, tiled=True)]
    all_to_all x1 -> x2, starting transfers between devices: 7.12 us -> 13.4 us  [the longest x1 7.12 us: start_gather(): lax.all_to_all(fan(fan_kernel, rows, (8,) + rows.shape, after), 'z', 0, 0...]
    all_to_all x1 -> x2, waiting for transfers between devices: 3.62 us -> 8.56 us  [the longest x1 4.94 us: local(): both = lax.all_to_all(both, 'z', 0, 0, tiled=True)]
  transfers between devices with their start and end apart: 20 -> 21, of which waited for: 14 -> 14; matrix products, arithmetic and copies ran while one was open for 3% -> 1% of each run, Pallas kernels for 8% -> 7%
where the time goes in v3:
time: 334 us; the launch traced here: 333 us
  waiting for transfers between devices  148 us (44%)
  Pallas kernels  60.7 us (18%)
  starting transfers between devices  60.3 us (18%)
  blocking collectives  31.7 us (9%)
  local copies, waits for them, and re-layouts  30.8 us (9%)
    ppermute x16, waiting for transfers between devices, swap(): return lax.ppermute(values, axis, [(i, i ^ bit) for i in range(size)])  137 us
    all_to_all x1, blocking collectives, local(): lax.all_to_all(fan(fan_plane_kernel, column, (16, 2, 8, 8, 512), [grads[1...  31.7 us
    unnamed x57, local copies, waits for them, and re-layouts  23.4 us
    pallas_call x1, Pallas kernels, middle(): pl.pallas_call(middle_kernel, grid=(4,), in_specs=[square, square, cols,...  22.4 us
    ppermute x16, starting transfers between devices, swap(): return lax.ppermute(values, axis, [(i, i ^ bit) for i in range(size)])  20.3 us
    all_to_all x1, starting transfers between devices, local(): lax.all_to_all(seg.reshape(64, 16, 1024), SEQ, 0, 0, tiled=True)  11.1 us
    all_to_all x1, starting transfers between devices, local(): lax.all_to_all(back.reshape(64, 16, 1024), SEQ, 0, 0, tiled=True)  10.1 us
    all_to_all x1, starting transfers between devices, start_gather(): lax.all_to_all(fan(fan_kernel, rows, (8,) + rows.shape, after), 'z', 0, 0...  7.12 us
  transfers between devices with their start and end apart: 21, of which 14 were waited for; matrix products, arithmetic and copies ran while one was open for 1% of the time, Pallas kernels for 7%

profile of v3, /device:TPU:1, one launch (start us, length us, event | category | flops | bytes accessed | tf_op | source)
XLA Modules:
  0.0 332.8 jit_solution(15199894271748117524)
XLA Ops:
  0.7 0.8 copy.44
  1.5 1.2 gather_fusion
  2.7 4.8 %grads_part.1 = (bf16[32,16384]{1,0:T(8,128)(2,1)}, bf16[32,16384]{1,0:T(8,128)(2,1)}, bf16[32,16384]{1,0:T(8,128)(2,1)}, bf16[32,16384]{1,0:T(8,128)(2,1)}) custom-call(bf16[64,16384]{1,0:T(8,128)(2,1)} %cot_ref.5, bf16[128,64]{1,0:T(8,128)(2,1)} %bitcast.48), custom_call_target="tpu_custom_call" | custom-call | bytes 12000 | tf_op jit(solution)/shard_map/grads_part/pallas_call | solution.py:55
  7.5 3.2 collective-permute-start.1
  11.4 1.7 collective-permute-done
  13.1 1.2 copy-done.11
  14.3 0.7 fan.2
  15.0 7.1 %all-to-all-start = ((bf16[8,2,8,512]{3,2,1,0:T(8,128)(2,1)}), bf16[8,2,8,512]{3,2,1,0:T(8,128)(2,1)S(1)}, u32[]{:S(2)}, u32[]{:S(2)}) async-start(bf16[8,2,8,512]{3,2,1,0:T(8,128)(2,1)} %fan.2), calls=%async_computation | async-start | bytes 262144 | tf_op jit(solution)/shard_map/all_to_all | solution.py:458
  22.1 4.3 %gated_part.1.refs_2_.rows_ref = bf16[1024,1024]{1,0:T(8,128)(2,1)} custom-call(bf16[64,16384]{1,0:T(8,128)(2,1)} %tok_ref.1, bf16[64,16384]{1,0:T(8,128)(2,1)} %gate_ref.5), custom_call_target="tpu_custom_call" | custom-call | bytes 12000 | tf_op jit(solution)/shard_map/gated_part/pallas_call | solution.py:77
  26.4 3.6 %all-to-all-done.column_ref = bf16[8,2,8,512]{3,2,1,0:T(8,128)(2,1)S(1)} async-done(((bf16[8,2,8,512]{3,2,1,0:T(8,128)(2,1)}), bf16[8,2,8,512]{3,2,1,0:T(8,128)(2,1)S(1)}, u32[]{:S(2)}, u32[]{:S(2)}) %all-to-all-start) | async-done | bytes 131104 | tf_op jit(solution)/shard_map/all_to_all | solution.py:458
  30.0 5.7 %collective-permute-done.2.refs_1_.g2 = bf16[32,16384]{1,0:T(8,128)(2,1)S(1)} collective-permute-done((bf16[32,16384]{1,0:T(8,128)(2,1)}, bf16[32,16384]{1,0:T(8,128)(2,1)S(1)}, u32[]{:S(2)}, u32[]{:S(2)}) %collective-permute-start.2) | collective-permute-done | bytes 1048608 | tf_op jit(solution)/shard_map/ppermute | solution.py:441
  35.7 1.6 copy-done
  37.4 0.8 copy-done.9
  38.3 31.7 %all_to_all.30.own_ref = bf16[16,2,8,8,512]{4,3,2,1,0:T(8,128)(2,1)S(1)} all-to-all(bf16[16,2,8,8,512]{4,3,2,1,0:T(8,128)(2,1)S(1)} %fan.3), channel_id=1, replica_groups=mesh['z'=8,'yh'=2,'x'=4,'yl'=2,'core'=2] {'yh','x','yl'}, dimensions={0} | all-to-all | bytes 4194304 | tf_op jit(solution)/shard_map/all_to_all | solution.py:475
  69.9 1.5 slice_bitcast_fusion
  71.4 2.4 collective-permute-start.3
  73.9 2.2 collective-permute-done.3.other_ref
  76.1 0.7 assemble.2
  76.9 3.6 %segment.1 = bf16[1024,1024]{1,0:T(8,128)(2,1)S(1)} custom-call(bf16[1024,1024]{1,0:T(8,128)(2,1)S(1)} %bitcast.40, bf16[1024,1024]{1,0:T(8,128)(2,1)S(1)} %copy-done.1, f32[16,1024]{1,0:T(8,128)S(1)} %copy-done.20), custom_call_target="tpu_custom_call" | custom-call | bytes 18000 | tf_op jit(solution)/shard_map/segment/pallas_call | solution.py:154
  80.5 1.3 copy-done.5
  81.8 11.1 %all-to-all-start.2 = ((bf16[64,16,1024]{2,1,0:T(8,128)(2,1)}), bf16[64,16,1024]{2,1,0:T(8,128)(2,1)}, u32[]{:S(2)}, u32[]{:S(2)}) async-start(bf16[64,16,1024]{2,1,0:T(8,128)(2,1)} %bitcast.42), calls=%async_computation.2 | async-start | bytes 4194304 | tf_op jit(solution)/shard_map/all_to_all | solution.py:480
  92.9 0.7 collective-permute-start.4
  93.7 0.6 gather_fusion.1
  94.4 1.8 collective-permute-done.4.other_ref
  96.3 1.6 copy-done.3
  97.8 1.4 assemble.3
  99.2 1.3 copy-done.8
  100.6 38.7 %collective-permute-done.5.g3 = bf16[32,16384]{1,0:T(8,128)(2,1)} collective-permute-done((bf16[32,16384]{1,0:T(8,128)(2,1)}, bf16[32,16384]{1,0:T(8,128)(2,1)}, u32[]{:S(2)}, u32[]{:S(2)}) %collective-permute-start.5) | collective-permute-done | bytes 1048608 | tf_op jit(solution)/shard_map/ppermute | solution.py:441
  139.3 2.2 all-to-all-done.2
  141.4 1.2 copy-done.10
  142.7 1.2 copy-done.12
  143.9 22.4 %middle.1 = (bf16[1024,1024]{1,0:T(8,128)(2,1)}, bf16[1024,1024]{1,0:T(8,128)(2,1)}, bf16[1024,1024]{1,0:T(8,128)(2,1)}, bf16[64,16384]{1,0:T(8,128)(2,1)}, bf16...) custom-call(bf16[1024,1024]{1,0:T(8,128)(2,1)} %bitcast.8.moved_ref,, ...), custom_call_target="tpu_custom_call" | custom-call | bytes 75000 | tf_op jit(solution)/shard_map/middle/pallas_call | solution.py:248
  166.3 1.0 copy-done.19
  167.3 10.1 %all-to-all-start.3 = ((bf16[64,16,1024]{2,1,0:T(8,128)(2,1)}), bf16[64,16,1024]{2,1,0:T(8,128)(2,1)}, u32[]{:S(2)}, u32[]{:S(2)}) async-start(bf16[64,16,1024]{2,1,0:T(8,128)(2,1)} %bitcast.44), calls=%async_computation.3 | async-start | bytes 4194304 | tf_op jit(solution)/shard_map/all_to_all | solution.py:484
  177.4 1.2 collective-permute-start.6
  178.6 1.7 collective-permute-start.8
  180.3 1.6 copy-done.13
  181.9 1.6 copy-done.14
  183.5 4.1 %second_part.1 = (bf16[16,8,8,512]{3,2,1,0:T(8,128)(2,1)}, f32[16,8,8,512]{3,2,1,0:T(8,128)S(1)}) custom-call(s32[17]{0:T(128)S(1)} %pad_add_fusion.table_ref, bf16[1024,1024]{1,0:T(8,128)(2,1)S(1)} %copy-done.14, bf16[1024,1024]{1,0:T(8,128)(2,1)S(1)} %copy-done.13), custom_call_target="tpu_custom_call" | custom-call | bytes 21000 | tf_op jit(solution)/shard_map/second_part/pallas_call | solution.py:287
  187.6 1.4 copy-done.17
  189.1 34.9 %collective-permute-done.7.p2 = bf16[32,16384]{1,0:T(8,128)(2,1)} collective-permute-done((bf16[32,16384]{1,0:T(8,128)(2,1)}, bf16[32,16384]{1,0:T(8,128)(2,1)}, u32[]{:S(2)}, u32[]{:S(2)}) %collective-permute-start.7) | collective-permute-done | bytes 1048608 | tf_op jit(solution)/shard_map/ppermute | solution.py:441
  224.0 23.5 %collective-permute-done.8.p3 = bf16[32,16384]{1,0:T(8,128)(2,1)} collective-permute-done((bf16[32,16384]{1,0:T(8,128)(2,1)}, bf16[32,16384]{1,0:T(8,128)(2,1)}, u32[]{:S(2)}, u32[]{:S(2)}) %collective-permute-start.8) | collective-permute-done | bytes 1048608 | tf_op jit(solution)/shard_map/ppermute | solution.py:441
  247.5 5.9 %output_part.1 = (bf16[64,16384]{1,0:T(8,128)(2,1)}, f32[128,64]{1,0:T(8,128)}) custom-call(bf16[64,16384]{1,0:T(8,128)(2,1)} %get-tuple-element.30.mixer_ref, bf16[32,16384]{1,0:T(8,128)(2,1)} %copy-done.19, bf16[32,16384]{1,0:T(8,128)(2,1)} %collective-permute-done.6.p1, bf16[32,16384]{1,0:T(8,128)(2,1)} %collective-permute-done.7.p2, ...), custom_call_target="tpu_custom_call" | custom-call | bytes 24000 | tf_op jit(solution)/shard_map/output_part/pallas_call | solution.py:427
  253.4 1.6 copy-done.15
  255.0 4.9 %first_part.1 = (bf16[16,8,8,512]{3,2,1,0:T(8,128)(2,1)S(1)}, f32[16,8,8,512]{3,2,1,0:T(8,128)S(1)}, bf16[1024,1024]{1,0:T(8,128)(2,1)S(1)}) custom-call(s32[17]{0:T(128)S(1)} %pad_add_fusion.table_ref, bf16[1024,1024]{1,0:T(8,128)(2,1)} %bitcast.15.back_ref, bf16[1024,1024]{1,0:T(8,128)(2,1)S(1)} %copy-done.1, f32[16,1024]{1,0:T(8,128)S(1)} %copy-done.20, ...), custom_call_target="tpu_custom_call" | custom-call | bytes 21000 | tf_op jit(solution)/shard_map/first_part/pallas_call | solution.py:311
  259.9 1.4 copy-done.16
  261.7 2.3 collective-permute-done.10.got_ref
  264.3 1.3 copy-done.7
  265.6 5.5 %all-to-all-start.4 = ((bf16[16,2,8,8,512]{4,3,2,1,0:T(8,128)(2,1)}), bf16[16,2,8,8,512]{4,3,2,1,0:T(8,128)(2,1)S(1)}, u32[]{:S(2)}, u32[]{:S(2)}) async-start(bf16[16,2,8,8,512]{4,3,2,1,0:T(8,128)(2,1)} %copy-done.7), calls=%async_computation.4 | async-start | bytes 4194304 | tf_op jit(solution)/shard_map/all_to_all | solution.py:497
  272.7 2.6 collective-permute-start.13
  275.3 0.6 collective-permute-start.12
  276.0 24.3 %collective-permute-done.13 = f32[32,512]{1,0:T(8,128)S(1)} collective-permute-done((f32[32,512]{1,0:T(8,128)S(1)}, f32[32,512]{1,0:T(8,128)S(1)}, u32[]{:S(2)}, u32[]{:S(2)}) %collective-permute-start.13) | collective-permute-done | bytes 65568 | tf_op jit(solution)/shard_map/ppermute | solution.py:441
  300.4 2.6 collective-permute-start.14
  303.0 2.1 collective-permute-done.14
  305.2 1.0 plane_sum.1.after_ref
  306.2 6.2 %all-to-all-start.5 = ((bf16[8,6,8,512]{3,2,1,0:T(8,128)(2,1)}), bf16[8,6,8,512]{3,2,1,0:T(8,128)(2,1)S(1)}, u32[]{:S(2)}, u32[]{:S(2)}) async-start(bf16[8,6,8,512]{3,2,1,0:T(8,128)(2,1)} %plane_sum.1.after_ref), calls=%async_computation.5 | async-start | bytes 786432 | tf_op jit(solution)/shard_map/all_to_all | solution.py:501
  312.5 6.5 %input_part.1.after_ref = bf16[64,16384]{1,0:T(8,128)(2,1)} custom-call(bf16[1024,1024]{1,0:T(8,128)(2,1)} %copy-done.16, bf16[1024,1024]{1,0:T(8,128)(2,1)} %bitcast.41, bf16[64,16384]{1,0:T(8,128)(2,1)} %gate_ref.5, bf16[8,6,8,512]{3,2,1,0:T(8,128)(2,1)} %plane_sum.1.after_ref), custom_call_target="tpu_custom_call" | custom-call | bytes 21000 | tf_op jit(solution)/shard_map/input_part/pallas_call | solution.py:397
  319.0 4.9 %all-to-all-done.5.parts_ref = bf16[8,6,8,512]{3,2,1,0:T(8,128)(2,1)S(1)} async-done(((bf16[8,6,8,512]{3,2,1,0:T(8,128)(2,1)}), bf16[8,6,8,512]{3,2,1,0:T(8,128)(2,1)S(1)}, u32[]{:S(2)}, u32[]{:S(2)}) %all-to-all-start.5) | async-done | bytes 393248 | tf_op jit(solution)/shard_map/all_to_all | solution.py:501
  323.9 1.6 copy-done.6
  325.6 4.3 %collective-permute-start.15 = (f32[2,4,512]{2,1,0:T(4,128)S(1)}, f32[2,4,512]{2,1,0:T(4,128)S(1)}, u32[]{:S(2)}, u32[]{:S(2)}) collective-permute-start(f32[2,4,512]{2,1,0:T(4,128)S(1)} %get-tuple-element.78), channel_id=1, source_target_pairs={{0,1},{1,0},{2,3},{3,2},{4,5},{5,4},{6,7},{7,6},{8,9},{9,8},{10,11... | collective-permute-start | bytes 49160 | tf_op jit(solution)/shard_map/ppermute | solution.py:441
  330.0 0.7 copy.52
  330.7 0.6 reshape.100
  331.3 0.6 fusion.2
  332.1 0.7 reshape.99
  (85 shorter events, 4.2 us)
Async XLA Ops:
  0.6 10.1 %copy-start.24 = (bf16[4,1024]{1,0:T(4,128)(2,1)S(1)}, bf16[4,1024]{1,0:T(4,128)(2,1)}, u32[]{:S(2)}) copy-start(bf16[4,1024]{1,0:T(4,128)(2,1)} %param.13) | copy-start | bytes 24580
  0.6 10.1 %copy-start.23 = (bf16[4,1024]{1,0:T(4,128)(2,1)S(1)}, bf16[4,1024]{1,0:T(4,128)(2,1)}, u32[]{:S(2)}) copy-start(bf16[4,1024]{1,0:T(4,128)(2,1)} %param.14) | copy-start | bytes 24580
  7.5 22.5 %collective-permute-start.1 = (bf16[32,16384]{1,0:T(8,128)(2,1)}, bf16[32,16384]{1,0:T(8,128)(2,1)S(1)}, u32[]{:S(2)}, u32[]{:S(2)}) collective-permute-start(bf16[32,16384]{1,0:T(8,128)(2,1)} %get-tuple-element.27), channel_id=1, source_target_pairs={{0,1},{1,0},{2,3},{3,2},{4,5},{5,4},{6,7},{7,6},{8,9},{9,8},{10,11... | collective-permute-start | bytes 3145736 | tf_op jit(solution)/shard_map/ppermute | solution.py:441
  10.8 24.9 %collective-permute-start.2 = (bf16[32,16384]{1,0:T(8,128)(2,1)}, bf16[32,16384]{1,0:T(8,128)(2,1)S(1)}, u32[]{:S(2)}, u32[]{:S(2)}) collective-permute-start(bf16[32,16384]{1,0:T(8,128)(2,1)} %get-tuple-element.28), channel_id=1, source_target_pairs={{0,2},{1,3},{2,0},{3,1},{4,6},{5,7},{6,4},{7,5},{8,10},{9,11},{10,... | collective-permute-start | bytes 3145736 | tf_op jit(solution)/shard_map/ppermute | solution.py:441
  11.2 1.9 collective-permute-start
  13.1 1.2 copy-start.11
  15.0 15.0 %all-to-all-start = ((bf16[8,2,8,512]{3,2,1,0:T(8,128)(2,1)}), bf16[8,2,8,512]{3,2,1,0:T(8,128)(2,1)S(1)}, u32[]{:S(2)}, u32[]{:S(2)}) async-start(bf16[8,2,8,512]{3,2,1,0:T(8,128)(2,1)} %fan.2), calls=%async_computation | async-start | bytes 262144 | tf_op jit(solution)/shard_map/all_to_all | solution.py:458
  35.7 1.6 copy-start
  37.3 1.0 copy-start.9
  69.9 6.2 %copy-start.2 = (bf16[16,2,8,8,512]{4,3,2,1,0:T(8,128)(2,1)}, bf16[16,2,8,8,512]{4,3,2,1,0:T(8,128)(2,1)S(1)}, u32[]{:S(2)}) copy-start(bf16[16,2,8,8,512]{4,3,2,1,0:T(8,128)(2,1)S(1)} %all_to_all.30.own_ref) | copy-start | bytes 6291460
  71.4 4.7 %collective-permute-start.3 = (bf16[16,8,8,512]{3,2,1,0:T(8,128)(2,1)S(1)}, bf16[16,8,8,512]{3,2,1,0:T(8,128)(2,1)S(1)}, u32[]{:S(2)}, u32[]{:S(2)}) collective-permute-start(bf16[16,8,8,512]{3,2,1,0:T(8,128)(2,1)S(1)} %get-tuple-element.71), channel_id=1, source_target_pairs={{0,1},{1,0},{2,3},{3,2},{4,5},{5,4},{6,7},{7,6},{8,9},{9,8},{10,11... | collective-permute-start | bytes 3145736 | tf_op jit(solution)/shard_map/ppermute | solution.py:441
  73.9 2.9 copy-start.1
  73.9 2.9 copy-start.20
  76.8 3.6 %copy-start.4 = (bf16[8,16,8,1024]{3,2,1,0:T(8,128)(2,1)}, bf16[8,16,8,1024]{3,2,1,0:T(8,128)(2,1)S(1)}, u32[]{:S(2)}) copy-start(bf16[8,16,8,1024]{3,2,1,0:T(8,128)(2,1)S(1)} %assemble.2) | copy-start | bytes 6291460
  80.4 1.3 copy-start.5
  81.8 11.9 %copy-start.22 = (bf16[1,64,128]{2,1,0:T(8,128)(2,1)S(1)}, bf16[1,64,128]{2,1,0:T(8,128)(2,1)}, u32[]{:S(2)}) copy-start(bf16[1,64,128]{2,1,0:T(8,128)(2,1)} %param.15) | copy-start | bytes 49156
  81.8 59.7 %all-to-all-start.2 = ((bf16[64,16,1024]{2,1,0:T(8,128)(2,1)}), bf16[64,16,1024]{2,1,0:T(8,128)(2,1)}, u32[]{:S(2)}, u32[]{:S(2)}) async-start(bf16[64,16,1024]{2,1,0:T(8,128)(2,1)} %bitcast.42), calls=%async_computation.2 | async-start | bytes 4194304 | tf_op jit(solution)/shard_map/all_to_all | solution.py:480
  92.9 3.4 %collective-permute-start.4 = (bf16[16,8,8,512]{3,2,1,0:T(8,128)(2,1)}, bf16[16,8,8,512]{3,2,1,0:T(8,128)(2,1)}, u32[]{:S(2)}, u32[]{:S(2)}) collective-permute-start(bf16[16,8,8,512]{3,2,1,0:T(8,128)(2,1)} %get-tuple-element.70), channel_id=1, source_target_pairs={{0,1},{1,0},{2,3},{3,2},{4,5},{5,4},{6,7},{7,6},{8,9},{9,8},{10,11... | collective-permute-start | bytes 3145736 | tf_op jit(solution)/shard_map/ppermute | solution.py:441
  93.6 45.6 %collective-permute-start.5 = (bf16[32,16384]{1,0:T(8,128)(2,1)}, bf16[32,16384]{1,0:T(8,128)(2,1)}, u32[]{:S(2)}, u32[]{:S(2)}) collective-permute-start(bf16[32,16384]{1,0:T(8,128)(2,1)} %get-tuple-element.29), channel_id=1, source_target_pairs={{0,3},{1,2},{2,1},{3,0},{4,7},{5,6},{6,5},{7,4},{8,11},{9,10},{10,... | collective-permute-start | bytes 3145736 | tf_op jit(solution)/shard_map/ppermute | solution.py:441
  96.3 1.6 copy-start.3
  99.2 1.3 copy-start.8
  141.4 1.2 copy-start.10
  142.7 1.2 copy-start.12
  166.3 1.0 copy-start.19
  167.3 86.1 %all-to-all-start.3 = ((bf16[64,16,1024]{2,1,0:T(8,128)(2,1)}), bf16[64,16,1024]{2,1,0:T(8,128)(2,1)}, u32[]{:S(2)}, u32[]{:S(2)}) async-start(bf16[64,16,1024]{2,1,0:T(8,128)(2,1)} %bitcast.44), calls=%async_computation.3 | async-start | bytes 4194304 | tf_op jit(solution)/shard_map/all_to_all | solution.py:484
  177.4 11.7 %collective-permute-start.6 = (bf16[32,16384]{1,0:T(8,128)(2,1)}, bf16[32,16384]{1,0:T(8,128)(2,1)}, u32[]{:S(2)}, u32[]{:S(2)}) collective-permute-start(bf16[32,16384]{1,0:T(8,128)(2,1)} %get-tuple-element.32), channel_id=1, source_target_pairs={{0,1},{1,0},{2,3},{3,2},{4,5},{5,4},{6,7},{7,6},{8,9},{9,8},{10,11... | collective-permute-start | bytes 3145736 | tf_op jit(solution)/shard_map/ppermute | solution.py:441
  178.6 45.4 %collective-permute-start.7 = (bf16[32,16384]{1,0:T(8,128)(2,1)}, bf16[32,16384]{1,0:T(8,128)(2,1)}, u32[]{:S(2)}, u32[]{:S(2)}) collective-permute-start(bf16[32,16384]{1,0:T(8,128)(2,1)} %get-tuple-element.33), channel_id=1, source_target_pairs={{0,2},{1,3},{2,0},{3,1},{4,6},{5,7},{6,4},{7,5},{8,10},{9,11},{10,... | collective-permute-start | bytes 3145736 | tf_op jit(solution)/shard_map/ppermute | solution.py:441
  178.6 68.9 %collective-permute-start.8 = (bf16[32,16384]{1,0:T(8,128)(2,1)}, bf16[32,16384]{1,0:T(8,128)(2,1)}, u32[]{:S(2)}, u32[]{:S(2)}) collective-permute-start(bf16[32,16384]{1,0:T(8,128)(2,1)} %get-tuple-element.34), channel_id=1, source_target_pairs={{0,3},{1,2},{2,1},{3,0},{4,7},{5,6},{6,5},{7,4},{8,11},{9,10},{10,... | collective-permute-start | bytes 3145736 | tf_op jit(solution)/shard_map/ppermute | solution.py:441
  180.3 1.6 copy-start.13
  181.9 1.6 copy-start.14
  187.6 1.4 copy-start.17
  189.0 64.5 %collective-permute-start.9 = (bf16[16,8,8,512]{3,2,1,0:T(8,128)(2,1)}, bf16[16,8,8,512]{3,2,1,0:T(8,128)(2,1)S(1)}, u32[]{:S(2)}, u32[]{:S(2)}) collective-permute-start(bf16[16,8,8,512]{3,2,1,0:T(8,128)(2,1)} %get-tuple-element.39), channel_id=1, source_target_pairs={{0,1},{1,0},{2,3},{3,2},{4,5},{5,4},{6,7},{7,6},{8,9},{9,8},{10,11... | collective-permute-start | bytes 3145736 | tf_op jit(solution)/shard_map/ppermute | solution.py:441
  253.4 1.6 copy-start.15
  255.0 8.9 %copy-start.18 = (f32[16,8,8,512]{3,2,1,0:T(8,128)S(1)}, f32[16,8,8,512]{3,2,1,0:T(8,128)}, u32[]{:S(2)}) copy-start(f32[16,8,8,512]{3,2,1,0:T(8,128)} %copy-done.17) | copy-start | bytes 6291460
  259.9 1.4 copy-start.16
  261.3 2.7 collective-permute-start.10
  264.3 1.3 copy-start.7
  265.6 6.4 %copy-start.21 = (f32[128,64]{1,0:T(8,128)S(1)}, f32[128,64]{1,0:T(8,128)}, u32[]{:S(2)}) copy-start(f32[128,64]{1,0:T(8,128)} %get-tuple-element.45) | copy-start | bytes 98308
  265.6 39.5 %all-to-all-start.4 = ((bf16[16,2,8,8,512]{4,3,2,1,0:T(8,128)(2,1)}), bf16[16,2,8,8,512]{4,3,2,1,0:T(8,128)(2,1)S(1)}, u32[]{:S(2)}, u32[]{:S(2)}) async-start(bf16[16,2,8,8,512]{4,3,2,1,0:T(8,128)(2,1)} %copy-done.7), calls=%async_computation.4 | async-start | bytes 4194304 | tf_op jit(solution)/shard_map/all_to_all | solution.py:497
  272.7 27.6 %collective-permute-start.13 = (f32[32,512]{1,0:T(8,128)S(1)}, f32[32,512]{1,0:T(8,128)S(1)}, u32[]{:S(2)}, u32[]{:S(2)}) collective-permute-start(f32[32,512]{1,0:T(8,128)S(1)} %constant_dynamic-update-slice_fusion.2), channel_id=1, source_target_pairs={{0,12},{4,8},{8,4},{12,0},{1,13},{5,9},{9,5},{13,1},{2,14},{6,10},... | collective-permute-start | bytes 196616 | tf_op jit(solution)/shard_map/ppermute | solution.py:441
  275.3 24.9 %collective-permute-start.12 = (f32[32,512]{1,0:T(8,128)S(1)}, f32[32,512]{1,0:T(8,128)S(1)}, u32[]{:S(2)}, u32[]{:S(2)}) collective-permute-start(f32[32,512]{1,0:T(8,128)S(1)} %constant_dynamic-update-slice_fusion.2), channel_id=1, source_target_pairs={{0,8},{4,12},{8,0},{12,4},{1,9},{5,13},{9,1},{13,5},{2,10},{6,14},... | collective-permute-start | bytes 196616 | tf_op jit(solution)/shard_map/ppermute | solution.py:441
  275.9 24.5 %collective-permute-start.11 = (f32[32,512]{1,0:T(8,128)S(1)}, f32[32,512]{1,0:T(8,128)S(1)}, u32[]{:S(2)}, u32[]{:S(2)}) collective-permute-start(f32[32,512]{1,0:T(8,128)S(1)} %constant_dynamic-update-slice_fusion.2), channel_id=1, source_target_pairs={{0,4},{4,0},{8,12},{12,8},{1,5},{5,1},{9,13},{13,9},{2,6},{6,2},{1... | collective-permute-start | bytes 196616 | tf_op jit(solution)/shard_map/ppermute | solution.py:441
  300.4 4.7 %collective-permute-start.14 = (f32[32,512]{1,0:T(8,128)S(1)}, f32[32,512]{1,0:T(8,128)S(1)}, u32[]{:S(2)}, u32[]{:S(2)}) collective-permute-start(f32[32,512]{1,0:T(8,128)S(1)} %add_add_fusion), channel_id=1, source_target_pairs={{0,16},{16,0},{1,17},{17,1},{2,18},{18,2},{3,19},{19,3},{4,20},{20... | collective-permute-start | bytes 196616 | tf_op jit(solution)/shard_map/ppermute | solution.py:441
  306.2 17.7 %all-to-all-start.5 = ((bf16[8,6,8,512]{3,2,1,0:T(8,128)(2,1)}), bf16[8,6,8,512]{3,2,1,0:T(8,128)(2,1)S(1)}, u32[]{:S(2)}, u32[]{:S(2)}) async-start(bf16[8,6,8,512]{3,2,1,0:T(8,128)(2,1)} %plane_sum.1.after_ref), calls=%async_computation.5 | async-start | bytes 786432 | tf_op jit(solution)/shard_map/all_to_all | solution.py:501
  323.9 1.6 copy-start.6
  325.6 5.7 %collective-permute-start.15 = (f32[2,4,512]{2,1,0:T(4,128)S(1)}, f32[2,4,512]{2,1,0:T(4,128)S(1)}, u32[]{:S(2)}, u32[]{:S(2)}) collective-permute-start(f32[2,4,512]{2,1,0:T(4,128)S(1)} %get-tuple-element.78), channel_id=1, source_target_pairs={{0,1},{1,0},{2,3},{3,2},{4,5},{5,4},{6,7},{7,6},{8,9},{9,8},{10,11... | collective-permute-start | bytes 49160 | tf_op jit(solution)/shard_map/ppermute | solution.py:441

commit v4 on v3

--- a/solution.py
+++ b/solution.py
@@ -79,7 +79,7 @@
         grid=(4,),
         in_specs=[cols, cols],
         out_specs=pl.BlockSpec((256, 1024), lambda i: (i, 0)),
-        out_shape=jax.ShapeDtypeStruct((1024, 1024), BF16),
+        out_shape=pltpu.HBM((1024, 1024), BF16),
         compiler_params=params(60),
         cost_estimate=cost(4),
         name="gated_part",
@@ -126,7 +126,7 @@
         kernel,
         in_specs=[vmem] + [pl.BlockSpec(memory_space=pl.ANY)] * len(after),
         out_specs=vmem,
-        out_shape=jax.ShapeDtypeStruct(shape, BF16),
+        out_shape=pltpu.HBM(shape, BF16),
         compiler_params=params(10),
         cost_estimate=cost(1),
         name="fan",
@@ -160,7 +160,7 @@
             pl.BlockSpec((16, 256), lambda i: (0, i)),
         ],
         out_specs=pl.BlockSpec((256, 1024), lambda i: (i, 0)),
-        out_shape=jax.ShapeDtypeStruct((1024, 1024), BF16),
+        out_shape=pltpu.HBM((1024, 1024), BF16),
         compiler_params=params(24),
         cost_estimate=cost(6),
         name="segment",
@@ -243,14 +243,14 @@
     part = pl.BlockSpec((32, 4096), lambda i: (0, i))
     square = full((1024, 1024))
     rows = pl.BlockSpec((256, 1024), lambda i: (i, 0))
-    big = jax.ShapeDtypeStruct((1024, 1024), BF16)
-    small = jax.ShapeDtypeStruct((32, positions), BF16)
+    big = pltpu.HBM((1024, 1024), BF16)
+    small = pltpu.HBM((32, positions), BF16)
     return pl.pallas_call(
         middle_kernel,
         grid=(4,),
         in_specs=[square, square, cols, cols] + [part] * 4 + [full(wu.shape)],
         out_specs=[square, rows, rows, cols] + [part] * 4 + [full((64, 128))],
-        out_shape=[big, big, big, jax.ShapeDtypeStruct((chan, positions), BF16)]
+        out_shape=[big, big, big, pltpu.HBM((chan, positions), BF16)]
         + [small] * 4
         + [jax.ShapeDtypeStruct((64, 128), F32)],
         scratch_shapes=[pltpu.VMEM((8192, 128), F32), pltpu.VMEM((256, 1024), F32)],
@@ -313,7 +313,7 @@
         in_specs=[pl.BlockSpec(memory_space=pltpu.SMEM), vmem, vmem, vmem]
         + [pl.BlockSpec(memory_space=pl.ANY)] * len(after),
         out_specs=[vmem, vmem, vmem],
-        out_shape=HALF + [jax.ShapeDtypeStruct((1024, 1024), BF16)],
+        out_shape=HALF + [pltpu.HBM((1024, 1024), BF16)],
         scratch_shapes=[pltpu.VMEM((1024, 1024), F32)],
         compiler_params=params(28),
         cost_estimate=cost(7),
@@ -333,7 +333,7 @@
         join_kernel,
         in_specs=[vmem] * 4,
         out_specs=vmem,
-        out_shape=jax.ShapeDtypeStruct((16, 2, 8, 8, 512), BF16),
+        out_shape=pltpu.HBM((16, 2, 8, 8, 512), BF16),
         compiler_params=params(20),
         cost_estimate=cost(3),
         name="join",
@@ -385,7 +385,8 @@
     )(parts, after)
 
 
-def input_kernel(shifted_ref, first_ref, gate_ref, after_ref, out_ref):
+def input_kernel(shifted_ref, first_ref, gate_ref, after_ref, out_ref, done_ref):
+    done_ref[...] = jnp.zeros_like(done_ref)
     spread = tn(shifted_ref[...], first_ref[...])
     for q in range(4):
         at = slice(q * 1024, (q + 1) * 1024)
@@ -403,8 +404,11 @@
             cols,
             pl.BlockSpec(memory_space=pl.ANY),
         ],
-        out_specs=cols,
-        out_shape=jax.ShapeDtypeStruct(gate_in.shape, BF16),
+        out_specs=[cols, full((8, 128))],
+        out_shape=[
+            jax.ShapeDtypeStruct(gate_in.shape, BF16),
+            jax.ShapeDtypeStruct((8, 128), F32),
+        ],
         compiler_params=params(60),
         cost_estimate=cost(7),
         name="input_part",
@@ -490,16 +494,16 @@
     down = down.reshape(4, 32, 64)[order].reshape(128, 64)
     small = jnp.concatenate([up.reshape(16, 512), down.reshape(16, 512)], axis=0)
     first_send, first_keep, shifted = first_part(
-        table, returned, rows, twiddle, [mixed_out, second_got]
+        table, returned, rows, twiddle, [down, second_got]
     )
     small = (small + swap(small, "x", 1)) + (swap(small, "x", 2) + swap(small, "x", 3))
     joined = join(first_keep, swap(first_send, "core", 1), second_keep, second_got)
     parts = lax.all_to_all(joined, PLANE, 0, 0, tiled=True)
     small = small + swap(small, "yh", 1)
     both = plane_sum(parts, small)
-    input_grad = input_part(shifted, first, gate_in, both)
+    input_grad, done = input_part(shifted, first, gate_in, both)
     both = lax.all_to_all(both, "z", 0, 0, tiled=True)
-    both = z_sum(both, input_grad)
+    both = z_sum(both, done)
     small = both[2:].reshape(32, 512)
     both = both[:2].reshape(2, 2, 4, 512)
     mine = lax.dynamic_index_in_dim(both, core, 1, keepdims=False)

time: 334 us -> 332 us (level)
  local copies, waits for them, and re-layouts: 30.8 us -> 25 us
    unnamed x57 -> x47, local copies, waits for them, and re-layouts: 23.4 us -> 16.8 us
  transfers between devices with their start and end apart: 21 -> 21, of which waited for: 14 -> 14; matrix products, arithmetic and copies ran while one was open for 1% -> 2% of each run, Pallas kernels for 7% -> 7%
where the time goes in v4:
time: 332 us; the launch traced here: 331 us
  waiting for transfers between devices  149 us (45%)
  Pallas kernels  63.8 us (19%)
  starting transfers between devices  60.3 us (18%)
  blocking collectives  31.9 us (10%)
  local copies, waits for them, and re-layouts  25 us (8%)
    ppermute x16, waiting for transfers between devices, swap(): return lax.ppermute(values, axis, [(i, i ^ bit) for i in range(size)])  138 us
    all_to_all x1, blocking collectives, local(): lax.all_to_all(fan(fan_plane_kernel, column, (16, 2, 8, 8, 512), [grads[1...  31.9 us
    pallas_call x1, Pallas kernels, middle(): pl.pallas_call(middle_kernel, grid=(4,), in_specs=[square, square, cols,...  21.8 us
    ppermute x16, starting transfers between devices, swap(): return lax.ppermute(values, axis, [(i, i ^ bit) for i in range(size)])  20.4 us
    unnamed x47, local copies, waits for them, and re-layouts  16.8 us
    all_to_all x1, starting transfers between devices, local(): lax.all_to_all(seg.reshape(64, 16, 1024), SEQ, 0, 0, tiled=True)  11.1 us
    all_to_all x1, starting transfers between devices, local(): lax.all_to_all(back.reshape(64, 16, 1024), SEQ, 0, 0, tiled=True)  10.1 us
    all_to_all x1, starting transfers between devices, start_gather(): lax.all_to_all(fan(fan_kernel, rows, (8,) + rows.shape, after), 'z', 0, 0...  7.11 us
  transfers between devices with their start and end apart: 21, of which 14 were waited for; matrix products, arithmetic and copies ran while one was open for 2% of the time, Pallas kernels for 7%

profile of v4, /device:TPU:1, one launch (start us, length us, event | category | flops | bytes accessed | tf_op | source)
XLA Modules:
  0.0 330.8 jit_solution(17404624022283965517)
XLA Ops:
  0.7 0.8 copy.44
  1.5 1.2 gather_fusion
  2.7 4.8 %grads_part.1 = (bf16[32,16384]{1,0:T(8,128)(2,1)}, bf16[32,16384]{1,0:T(8,128)(2,1)}, bf16[32,16384]{1,0:T(8,128)(2,1)}, bf16[32,16384]{1,0:T(8,128)(2,1)}) custom-call(bf16[64,16384]{1,0:T(8,128)(2,1)} %cot_ref.5, bf16[128,64]{1,0:T(8,128)(2,1)} %bitcast.50), custom_call_target="tpu_custom_call" | custom-call | bytes 12000 | tf_op jit(solution)/shard_map/grads_part/pallas_call | solution.py:55
  7.5 3.3 collective-permute-start.1
  11.4 1.7 collective-permute-done
  13.1 1.2 copy-done.9
  14.3 0.7 fan.2
  15.0 7.1 %all-to-all-start = ((bf16[8,2,8,512]{3,2,1,0:T(8,128)(2,1)}), bf16[8,2,8,512]{3,2,1,0:T(8,128)(2,1)S(1)}, u32[]{:S(2)}, u32[]{:S(2)}) async-start(bf16[8,2,8,512]{3,2,1,0:T(8,128)(2,1)} %fan.2), calls=%async_computation | async-start | bytes 262144 | tf_op jit(solution)/shard_map/all_to_all | solution.py:462
  22.1 4.3 %gated_part.1.refs_2_.rows_ref = bf16[1024,1024]{1,0:T(8,128)(2,1)} custom-call(bf16[64,16384]{1,0:T(8,128)(2,1)} %tok_ref.1, bf16[64,16384]{1,0:T(8,128)(2,1)} %gate_ref.5), custom_call_target="tpu_custom_call" | custom-call | bytes 12000 | tf_op jit(solution)/shard_map/gated_part/pallas_call | solution.py:77
  26.4 3.6 %all-to-all-done.column_ref = bf16[8,2,8,512]{3,2,1,0:T(8,128)(2,1)S(1)} async-done(((bf16[8,2,8,512]{3,2,1,0:T(8,128)(2,1)}), bf16[8,2,8,512]{3,2,1,0:T(8,128)(2,1)S(1)}, u32[]{:S(2)}, u32[]{:S(2)}) %all-to-all-start) | async-done | bytes 131104 | tf_op jit(solution)/shard_map/all_to_all | solution.py:462
  30.0 5.7 %collective-permute-done.2.refs_1_.g2 = bf16[32,16384]{1,0:T(8,128)(2,1)S(1)} collective-permute-done((bf16[32,16384]{1,0:T(8,128)(2,1)}, bf16[32,16384]{1,0:T(8,128)(2,1)S(1)}, u32[]{:S(2)}, u32[]{:S(2)}) %collective-permute-start.2) | collective-permute-done | bytes 1048608 | tf_op jit(solution)/shard_map/ppermute | solution.py:445
  35.7 1.6 copy-done
  37.3 1.6 fan.3
  39.0 31.9 %all_to_all.30.own_ref = bf16[16,2,8,8,512]{4,3,2,1,0:T(8,128)(2,1)S(1)} all-to-all(bf16[16,2,8,8,512]{4,3,2,1,0:T(8,128)(2,1)} %fan.3), channel_id=1, replica_groups=mesh['z'=8,'yh'=2,'x'=4,'yl'=2,'core'=2] {'yh','x','yl'}, dimensions={0} | all-to-all | bytes 4194304 | tf_op jit(solution)/shard_map/all_to_all | solution.py:479
  70.9 1.4 slice_bitcast_fusion
  72.3 2.4 collective-permute-start.3
  74.8 2.2 collective-permute-done.3.other_ref
  77.0 0.7 assemble.2
  77.7 4.3 %segment.1 = bf16[1024,1024]{1,0:T(8,128)(2,1)} custom-call(bf16[1024,1024]{1,0:T(8,128)(2,1)S(1)} %bitcast.41, bf16[1024,1024]{1,0:T(8,128)(2,1)S(1)} %copy-done.1, f32[16,1024]{1,0:T(8,128)S(1)} %copy-done.15), custom_call_target="tpu_custom_call" | custom-call | bytes 18000 | tf_op jit(solution)/shard_map/segment/pallas_call | solution.py:154
  82.1 11.1 %all-to-all-start.2 = ((bf16[64,16,1024]{2,1,0:T(8,128)(2,1)}), bf16[64,16,1024]{2,1,0:T(8,128)(2,1)}, u32[]{:S(2)}, u32[]{:S(2)}) async-start(bf16[64,16,1024]{2,1,0:T(8,128)(2,1)} %bitcast.45), calls=%async_computation.2 | async-start | bytes 4194304 | tf_op jit(solution)/shard_map/all_to_all | solution.py:484
  93.2 0.7 collective-permute-start.4
  94.0 0.6 gather_fusion.1
  94.7 1.8 collective-permute-done.4.other_ref
  96.6 1.6 copy-done.3
  98.1 1.4 assemble.3
  99.5 1.3 copy-done.5
  100.8 38.7 %collective-permute-done.5.g3 = bf16[32,16384]{1,0:T(8,128)(2,1)} collective-permute-done((bf16[32,16384]{1,0:T(8,128)(2,1)}, bf16[32,16384]{1,0:T(8,128)(2,1)}, u32[]{:S(2)}, u32[]{:S(2)}) %collective-permute-start.5) | collective-permute-done | bytes 1048608 | tf_op jit(solution)/shard_map/ppermute | solution.py:445
  139.6 2.2 all-to-all-done.2
  141.7 1.6 copy-done.6
  143.3 1.2 copy-done.8
  144.6 1.2 copy-done.10
  145.8 21.8 %middle.1 = (bf16[1024,1024]{1,0:T(8,128)(2,1)}, bf16[1024,1024]{1,0:T(8,128)(2,1)}, bf16[1024,1024]{1,0:T(8,128)(2,1)}, bf16[64,16384]{1,0:T(8,128)(2,1)}, bf16...) custom-call(bf16[1024,1024]{1,0:T(8,128)(2,1)} %bitcast.8.moved_ref,, ...), custom_call_target="tpu_custom_call" | custom-call | bytes 75000 | tf_op jit(solution)/shard_map/middle/pallas_call | solution.py:248
  167.6 10.1 %all-to-all-start.3 = ((bf16[64,16,1024]{2,1,0:T(8,128)(2,1)}), bf16[64,16,1024]{2,1,0:T(8,128)(2,1)}, u32[]{:S(2)}, u32[]{:S(2)}) async-start(bf16[64,16,1024]{2,1,0:T(8,128)(2,1)} %bitcast.46), calls=%async_computation.3 | async-start | bytes 4194304 | tf_op jit(solution)/shard_map/all_to_all | solution.py:488
  177.8 1.2 collective-permute-start.6
  179.0 1.7 collective-permute-start.8
  180.7 1.6 copy-done.11
  182.3 1.6 copy-done.12
  183.9 4.1 %second_part.1 = (bf16[16,8,8,512]{3,2,1,0:T(8,128)(2,1)}, f32[16,8,8,512]{3,2,1,0:T(8,128)S(1)}) custom-call(s32[17]{0:T(128)S(1)} %pad_add_fusion.table_ref, bf16[1024,1024]{1,0:T(8,128)(2,1)S(1)} %copy-done.12, bf16[1024,1024]{1,0:T(8,128)(2,1)S(1)} %copy-done.11), custom_call_target="tpu_custom_call" | custom-call | bytes 21000 | tf_op jit(solution)/shard_map/second_part/pallas_call | solution.py:287
  188.0 1.4 copy-done.13
  189.5 34.9 %collective-permute-done.7.p2 = bf16[32,16384]{1,0:T(8,128)(2,1)} collective-permute-done((bf16[32,16384]{1,0:T(8,128)(2,1)}, bf16[32,16384]{1,0:T(8,128)(2,1)}, u32[]{:S(2)}, u32[]{:S(2)}) %collective-permute-start.7) | collective-permute-done | bytes 1048608 | tf_op jit(solution)/shard_map/ppermute | solution.py:445
  224.4 23.5 %collective-permute-done.8.p3 = bf16[32,16384]{1,0:T(8,128)(2,1)} collective-permute-done((bf16[32,16384]{1,0:T(8,128)(2,1)}, bf16[32,16384]{1,0:T(8,128)(2,1)}, u32[]{:S(2)}, u32[]{:S(2)}) %collective-permute-start.8) | collective-permute-done | bytes 1048608 | tf_op jit(solution)/shard_map/ppermute | solution.py:445
  247.9 5.9 %output_part.1 = (bf16[64,16384]{1,0:T(8,128)(2,1)}, f32[128,64]{1,0:T(8,128)}) custom-call(bf16[64,16384]{1,0:T(8,128)(2,1)} %get-tuple-element.32.mixer_ref, bf16[32,16384]{1,0:T(8,128)(2,1)} %get-tuple-element.33.p0, bf16[32,16384]{1,0:T(8,128)(2,1)} %collective-permute-done.6.p1, bf16[32,16384]{1,0:T(8,128)(2,1)} %collective-permute-done.7.p2, ...), custom_call_target="tpu_custom_call" | custom-call | bytes 24000 | tf_op jit(solution)/shard_map/output_part/pallas_call | solution.py:431
  253.8 1.4 gather_fusion.2
  255.3 4.9 %first_part.1 = (bf16[16,8,8,512]{3,2,1,0:T(8,128)(2,1)S(1)}, f32[16,8,8,512]{3,2,1,0:T(8,128)S(1)}, bf16[1024,1024]{1,0:T(8,128)(2,1)}) custom-call(s32[17]{0:T(128)S(1)} %pad_add_fusion.table_ref, bf16[1024,1024]{1,0:T(8,128)(2,1)} %bitcast.15.back_ref, bf16[1024,1024]{1,0:T(8,128)(2,1)S(1)} %copy-done.1, f32[16,1024]{1,0:T(8,128)S(1)} %copy-done.15, ...), custom_call_target="tpu_custom_call" | custom-call | bytes 21000 | tf_op jit(solution)/shard_map/first_part/pallas_call | solution.py:311
  260.1 0.5 collective-permute-start.10
  260.6 2.3 collective-permute-done.10.got_ref
  262.9 1.7 join.1
  264.6 5.3 %all-to-all-start.4 = ((bf16[16,2,8,8,512]{4,3,2,1,0:T(8,128)(2,1)}), bf16[16,2,8,8,512]{4,3,2,1,0:T(8,128)(2,1)S(1)}, u32[]{:S(2)}, u32[]{:S(2)}) async-start(bf16[16,2,8,8,512]{4,3,2,1,0:T(8,128)(2,1)} %join.1), calls=%async_computation.4 | async-start | bytes 4194304 | tf_op jit(solution)/shard_map/all_to_all | solution.py:501
  270.0 0.6 gather_fusion.3
  270.9 2.6 collective-permute-start.13
  273.6 0.6 collective-permute-start.12
  274.3 24.8 %collective-permute-done.13 = f32[32,512]{1,0:T(8,128)S(1)} collective-permute-done((f32[32,512]{1,0:T(8,128)S(1)}, f32[32,512]{1,0:T(8,128)S(1)}, u32[]{:S(2)}, u32[]{:S(2)}) %collective-permute-start.13) | collective-permute-done | bytes 65568 | tf_op jit(solution)/shard_map/ppermute | solution.py:445
  299.3 2.6 collective-permute-start.14
  301.9 2.1 collective-permute-done.14
  304.0 1.1 plane_sum.1.after_ref
  305.1 6.2 %all-to-all-start.5 = ((bf16[8,6,8,512]{3,2,1,0:T(8,128)(2,1)}), bf16[8,6,8,512]{3,2,1,0:T(8,128)(2,1)S(1)}, u32[]{:S(2)}, u32[]{:S(2)}) async-start(bf16[8,6,8,512]{3,2,1,0:T(8,128)(2,1)} %plane_sum.1.after_ref), calls=%async_computation.5 | async-start | bytes 786432 | tf_op jit(solution)/shard_map/all_to_all | solution.py:505
  311.3 6.5 %input_part.1 = (bf16[64,16384]{1,0:T(8,128)(2,1)}, f32[8,128]{1,0:T(8,128)}) custom-call(bf16[1024,1024]{1,0:T(8,128)(2,1)} %get-tuple-element.43.shifted_ref, bf16[1024,1024]{1,0:T(8,128)(2,1)} %bitcast.42, bf16[64,16384]{1,0:T(8,128)(2,1)} %gate_ref.5, bf16[8,6,8,512]{3,2,1,0:T(8,128)(2,1)} %plane_sum.1.after_ref), custom_call_target="tpu_custom_call" | custom-call | bytes 21000 | tf_op jit(solution)/shard_map/input_part/pallas_call | solution.py:398
  317.8 4.9 %all-to-all-done.5.parts_ref = bf16[8,6,8,512]{3,2,1,0:T(8,128)(2,1)S(1)} async-done(((bf16[8,6,8,512]{3,2,1,0:T(8,128)(2,1)}), bf16[8,6,8,512]{3,2,1,0:T(8,128)(2,1)S(1)}, u32[]{:S(2)}, u32[]{:S(2)}) %all-to-all-start.5) | async-done | bytes 393248 | tf_op jit(solution)/shard_map/all_to_all | solution.py:505
  322.8 0.7 copy-done.16
  323.6 4.3 %collective-permute-start.15 = (f32[2,4,512]{2,1,0:T(4,128)S(1)}, f32[2,4,512]{2,1,0:T(4,128)S(1)}, u32[]{:S(2)}, u32[]{:S(2)}) collective-permute-start(f32[2,4,512]{2,1,0:T(4,128)S(1)} %get-tuple-element.82), channel_id=1, source_target_pairs={{0,1},{1,0},{2,3},{3,2},{4,5},{5,4},{6,7},{7,6},{8,9},{9,8},{10,11... | collective-permute-start | bytes 49160 | tf_op jit(solution)/shard_map/ppermute | solution.py:445
  327.9 0.7 copy.52
  328.6 0.6 reshape.104
  329.3 0.6 fusion.2
  330.1 0.7 reshape.103
  (75 shorter events, 2.3 us)
Async XLA Ops:
  0.6 10.1 %copy-start.19 = (bf16[4,1024]{1,0:T(4,128)(2,1)S(1)}, bf16[4,1024]{1,0:T(4,128)(2,1)}, u32[]{:S(2)}) copy-start(bf16[4,1024]{1,0:T(4,128)(2,1)} %param.13) | copy-start | bytes 24580
  0.6 10.2 %copy-start.18 = (bf16[4,1024]{1,0:T(4,128)(2,1)S(1)}, bf16[4,1024]{1,0:T(4,128)(2,1)}, u32[]{:S(2)}) copy-start(bf16[4,1024]{1,0:T(4,128)(2,1)} %param.14) | copy-start | bytes 24580
  7.5 22.5 %collective-permute-start.1 = (bf16[32,16384]{1,0:T(8,128)(2,1)}, bf16[32,16384]{1,0:T(8,128)(2,1)S(1)}, u32[]{:S(2)}, u32[]{:S(2)}) collective-permute-start(bf16[32,16384]{1,0:T(8,128)(2,1)} %get-tuple-element.29), channel_id=1, source_target_pairs={{0,1},{1,0},{2,3},{3,2},{4,5},{5,4},{6,7},{7,6},{8,9},{9,8},{10,11... | collective-permute-start | bytes 3145736 | tf_op jit(solution)/shard_map/ppermute | solution.py:445
  10.8 24.9 %collective-permute-start.2 = (bf16[32,16384]{1,0:T(8,128)(2,1)}, bf16[32,16384]{1,0:T(8,128)(2,1)S(1)}, u32[]{:S(2)}, u32[]{:S(2)}) collective-permute-start(bf16[32,16384]{1,0:T(8,128)(2,1)} %get-tuple-element.30), channel_id=1, source_target_pairs={{0,2},{1,3},{2,0},{3,1},{4,6},{5,7},{6,4},{7,5},{8,10},{9,11},{10,... | collective-permute-start | bytes 3145736 | tf_op jit(solution)/shard_map/ppermute | solution.py:445
  11.2 1.9 collective-permute-start
  13.1 1.2 copy-start.9
  15.0 15.0 %all-to-all-start = ((bf16[8,2,8,512]{3,2,1,0:T(8,128)(2,1)}), bf16[8,2,8,512]{3,2,1,0:T(8,128)(2,1)S(1)}, u32[]{:S(2)}, u32[]{:S(2)}) async-start(bf16[8,2,8,512]{3,2,1,0:T(8,128)(2,1)} %fan.2), calls=%async_computation | async-start | bytes 262144 | tf_op jit(solution)/shard_map/all_to_all | solution.py:462
  35.7 1.6 copy-start
  37.3 1.7 copy-start.7
  70.9 6.2 %copy-start.2 = (bf16[16,2,8,8,512]{4,3,2,1,0:T(8,128)(2,1)}, bf16[16,2,8,8,512]{4,3,2,1,0:T(8,128)(2,1)S(1)}, u32[]{:S(2)}) copy-start(bf16[16,2,8,8,512]{4,3,2,1,0:T(8,128)(2,1)S(1)} %all_to_all.30.own_ref) | copy-start | bytes 6291460
  72.3 4.7 %collective-permute-start.3 = (bf16[16,8,8,512]{3,2,1,0:T(8,128)(2,1)S(1)}, bf16[16,8,8,512]{3,2,1,0:T(8,128)(2,1)S(1)}, u32[]{:S(2)}, u32[]{:S(2)}) collective-permute-start(bf16[16,8,8,512]{3,2,1,0:T(8,128)(2,1)S(1)} %get-tuple-element.75), channel_id=1, source_target_pairs={{0,1},{1,0},{2,3},{3,2},{4,5},{5,4},{6,7},{7,6},{8,9},{9,8},{10,11... | collective-permute-start | bytes 3145736 | tf_op jit(solution)/shard_map/ppermute | solution.py:445
  74.8 2.9 copy-start.1
  74.8 2.9 copy-start.15
  77.7 4.4 %copy-start.4 = (bf16[8,16,8,1024]{3,2,1,0:T(8,128)(2,1)}, bf16[8,16,8,1024]{3,2,1,0:T(8,128)(2,1)S(1)}, u32[]{:S(2)}) copy-start(bf16[8,16,8,1024]{3,2,1,0:T(8,128)(2,1)S(1)} %assemble.2) | copy-start | bytes 6291460
  82.1 11.9 %copy-start.17 = (bf16[1,64,128]{2,1,0:T(8,128)(2,1)S(1)}, bf16[1,64,128]{2,1,0:T(8,128)(2,1)}, u32[]{:S(2)}) copy-start(bf16[1,64,128]{2,1,0:T(8,128)(2,1)} %param.15) | copy-start | bytes 49156
  82.1 59.7 %all-to-all-start.2 = ((bf16[64,16,1024]{2,1,0:T(8,128)(2,1)}), bf16[64,16,1024]{2,1,0:T(8,128)(2,1)}, u32[]{:S(2)}, u32[]{:S(2)}) async-start(bf16[64,16,1024]{2,1,0:T(8,128)(2,1)} %bitcast.45), calls=%async_computation.2 | async-start | bytes 4194304 | tf_op jit(solution)/shard_map/all_to_all | solution.py:484
  93.2 3.4 %collective-permute-start.4 = (bf16[16,8,8,512]{3,2,1,0:T(8,128)(2,1)}, bf16[16,8,8,512]{3,2,1,0:T(8,128)(2,1)}, u32[]{:S(2)}, u32[]{:S(2)}) collective-permute-start(bf16[16,8,8,512]{3,2,1,0:T(8,128)(2,1)} %get-tuple-element.74), channel_id=1, source_target_pairs={{0,1},{1,0},{2,3},{3,2},{4,5},{5,4},{6,7},{7,6},{8,9},{9,8},{10,11... | collective-permute-start | bytes 3145736 | tf_op jit(solution)/shard_map/ppermute | solution.py:445
  93.9 45.6 %collective-permute-start.5 = (bf16[32,16384]{1,0:T(8,128)(2,1)}, bf16[32,16384]{1,0:T(8,128)(2,1)}, u32[]{:S(2)}, u32[]{:S(2)}) collective-permute-start(bf16[32,16384]{1,0:T(8,128)(2,1)} %get-tuple-element.31), channel_id=1, source_target_pairs={{0,3},{1,2},{2,1},{3,0},{4,7},{5,6},{6,5},{7,4},{8,11},{9,10},{10,... | collective-permute-start | bytes 3145736 | tf_op jit(solution)/shard_map/ppermute | solution.py:445
  96.6 1.6 copy-start.3
  99.5 1.3 copy-start.5
  141.7 1.6 copy-start.6
  143.3 1.2 copy-start.8
  144.6 1.2 copy-start.10
  167.6 87.6 %all-to-all-start.3 = ((bf16[64,16,1024]{2,1,0:T(8,128)(2,1)}), bf16[64,16,1024]{2,1,0:T(8,128)(2,1)}, u32[]{:S(2)}, u32[]{:S(2)}) async-start(bf16[64,16,1024]{2,1,0:T(8,128)(2,1)} %bitcast.46), calls=%async_computation.3 | async-start | bytes 4194304 | tf_op jit(solution)/shard_map/all_to_all | solution.py:488
  177.8 11.7 %collective-permute-start.6 = (bf16[32,16384]{1,0:T(8,128)(2,1)}, bf16[32,16384]{1,0:T(8,128)(2,1)}, u32[]{:S(2)}, u32[]{:S(2)}) collective-permute-start(bf16[32,16384]{1,0:T(8,128)(2,1)} %get-tuple-element.34), channel_id=1, source_target_pairs={{0,1},{1,0},{2,3},{3,2},{4,5},{5,4},{6,7},{7,6},{8,9},{9,8},{10,11... | collective-permute-start | bytes 3145736 | tf_op jit(solution)/shard_map/ppermute | solution.py:445
  179.0 45.4 %collective-permute-start.7 = (bf16[32,16384]{1,0:T(8,128)(2,1)}, bf16[32,16384]{1,0:T(8,128)(2,1)}, u32[]{:S(2)}, u32[]{:S(2)}) collective-permute-start(bf16[32,16384]{1,0:T(8,128)(2,1)} %get-tuple-element.35), channel_id=1, source_target_pairs={{0,2},{1,3},{2,0},{3,1},{4,6},{5,7},{6,4},{7,5},{8,10},{9,11},{10,... | collective-permute-start | bytes 3145736 | tf_op jit(solution)/shard_map/ppermute | solution.py:445
  179.0 68.9 %collective-permute-start.8 = (bf16[32,16384]{1,0:T(8,128)(2,1)}, bf16[32,16384]{1,0:T(8,128)(2,1)}, u32[]{:S(2)}, u32[]{:S(2)}) collective-permute-start(bf16[32,16384]{1,0:T(8,128)(2,1)} %get-tuple-element.36), channel_id=1, source_target_pairs={{0,3},{1,2},{2,1},{3,0},{4,7},{5,6},{6,5},{7,4},{8,11},{9,10},{10,... | collective-permute-start | bytes 3145736 | tf_op jit(solution)/shard_map/ppermute | solution.py:445
  180.7 1.6 copy-start.11
  182.3 1.6 copy-start.12
  188.0 1.4 copy-start.13
  189.4 65.9 %collective-permute-start.9 = (bf16[16,8,8,512]{3,2,1,0:T(8,128)(2,1)}, bf16[16,8,8,512]{3,2,1,0:T(8,128)(2,1)S(1)}, u32[]{:S(2)}, u32[]{:S(2)}) collective-permute-start(bf16[16,8,8,512]{3,2,1,0:T(8,128)(2,1)} %get-tuple-element.42), channel_id=1, source_target_pairs={{0,1},{1,0},{2,3},{3,2},{4,5},{5,4},{6,7},{7,6},{8,9},{9,8},{10,11... | collective-permute-start | bytes 3145736 | tf_op jit(solution)/shard_map/ppermute | solution.py:445
  255.3 7.6 %copy-start.14 = (f32[16,8,8,512]{3,2,1,0:T(8,128)S(1)}, f32[16,8,8,512]{3,2,1,0:T(8,128)}, u32[]{:S(2)}) copy-start(f32[16,8,8,512]{3,2,1,0:T(8,128)} %copy-done.13) | copy-start | bytes 6291460
  260.1 2.8 collective-permute-start.10
  264.6 39.4 %all-to-all-start.4 = ((bf16[16,2,8,8,512]{4,3,2,1,0:T(8,128)(2,1)}), bf16[16,2,8,8,512]{4,3,2,1,0:T(8,128)(2,1)S(1)}, u32[]{:S(2)}, u32[]{:S(2)}) async-start(bf16[16,2,8,8,512]{4,3,2,1,0:T(8,128)(2,1)} %join.1), calls=%async_computation.4 | async-start | bytes 4194304 | tf_op jit(solution)/shard_map/all_to_all | solution.py:501
  270.9 28.1 %collective-permute-start.13 = (f32[32,512]{1,0:T(8,128)S(1)}, f32[32,512]{1,0:T(8,128)S(1)}, u32[]{:S(2)}, u32[]{:S(2)}) collective-permute-start(f32[32,512]{1,0:T(8,128)S(1)} %constant_dynamic-update-slice_fusion.2), channel_id=1, source_target_pairs={{0,12},{4,8},{8,4},{12,0},{1,13},{5,9},{9,5},{13,1},{2,14},{6,10},... | collective-permute-start | bytes 196616 | tf_op jit(solution)/shard_map/ppermute | solution.py:445
  273.6 25.5 %collective-permute-start.12 = (f32[32,512]{1,0:T(8,128)S(1)}, f32[32,512]{1,0:T(8,128)S(1)}, u32[]{:S(2)}, u32[]{:S(2)}) collective-permute-start(f32[32,512]{1,0:T(8,128)S(1)} %constant_dynamic-update-slice_fusion.2), channel_id=1, source_target_pairs={{0,8},{4,12},{8,0},{12,4},{1,9},{5,13},{9,1},{13,5},{2,10},{6,14},... | collective-permute-start | bytes 196616 | tf_op jit(solution)/shard_map/ppermute | solution.py:445
  274.2 25.1 %collective-permute-start.11 = (f32[32,512]{1,0:T(8,128)S(1)}, f32[32,512]{1,0:T(8,128)S(1)}, u32[]{:S(2)}, u32[]{:S(2)}) collective-permute-start(f32[32,512]{1,0:T(8,128)S(1)} %constant_dynamic-update-slice_fusion.2), channel_id=1, source_target_pairs={{0,4},{4,0},{8,12},{12,8},{1,5},{5,1},{9,13},{13,9},{2,6},{6,2},{1... | collective-permute-start | bytes 196616 | tf_op jit(solution)/shard_map/ppermute | solution.py:445
  299.3 4.7 %collective-permute-start.14 = (f32[32,512]{1,0:T(8,128)S(1)}, f32[32,512]{1,0:T(8,128)S(1)}, u32[]{:S(2)}, u32[]{:S(2)}) collective-permute-start(f32[32,512]{1,0:T(8,128)S(1)} %add_add_fusion), channel_id=1, source_target_pairs={{0,16},{16,0},{1,17},{17,1},{2,18},{18,2},{3,19},{19,3},{4,20},{20... | collective-permute-start | bytes 196616 | tf_op jit(solution)/shard_map/ppermute | solution.py:445
  305.1 17.7 %all-to-all-start.5 = ((bf16[8,6,8,512]{3,2,1,0:T(8,128)(2,1)}), bf16[8,6,8,512]{3,2,1,0:T(8,128)(2,1)S(1)}, u32[]{:S(2)}, u32[]{:S(2)}) async-start(bf16[8,6,8,512]{3,2,1,0:T(8,128)(2,1)} %plane_sum.1.after_ref), calls=%async_computation.5 | async-start | bytes 786432 | tf_op jit(solution)/shard_map/all_to_all | solution.py:505
  322.8 0.7 copy-start.16
  323.6 5.7 %collective-permute-start.15 = (f32[2,4,512]{2,1,0:T(4,128)S(1)}, f32[2,4,512]{2,1,0:T(4,128)S(1)}, u32[]{:S(2)}, u32[]{:S(2)}) collective-permute-start(f32[2,4,512]{2,1,0:T(4,128)S(1)} %get-tuple-element.82), channel_id=1, source_target_pairs={{0,1},{1,0},{2,3},{3,2},{4,5},{5,4},{6,7},{7,6},{8,9},{9,8},{10,11... | collective-permute-start | bytes 49160 | tf_op jit(solution)/shard_map/ppermute | solution.py:445

commit v5 on v4

--- a/solution.py
+++ b/solution.py
@@ -415,7 +415,7 @@
     )(shifted, first, gate_in, after)
 
 
-def output_kernel(mixer_ref, p0, p1, p2, p3, cot_ref, wd_ref, out_ref, down_ref):
+def output_kernel(mixer_ref, p0, p1, p2, p3, cot_ref, wd_ref, after_ref, out_ref, down_ref):
     @pl.when(pl.program_id(0) == 0)
     def _():
         down_ref[...] = jnp.zeros_like(down_ref)
@@ -425,19 +425,19 @@
     down_ref[...] += nt(permuted, cot_ref[...])
 
 
-def output_part(mixer, parts, cotangent, wd):
+def output_part(mixer, parts, cotangent, wd, after):
     cols = pl.BlockSpec((64, 4096), lambda i: (0, i))
     part = pl.BlockSpec((32, 4096), lambda i: (0, i))
     return pl.pallas_call(
         output_kernel,
         grid=(4,),
-        in_specs=[cols] + [part] * 4 + [cols, full(wd.shape)],
+        in_specs=[cols] + [part] * 4 + [cols, full(wd.shape), pl.BlockSpec(memory_space=pl.ANY)],
         out_specs=[cols, full((128, 64))],
         out_shape=[jax.ShapeDtypeStruct(mixer.shape, BF16), jax.ShapeDtypeStruct((128, 64), F32)],
         compiler_params=params(60),
         cost_estimate=cost(8),
         name="output_part",
-    )(mixer, *parts, cotangent, wd)
+    )(mixer, *parts, cotangent, wd, after)
 
 
 def swap(values, axis, bit):
@@ -489,16 +489,16 @@
     acts = chan_swap(acts)
     second_send, second_keep = second_part(table, weighted, left)
     second_got = swap(second_send, "core", 1)
-    mixed_out, down = output_part(mixer, acts, cotangent, wd)
+    first_send, first_keep, shifted = first_part(
+        table, returned, rows, twiddle, [acts[1], acts[2], acts[3], second_got]
+    )
+    joined = join(first_keep, swap(first_send, "core", 1), second_keep, second_got)
+    parts = lax.all_to_all(joined, PLANE, 0, 0, tiled=True)
+    mixed_out, down = output_part(mixer, acts, cotangent, wd, joined)
     up = up.reshape(64, 4, 32)[:, order].reshape(64, 128)
     down = down.reshape(4, 32, 64)[order].reshape(128, 64)
     small = jnp.concatenate([up.reshape(16, 512), down.reshape(16, 512)], axis=0)
-    first_send, first_keep, shifted = first_part(
-        table, returned, rows, twiddle, [down, second_got]
-    )
     small = (small + swap(small, "x", 1)) + (swap(small, "x", 2) + swap(small, "x", 3))
-    joined = join(first_keep, swap(first_send, "core", 1), second_keep, second_got)
-    parts = lax.all_to_all(joined, PLANE, 0, 0, tiled=True)
     small = small + swap(small, "yh", 1)
     both = plane_sum(parts, small)
     input_grad, done = input_part(shifted, first, gate_in, both)

time: 332 us -> 330 us (level)
  waiting for transfers between devices: 149 us -> 141 us
  local copies, waits for them, and re-layouts: 25 us -> 31.7 us
    ppermute x16, waiting for transfers between devices: 138 us -> 131 us  [swap(): return lax.ppermute(values, axis, [(i, i ^ bit) for i in range(size)])]
    unnamed x47 -> x61, local copies, waits for them, and re-layouts: 16.8 us -> 23.4 us
where the time goes in v5:
time: 330 us; the launch traced here: 329 us
  waiting for transfers between devices  141 us (43%)
  Pallas kernels  62.8 us (19%)
  starting transfers between devices  60.2 us (18%)
  blocking collectives  31.9 us (10%)
  local copies, waits for them, and re-layouts  31.7 us (10%)
    ppermute x16, waiting for transfers between devices, swap(): return lax.ppermute(values, axis, [(i, i ^ bit) for i in range(size)])  131 us
    all_to_all x1, blocking collectives, local(): lax.all_to_all(fan(fan_plane_kernel, column, (16, 2, 8, 8, 512), [grads[1...  31.9 us
    unnamed x61, local copies, waits for them, and re-layouts  23.4 us
    pallas_call x1, Pallas kernels, middle(): pl.pallas_call(middle_kernel, grid=(4,), in_specs=[square, square, cols,...  21.8 us
    ppermute x16, starting transfers between devices, swap(): return lax.ppermute(values, axis, [(i, i ^ bit) for i in range(size)])  20.3 us
    all_to_all x1, starting transfers between devices, local(): lax.all_to_all(seg.reshape(64, 16, 1024), SEQ, 0, 0, tiled=True)  11.1 us
    all_to_all x1, starting transfers between devices, local(): lax.all_to_all(back.reshape(64, 16, 1024), SEQ, 0, 0, tiled=True)  10.1 us
    all_to_all x1, starting transfers between devices, start_gather(): lax.all_to_all(fan(fan_kernel, rows, (8,) + rows.shape, after), 'z', 0, 0...  7.11 us
  transfers between devices with their start and end apart: 21, of which 14 were waited for; matrix products, arithmetic and copies ran while one was open for 2% of the time, Pallas kernels for 7%

profile of v5, /device:TPU:1, one launch (start us, length us, event | category | flops | bytes accessed | tf_op | source)
XLA Modules:
  0.0 329.0 jit_solution(9740941473671072149)
XLA Ops:
  0.7 0.8 copy.44
  1.5 1.2 gather_fusion
  2.7 4.8 %grads_part.1 = (bf16[32,16384]{1,0:T(8,128)(2,1)}, bf16[32,16384]{1,0:T(8,128)(2,1)}, bf16[32,16384]{1,0:T(8,128)(2,1)}, bf16[32,16384]{1,0:T(8,128)(2,1)}) custom-call(bf16[64,16384]{1,0:T(8,128)(2,1)} %cot_ref.5, bf16[128,64]{1,0:T(8,128)(2,1)} %bitcast.48), custom_call_target="tpu_custom_call" | custom-call | bytes 12000 | tf_op jit(solution)/shard_map/grads_part/pallas_call | solution.py:55
  7.5 3.2 collective-permute-start.1
  11.4 1.7 collective-permute-done
  13.1 1.2 copy-done.14
  14.3 0.7 fan.2
  15.0 7.1 %all-to-all-start = ((bf16[8,2,8,512]{3,2,1,0:T(8,128)(2,1)}), bf16[8,2,8,512]{3,2,1,0:T(8,128)(2,1)S(1)}, u32[]{:S(2)}, u32[]{:S(2)}) async-start(bf16[8,2,8,512]{3,2,1,0:T(8,128)(2,1)} %fan.2), calls=%async_computation | async-start | bytes 262144 | tf_op jit(solution)/shard_map/all_to_all | solution.py:462
  22.1 4.3 %gated_part.1.refs_2_.rows_ref = bf16[1024,1024]{1,0:T(8,128)(2,1)} custom-call(bf16[64,16384]{1,0:T(8,128)(2,1)} %tok_ref.1, bf16[64,16384]{1,0:T(8,128)(2,1)} %gate_ref.5), custom_call_target="tpu_custom_call" | custom-call | bytes 12000 | tf_op jit(solution)/shard_map/gated_part/pallas_call | solution.py:77
  26.4 3.6 %all-to-all-done.column_ref = bf16[8,2,8,512]{3,2,1,0:T(8,128)(2,1)S(1)} async-done(((bf16[8,2,8,512]{3,2,1,0:T(8,128)(2,1)}), bf16[8,2,8,512]{3,2,1,0:T(8,128)(2,1)S(1)}, u32[]{:S(2)}, u32[]{:S(2)}) %all-to-all-start) | async-done | bytes 131104 | tf_op jit(solution)/shard_map/all_to_all | solution.py:462
  30.0 5.7 %collective-permute-done.2.refs_1_.g2 = bf16[32,16384]{1,0:T(8,128)(2,1)S(1)} collective-permute-done((bf16[32,16384]{1,0:T(8,128)(2,1)}, bf16[32,16384]{1,0:T(8,128)(2,1)S(1)}, u32[]{:S(2)}, u32[]{:S(2)}) %collective-permute-start.2) | collective-permute-done | bytes 1048608 | tf_op jit(solution)/shard_map/ppermute | solution.py:445
  35.7 1.6 copy-done
  37.3 1.6 fan.3
  38.9 31.9 %all_to_all.30.own_ref = bf16[16,2,8,8,512]{4,3,2,1,0:T(8,128)(2,1)S(1)} all-to-all(bf16[16,2,8,8,512]{4,3,2,1,0:T(8,128)(2,1)} %fan.3), channel_id=1, replica_groups=mesh['z'=8,'yh'=2,'x'=4,'yl'=2,'core'=2] {'yh','x','yl'}, dimensions={0} | all-to-all | bytes 4194304 | tf_op jit(solution)/shard_map/all_to_all | solution.py:479
  70.8 1.5 slice_bitcast_fusion
  72.4 2.4 collective-permute-start.3
  74.9 2.2 collective-permute-done.3.other_ref
  77.1 0.7 assemble.2
  77.8 4.4 %segment.1 = bf16[1024,1024]{1,0:T(8,128)(2,1)} custom-call(bf16[1024,1024]{1,0:T(8,128)(2,1)S(1)} %bitcast.40, bf16[1024,1024]{1,0:T(8,128)(2,1)S(1)} %copy-done.1, f32[16,1024]{1,0:T(8,128)S(1)} %copy-done.22), custom_call_target="tpu_custom_call" | custom-call | bytes 18000 | tf_op jit(solution)/shard_map/segment/pallas_call | solution.py:154
  82.2 11.1 %all-to-all-start.2 = ((bf16[64,16,1024]{2,1,0:T(8,128)(2,1)}), bf16[64,16,1024]{2,1,0:T(8,128)(2,1)}, u32[]{:S(2)}, u32[]{:S(2)}) async-start(bf16[64,16,1024]{2,1,0:T(8,128)(2,1)} %bitcast.43), calls=%async_computation.2 | async-start | bytes 4194304 | tf_op jit(solution)/shard_map/all_to_all | solution.py:484
  93.3 0.7 collective-permute-start.4
  94.8 1.8 collective-permute-done.4.other_ref
  96.7 1.6 copy-done.3
  98.3 1.4 assemble.3
  99.6 1.3 copy-done.5
  101.0 38.7 %collective-permute-done.5.g3 = bf16[32,16384]{1,0:T(8,128)(2,1)} collective-permute-done((bf16[32,16384]{1,0:T(8,128)(2,1)}, bf16[32,16384]{1,0:T(8,128)(2,1)}, u32[]{:S(2)}, u32[]{:S(2)}) %collective-permute-start.5) | collective-permute-done | bytes 1048608 | tf_op jit(solution)/shard_map/ppermute | solution.py:445
  139.7 2.2 all-to-all-done.2
  141.9 1.6 copy-done.6
  143.5 1.2 copy-done.8
  144.7 1.2 copy-done.15
  145.9 21.8 %middle.1 = (bf16[1024,1024]{1,0:T(8,128)(2,1)}, bf16[1024,1024]{1,0:T(8,128)(2,1)}, bf16[1024,1024]{1,0:T(8,128)(2,1)}, bf16[64,16384]{1,0:T(8,128)(2,1)}, bf16...) custom-call(bf16[1024,1024]{1,0:T(8,128)(2,1)} %bitcast.8.moved_ref,, ...), custom_call_target="tpu_custom_call" | custom-call | bytes 75000 | tf_op jit(solution)/shard_map/middle/pallas_call | solution.py:248
  167.7 10.1 %all-to-all-start.3 = ((bf16[64,16,1024]{2,1,0:T(8,128)(2,1)}), bf16[64,16,1024]{2,1,0:T(8,128)(2,1)}, u32[]{:S(2)}, u32[]{:S(2)}) async-start(bf16[64,16,1024]{2,1,0:T(8,128)(2,1)} %bitcast.44), calls=%async_computation.3 | async-start | bytes 4194304 | tf_op jit(solution)/shard_map/all_to_all | solution.py:488
  177.8 1.2 collective-permute-start.6
  179.0 1.7 collective-permute-start.8
  180.8 1.6 copy-done.18
  182.4 1.6 copy-done.19
  184.0 3.1 second_part.1
  187.1 1.3 copy-done.20
  188.5 35.9 %collective-permute-done.7.refs_1_.p2 = bf16[32,16384]{1,0:T(8,128)(2,1)S(1)} collective-permute-done((bf16[32,16384]{1,0:T(8,128)(2,1)}, bf16[32,16384]{1,0:T(8,128)(2,1)S(1)}, u32[]{:S(2)}, u32[]{:S(2)}) %collective-permute-start.7) | collective-permute-done | bytes 1048608 | tf_op jit(solution)/shard_map/ppermute | solution.py:445
  224.4 1.0 copy-done.10
  225.5 22.4 %collective-permute-done.8.refs_2_.p3 = bf16[32,16384]{1,0:T(8,128)(2,1)S(1)} collective-permute-done((bf16[32,16384]{1,0:T(8,128)(2,1)}, bf16[32,16384]{1,0:T(8,128)(2,1)S(1)}, u32[]{:S(2)}, u32[]{:S(2)}) %collective-permute-start.8) | collective-permute-done | bytes 1048608 | tf_op jit(solution)/shard_map/ppermute | solution.py:445
  247.9 1.0 copy-done.12
  248.8 1.0 copy-done.16
  249.8 1.2 copy-done.11
  251.0 1.2 copy-done.13
  252.3 1.2 copy-done.17
  253.5 4.9 %first_part.1 = (bf16[16,8,8,512]{3,2,1,0:T(8,128)(2,1)S(1)}, f32[16,8,8,512]{3,2,1,0:T(8,128)S(1)}, bf16[1024,1024]{1,0:T(8,128)(2,1)}) custom-call(s32[17]{0:T(128)S(1)} %pad_add_fusion.table_ref, bf16[1024,1024]{1,0:T(8,128)(2,1)} %bitcast.15.back_ref, bf16[1024,1024]{1,0:T(8,128)(2,1)S(1)} %copy-done.1, f32[16,1024]{1,0:T(8,128)S(1)} %copy-done.22, ...), custom_call_target="tpu_custom_call" | custom-call | bytes 21000 | tf_op jit(solution)/shard_map/first_part/pallas_call | solution.py:311
  258.9 2.3 collective-permute-done.10.got_ref
  261.1 1.7 join.1.after_ref
  262.8 5.3 %all-to-all-start.4 = ((bf16[16,2,8,8,512]{4,3,2,1,0:T(8,128)(2,1)}), bf16[16,2,8,8,512]{4,3,2,1,0:T(8,128)(2,1)S(1)}, u32[]{:S(2)}, u32[]{:S(2)}) async-start(bf16[16,2,8,8,512]{4,3,2,1,0:T(8,128)(2,1)} %join.1.after_ref), calls=%async_computation.4 | async-start | bytes 4194304 | tf_op jit(solution)/shard_map/all_to_all | solution.py:496
  269.1 5.9 %output_part.1 = (bf16[64,16384]{1,0:T(8,128)(2,1)}, f32[128,64]{1,0:T(8,128)}) custom-call(bf16[64,16384]{1,0:T(8,128)(2,1)} %get-tuple-element.32.mixer_ref, bf16[32,16384]{1,0:T(8,128)(2,1)} %get-tuple-element.33.p0, bf16[32,16384]{1,0:T(8,128)(2,1)} %copy-done.9, bf16[32,16384]{1,0:T(8,128)(2,1)} %copy-done.10, bf16[32,16384]{1,0:T(8,128)(2,1)} %copy-done.12, ...), custom_call_target="tpu_custom_call" | custom-call | bytes 24000 | tf_op jit(solution)/shard_map/output_part/pallas_call | solution.py:431
  275.0 1.4 gather_fusion.3
  276.5 2.6 collective-permute-start.13
  279.8 17.5 %collective-permute-done.13 = f32[32,512]{1,0:T(8,128)S(1)} collective-permute-done((f32[32,512]{1,0:T(8,128)S(1)}, f32[32,512]{1,0:T(8,128)S(1)}, u32[]{:S(2)}, u32[]{:S(2)}) %collective-permute-start.13) | collective-permute-done | bytes 65568 | tf_op jit(solution)/shard_map/ppermute | solution.py:445
  297.5 2.6 collective-permute-start.14
  300.1 2.1 collective-permute-done.14
  302.2 1.0 plane_sum.1.after_ref
  303.3 6.2 %all-to-all-start.5 = ((bf16[8,6,8,512]{3,2,1,0:T(8,128)(2,1)}), bf16[8,6,8,512]{3,2,1,0:T(8,128)(2,1)S(1)}, u32[]{:S(2)}, u32[]{:S(2)}) async-start(bf16[8,6,8,512]{3,2,1,0:T(8,128)(2,1)} %plane_sum.1.after_ref), calls=%async_computation.5 | async-start | bytes 786432 | tf_op jit(solution)/shard_map/all_to_all | solution.py:505
  309.5 6.5 %input_part.1 = (bf16[64,16384]{1,0:T(8,128)(2,1)}, f32[8,128]{1,0:T(8,128)}) custom-call(bf16[1024,1024]{1,0:T(8,128)(2,1)} %get-tuple-element.45.shifted_ref, bf16[1024,1024]{1,0:T(8,128)(2,1)} %bitcast.41, bf16[64,16384]{1,0:T(8,128)(2,1)} %gate_ref.5, bf16[8,6,8,512]{3,2,1,0:T(8,128)(2,1)} %plane_sum.1.after_ref), custom_call_target="tpu_custom_call" | custom-call | bytes 21000 | tf_op jit(solution)/shard_map/input_part/pallas_call | solution.py:398
  316.0 4.9 %all-to-all-done.5.parts_ref = bf16[8,6,8,512]{3,2,1,0:T(8,128)(2,1)S(1)} async-done(((bf16[8,6,8,512]{3,2,1,0:T(8,128)(2,1)}), bf16[8,6,8,512]{3,2,1,0:T(8,128)(2,1)S(1)}, u32[]{:S(2)}, u32[]{:S(2)}) %all-to-all-start.5) | async-done | bytes 393248 | tf_op jit(solution)/shard_map/all_to_all | solution.py:505
  320.9 0.7 copy-done.23
  321.7 4.3 %collective-permute-start.15 = (f32[2,4,512]{2,1,0:T(4,128)S(1)}, f32[2,4,512]{2,1,0:T(4,128)S(1)}, u32[]{:S(2)}, u32[]{:S(2)}) collective-permute-start(f32[2,4,512]{2,1,0:T(4,128)S(1)} %get-tuple-element.82), channel_id=1, source_target_pairs={{0,1},{1,0},{2,3},{3,2},{4,5},{5,4},{6,7},{7,6},{8,9},{9,8},{10,11... | collective-permute-start | bytes 49160 | tf_op jit(solution)/shard_map/ppermute | solution.py:445
  326.1 0.7 copy.52
  328.2 0.7 reshape.99
  (89 shorter events, 5.6 us)
Async XLA Ops:
  0.6 10.2 %copy-start.26 = (bf16[4,1024]{1,0:T(4,128)(2,1)S(1)}, bf16[4,1024]{1,0:T(4,128)(2,1)}, u32[]{:S(2)}) copy-start(bf16[4,1024]{1,0:T(4,128)(2,1)} %param.13) | copy-start | bytes 24580
  0.6 10.2 %copy-start.25 = (bf16[4,1024]{1,0:T(4,128)(2,1)S(1)}, bf16[4,1024]{1,0:T(4,128)(2,1)}, u32[]{:S(2)}) copy-start(bf16[4,1024]{1,0:T(4,128)(2,1)} %param.14) | copy-start | bytes 24580
  7.5 22.5 %collective-permute-start.1 = (bf16[32,16384]{1,0:T(8,128)(2,1)}, bf16[32,16384]{1,0:T(8,128)(2,1)S(1)}, u32[]{:S(2)}, u32[]{:S(2)}) collective-permute-start(bf16[32,16384]{1,0:T(8,128)(2,1)} %get-tuple-element.29), channel_id=1, source_target_pairs={{0,1},{1,0},{2,3},{3,2},{4,5},{5,4},{6,7},{7,6},{8,9},{9,8},{10,11... | collective-permute-start | bytes 3145736 | tf_op jit(solution)/shard_map/ppermute | solution.py:445
  10.8 24.9 %collective-permute-start.2 = (bf16[32,16384]{1,0:T(8,128)(2,1)}, bf16[32,16384]{1,0:T(8,128)(2,1)S(1)}, u32[]{:S(2)}, u32[]{:S(2)}) collective-permute-start(bf16[32,16384]{1,0:T(8,128)(2,1)} %get-tuple-element.30), channel_id=1, source_target_pairs={{0,2},{1,3},{2,0},{3,1},{4,6},{5,7},{6,4},{7,5},{8,10},{9,11},{10,... | collective-permute-start | bytes 3145736 | tf_op jit(solution)/shard_map/ppermute | solution.py:445
  11.2 1.9 collective-permute-start
  13.1 1.2 copy-start.14
  15.0 15.0 %all-to-all-start = ((bf16[8,2,8,512]{3,2,1,0:T(8,128)(2,1)}), bf16[8,2,8,512]{3,2,1,0:T(8,128)(2,1)S(1)}, u32[]{:S(2)}, u32[]{:S(2)}) async-start(bf16[8,2,8,512]{3,2,1,0:T(8,128)(2,1)} %fan.2), calls=%async_computation | async-start | bytes 262144 | tf_op jit(solution)/shard_map/all_to_all | solution.py:462
  35.7 1.6 copy-start
  37.3 1.6 copy-start.7
  70.8 6.2 %copy-start.2 = (bf16[16,2,8,8,512]{4,3,2,1,0:T(8,128)(2,1)}, bf16[16,2,8,8,512]{4,3,2,1,0:T(8,128)(2,1)S(1)}, u32[]{:S(2)}) copy-start(bf16[16,2,8,8,512]{4,3,2,1,0:T(8,128)(2,1)S(1)} %all_to_all.30.own_ref) | copy-start | bytes 6291460
  72.4 4.7 %collective-permute-start.3 = (bf16[16,8,8,512]{3,2,1,0:T(8,128)(2,1)S(1)}, bf16[16,8,8,512]{3,2,1,0:T(8,128)(2,1)S(1)}, u32[]{:S(2)}, u32[]{:S(2)}) collective-permute-start(bf16[16,8,8,512]{3,2,1,0:T(8,128)(2,1)S(1)} %get-tuple-element.75), channel_id=1, source_target_pairs={{0,1},{1,0},{2,3},{3,2},{4,5},{5,4},{6,7},{7,6},{8,9},{9,8},{10,11... | collective-permute-start | bytes 3145736 | tf_op jit(solution)/shard_map/ppermute | solution.py:445
  74.9 2.9 copy-start.1
  74.9 2.9 copy-start.22
  77.8 4.4 %copy-start.4 = (bf16[8,16,8,1024]{3,2,1,0:T(8,128)(2,1)}, bf16[8,16,8,1024]{3,2,1,0:T(8,128)(2,1)S(1)}, u32[]{:S(2)}) copy-start(bf16[8,16,8,1024]{3,2,1,0:T(8,128)(2,1)S(1)} %assemble.2) | copy-start | bytes 6291460
  82.2 11.8 %copy-start.24 = (bf16[1,64,128]{2,1,0:T(8,128)(2,1)S(1)}, bf16[1,64,128]{2,1,0:T(8,128)(2,1)}, u32[]{:S(2)}) copy-start(bf16[1,64,128]{2,1,0:T(8,128)(2,1)} %param.15) | copy-start | bytes 49156
  82.2 59.7 %all-to-all-start.2 = ((bf16[64,16,1024]{2,1,0:T(8,128)(2,1)}), bf16[64,16,1024]{2,1,0:T(8,128)(2,1)}, u32[]{:S(2)}, u32[]{:S(2)}) async-start(bf16[64,16,1024]{2,1,0:T(8,128)(2,1)} %bitcast.43), calls=%async_computation.2 | async-start | bytes 4194304 | tf_op jit(solution)/shard_map/all_to_all | solution.py:484
  93.3 3.4 %collective-permute-start.4 = (bf16[16,8,8,512]{3,2,1,0:T(8,128)(2,1)}, bf16[16,8,8,512]{3,2,1,0:T(8,128)(2,1)}, u32[]{:S(2)}, u32[]{:S(2)}) collective-permute-start(bf16[16,8,8,512]{3,2,1,0:T(8,128)(2,1)} %get-tuple-element.74), channel_id=1, source_target_pairs={{0,1},{1,0},{2,3},{3,2},{4,5},{5,4},{6,7},{7,6},{8,9},{9,8},{10,11... | collective-permute-start | bytes 3145736 | tf_op jit(solution)/shard_map/ppermute | solution.py:445
  94.0 45.6 %collective-permute-start.5 = (bf16[32,16384]{1,0:T(8,128)(2,1)}, bf16[32,16384]{1,0:T(8,128)(2,1)}, u32[]{:S(2)}, u32[]{:S(2)}) collective-permute-start(bf16[32,16384]{1,0:T(8,128)(2,1)} %get-tuple-element.31), channel_id=1, source_target_pairs={{0,3},{1,2},{2,1},{3,0},{4,7},{5,6},{6,5},{7,4},{8,11},{9,10},{10,... | collective-permute-start | bytes 3145736 | tf_op jit(solution)/shard_map/ppermute | solution.py:445
  96.7 1.6 copy-start.3
  99.6 1.3 copy-start.5
  141.9 1.6 copy-start.6
  143.5 1.2 copy-start.8
  144.7 1.2 copy-start.15
  167.7 82.1 %all-to-all-start.3 = ((bf16[64,16,1024]{2,1,0:T(8,128)(2,1)}), bf16[64,16,1024]{2,1,0:T(8,128)(2,1)}, u32[]{:S(2)}, u32[]{:S(2)}) async-start(bf16[64,16,1024]{2,1,0:T(8,128)(2,1)} %bitcast.44), calls=%async_computation.3 | async-start | bytes 4194304 | tf_op jit(solution)/shard_map/all_to_all | solution.py:488
  177.8 10.7 %collective-permute-start.6 = (bf16[32,16384]{1,0:T(8,128)(2,1)}, bf16[32,16384]{1,0:T(8,128)(2,1)S(1)}, u32[]{:S(2)}, u32[]{:S(2)}) collective-permute-start(bf16[32,16384]{1,0:T(8,128)(2,1)} %get-tuple-element.34), channel_id=1, source_target_pairs={{0,1},{1,0},{2,3},{3,2},{4,5},{5,4},{6,7},{7,6},{8,9},{9,8},{10,11... | collective-permute-start | bytes 3145736 | tf_op jit(solution)/shard_map/ppermute | solution.py:445
  179.0 45.4 %collective-permute-start.7 = (bf16[32,16384]{1,0:T(8,128)(2,1)}, bf16[32,16384]{1,0:T(8,128)(2,1)S(1)}, u32[]{:S(2)}, u32[]{:S(2)}) collective-permute-start(bf16[32,16384]{1,0:T(8,128)(2,1)} %get-tuple-element.35), channel_id=1, source_target_pairs={{0,2},{1,3},{2,0},{3,1},{4,6},{5,7},{6,4},{7,5},{8,10},{9,11},{10,... | collective-permute-start | bytes 3145736 | tf_op jit(solution)/shard_map/ppermute | solution.py:445
  179.0 68.8 %collective-permute-start.8 = (bf16[32,16384]{1,0:T(8,128)(2,1)}, bf16[32,16384]{1,0:T(8,128)(2,1)S(1)}, u32[]{:S(2)}, u32[]{:S(2)}) collective-permute-start(bf16[32,16384]{1,0:T(8,128)(2,1)} %get-tuple-element.36), channel_id=1, source_target_pairs={{0,3},{1,2},{2,1},{3,0},{4,7},{5,6},{6,5},{7,4},{8,11},{9,10},{10,... | collective-permute-start | bytes 3145736 | tf_op jit(solution)/shard_map/ppermute | solution.py:445
  180.8 1.6 copy-start.18
  182.4 1.6 copy-start.19
  187.1 1.3 copy-start.20
  188.4 60.4 %collective-permute-start.9 = (bf16[16,8,8,512]{3,2,1,0:T(8,128)(2,1)S(1)}, bf16[16,8,8,512]{3,2,1,0:T(8,128)(2,1)S(1)}, u32[]{:S(2)}, u32[]{:S(2)}) collective-permute-start(bf16[16,8,8,512]{3,2,1,0:T(8,128)(2,1)S(1)} %get-tuple-element.40), channel_id=1, source_target_pairs={{0,1},{1,0},{2,3},{3,2},{4,5},{5,4},{6,7},{7,6},{8,9},{9,8},{10,11... | collective-permute-start | bytes 3145736 | tf_op jit(solution)/shard_map/ppermute | solution.py:445
  188.5 69.8 %copy-start.9 = (bf16[32,16384]{1,0:T(8,128)(2,1)}, bf16[32,16384]{1,0:T(8,128)(2,1)S(1)}, u32[]{:S(2)}) copy-start(bf16[32,16384]{1,0:T(8,128)(2,1)S(1)} %collective-permute-done.6.refs_0_.p1) | copy-start | bytes 3145732
  224.4 1.1 copy-start.10
  247.9 1.0 copy-start.12
  248.8 1.0 copy-start.16
  249.8 1.2 copy-start.11
  251.0 1.2 copy-start.13
  252.3 1.2 copy-start.17
  253.5 7.7 %copy-start.21 = (f32[16,8,8,512]{3,2,1,0:T(8,128)S(1)}, f32[16,8,8,512]{3,2,1,0:T(8,128)}, u32[]{:S(2)}) copy-start(f32[16,8,8,512]{3,2,1,0:T(8,128)} %copy-done.20) | copy-start | bytes 6291460
  258.4 2.8 collective-permute-start.10
  262.8 39.4 %all-to-all-start.4 = ((bf16[16,2,8,8,512]{4,3,2,1,0:T(8,128)(2,1)}), bf16[16,2,8,8,512]{4,3,2,1,0:T(8,128)(2,1)S(1)}, u32[]{:S(2)}, u32[]{:S(2)}) async-start(bf16[16,2,8,8,512]{4,3,2,1,0:T(8,128)(2,1)} %join.1.after_ref), calls=%async_computation.4 | async-start | bytes 4194304 | tf_op jit(solution)/shard_map/all_to_all | solution.py:496
  276.5 20.8 %collective-permute-start.13 = (f32[32,512]{1,0:T(8,128)S(1)}, f32[32,512]{1,0:T(8,128)S(1)}, u32[]{:S(2)}, u32[]{:S(2)}) collective-permute-start(f32[32,512]{1,0:T(8,128)S(1)} %constant_dynamic-update-slice_fusion.2), channel_id=1, source_target_pairs={{0,12},{4,8},{8,4},{12,0},{1,13},{5,9},{9,5},{13,1},{2,14},{6,10},... | collective-permute-start | bytes 196616 | tf_op jit(solution)/shard_map/ppermute | solution.py:445
  279.1 18.2 %collective-permute-start.12 = (f32[32,512]{1,0:T(8,128)S(1)}, f32[32,512]{1,0:T(8,128)S(1)}, u32[]{:S(2)}, u32[]{:S(2)}) collective-permute-start(f32[32,512]{1,0:T(8,128)S(1)} %constant_dynamic-update-slice_fusion.2), channel_id=1, source_target_pairs={{0,8},{4,12},{8,0},{12,4},{1,9},{5,13},{9,1},{13,5},{2,10},{6,14},... | collective-permute-start | bytes 196616 | tf_op jit(solution)/shard_map/ppermute | solution.py:445
  279.7 17.8 %collective-permute-start.11 = (f32[32,512]{1,0:T(8,128)S(1)}, f32[32,512]{1,0:T(8,128)S(1)}, u32[]{:S(2)}, u32[]{:S(2)}) collective-permute-start(f32[32,512]{1,0:T(8,128)S(1)} %constant_dynamic-update-slice_fusion.2), channel_id=1, source_target_pairs={{0,4},{4,0},{8,12},{12,8},{1,5},{5,1},{9,13},{13,9},{2,6},{6,2},{1... | collective-permute-start | bytes 196616 | tf_op jit(solution)/shard_map/ppermute | solution.py:445
  297.5 4.7 %collective-permute-start.14 = (f32[32,512]{1,0:T(8,128)S(1)}, f32[32,512]{1,0:T(8,128)S(1)}, u32[]{:S(2)}, u32[]{:S(2)}) collective-permute-start(f32[32,512]{1,0:T(8,128)S(1)} %add_add_fusion), channel_id=1, source_target_pairs={{0,16},{16,0},{1,17},{17,1},{2,18},{18,2},{3,19},{19,3},{4,20},{20... | collective-permute-start | bytes 196616 | tf_op jit(solution)/shard_map/ppermute | solution.py:445
  303.3 17.7 %all-to-all-start.5 = ((bf16[8,6,8,512]{3,2,1,0:T(8,128)(2,1)}), bf16[8,6,8,512]{3,2,1,0:T(8,128)(2,1)S(1)}, u32[]{:S(2)}, u32[]{:S(2)}) async-start(bf16[8,6,8,512]{3,2,1,0:T(8,128)(2,1)} %plane_sum.1.after_ref), calls=%async_computation.5 | async-start | bytes 786432 | tf_op jit(solution)/shard_map/all_to_all | solution.py:505
  320.9 0.7 copy-start.23
  321.7 5.7 %collective-permute-start.15 = (f32[2,4,512]{2,1,0:T(4,128)S(1)}, f32[2,4,512]{2,1,0:T(4,128)S(1)}, u32[]{:S(2)}, u32[]{:S(2)}) collective-permute-start(f32[2,4,512]{2,1,0:T(4,128)S(1)} %get-tuple-element.82), channel_id=1, source_target_pairs={{0,1},{1,0},{2,3},{3,2},{4,5},{5,4},{6,7},{7,6},{8,9},{9,8},{10,11... | collective-permute-start | bytes 49160 | tf_op jit(solution)/shard_map/ppermute | solution.py:445
